TPU v7x, 32 devices: a whole 2x2x4 slice. The times are simulated.
32 devices in a mesh: area: 4 (over z), line: 8 (over y, x, core).
Axes of the slice: x: 2, y: 2, z: 4, core: 2. Of those that a mesh axis runs over, the one named last changes fastest.
Arguments:
- traces: bfloat16 [8192, 2048], P(('area', 'line')), may hold values from -6 to 6
- owner: int32 [8192, 1], P(('area', 'line')), may hold values from 0 to 7; in each aligned block of 256 rows (0 to 255, 256 to 511, ...) at most 64 rows name the same one
- panel_index: int32 [8192], P(('area', 'line')), may hold values from 0 to 319
- receiver_slot: int32 [8192], P(('area', 'line')), may hold values from 0 to 63
- aperture_weight: float32 [8192], P(('area', 'line')), may hold values from 0.5 to 1.5
- panels: bfloat16 [4, 8, 256, 2048], P('area', 'line'), may hold values from -6 to 6
- plan: int32 [4, 4], replicated, may hold values from 0 to 7
Outputs:
- multiples: bfloat16 [4, 2048, 2048], P(None, ('area', 'line'))
Inputs may be any that keep to these rules, and one draw needn't show every extreme that they name: Among the traces of one device, no owner is named by more than 64 traces; some owner is named by exactly 64 of them.
All inputs are finite; a program needn't handle non-finite values.
Results may differ from a plain program's by a relative error of at most 0.014.
Values may be sent and summed in bfloat16 or wider, within the bound.
No kernel may reach another device: no remote copies, remote signals or barrier semaphores. Data moves between devices by JAX's collectives and lax.ppermute only.
A program may use at most 128 MiB of HBM per device.

v0:
```python
import math

import jax
import jax.numpy as jnp
from jax import lax
from jax.sharding import PartitionSpec as P

NF = 1024
EDGE = 64
STEPS = 4
RECV_DEV = 64


def from_root(block, axis, owner):
    block = jnp.where(lax.axis_index(axis) == owner, block, jnp.zeros_like(block))
    return lax.psum(block, axis)


def from_behind(block, axis, distance):
    devices = range(lax.axis_size(axis))
    route = [(i - distance, i) for i in devices if i - distance in devices]
    return lax.ppermute(block, axis, route)


def make_tables(samples, bins):
    sample_ids = jnp.arange(samples, dtype=jnp.int32)
    bin_ids = jnp.arange(bins, dtype=jnp.int32)
    phases = (sample_ids[:, None] * bin_ids[None, :] % samples).astype(jnp.float32) * (
        2.0 * math.pi / samples
    )
    scaling = 1.0 / math.sqrt(samples)
    forward = (jnp.concatenate([jnp.cos(phases), -jnp.sin(phases)], 1) * scaling).astype(
        jnp.bfloat16
    )
    weights = jnp.where(bin_ids == 0, 1.0, 2.0).astype(jnp.float32)[:, None]
    inverse = (
        jnp.concatenate([jnp.cos(phases).T * weights, -jnp.sin(phases).T * weights], 0) * scaling
    ).astype(jnp.bfloat16)
    return (forward, inverse)


def local(traces, owner, panel_index, receiver_slot, aperture_weight, panels, plan):
    line_count = lax.axis_size("line")
    row_count, samples = traces.shape
    capacity = 2 * row_count // line_count
    slot_count = line_count * capacity
    panel_rows = panels.shape[2]
    forward, inverse = make_tables(samples, NF)
    target = owner[:, 0]
    matches = (target[:, None] == jnp.arange(line_count, dtype=jnp.int32)[None, :]).astype(
        jnp.int32
    )
    ranking = jnp.sum((jnp.cumsum(matches, 0) - 1) * matches, 1)
    slots_at = target * capacity + ranking
    moved_index = jnp.zeros((slot_count,), jnp.int32).at[slots_at].set(panel_index)
    moved_recv = jnp.full((slot_count,), -1, jnp.int32).at[slots_at].set(receiver_slot)
    moved_weight = jnp.zeros((slot_count,), jnp.float32).at[slots_at].set(aperture_weight)
    buffer = jnp.zeros((slot_count, samples), jnp.bfloat16).at[slots_at].set(traces)
    received = (
        lax.all_to_all(
            buffer.reshape(line_count, capacity, samples),
            "line",
            split_axis=0,
            concat_axis=0,
            tiled=True,
        ),
        lax.all_to_all(
            moved_index.reshape(line_count, capacity),
            "line",
            split_axis=0,
            concat_axis=0,
            tiled=True,
        ),
        lax.all_to_all(
            moved_recv.reshape(line_count, capacity),
            "line",
            split_axis=0,
            concat_axis=0,
            tiled=True,
        ),
        lax.all_to_all(
            moved_weight.reshape(line_count, capacity).astype(jnp.bfloat16),
            "line",
            split_axis=0,
            concat_axis=0,
            tiled=True,
        ).astype(jnp.float32),
    )
    spectra = jnp.dot(
        received[0].reshape(slot_count, samples), forward, preferred_element_type=jnp.float32
    ).astype(jnp.bfloat16)
    got_index = received[1].reshape(slot_count)
    got_recv = received[2].reshape(slot_count)
    got_weight = received[3].reshape(slot_count)[:, None]
    selector = (got_recv[None, :] == jnp.arange(RECV_DEV, dtype=jnp.int32)[:, None]).astype(
        jnp.bfloat16
    )
    real_d = spectra[:, :NF].astype(jnp.float32)
    imag_d = spectra[:, NF:].astype(jnp.float32)
    area_now = lax.axis_index("area")
    own_panel = panels[0, 0]
    results = []
    for panel_step in range(STEPS):
        source_line = plan[area_now, panel_step]
        panel_now = from_root(own_panel, "line", source_line)
        panel_spec = jnp.dot(panel_now, forward, preferred_element_type=jnp.float32).astype(
            jnp.bfloat16
        )
        border = from_behind(panel_spec[panel_rows - EDGE :], "area", 1)
        extended = jnp.concatenate([panel_spec, border], 0)
        picked = jnp.take(extended, got_index, axis=0).astype(jnp.float32)
        real_p = picked[:, :NF]
        imag_p = picked[:, NF:]
        product = jnp.concatenate(
            [
                (real_p * real_d - imag_p * imag_d) * got_weight,
                (real_p * imag_d + imag_p * real_d) * got_weight,
            ],
            1,
        ).astype(jnp.bfloat16)
        receiver_spectra = jnp.dot(selector, product, preferred_element_type=jnp.float32).astype(
            jnp.bfloat16
        )
        results.append(
            jnp.dot(receiver_spectra, inverse, preferred_element_type=jnp.float32).astype(
                jnp.bfloat16
            )
        )
    return jnp.stack(results, 0)


def solution(mesh):
    in_specs = (
        P(("area", "line"), None),
        P(("area", "line"), None),
        P(("area", "line")),
        P(("area", "line")),
        P(("area", "line")),
        P("area", "line", None, None),
        P(),
    )
    out_specs = P(None, ("area", "line"), None)
    return jax.shard_map(local, mesh=mesh, in_specs=in_specs, out_specs=out_specs, check_vma=False)
```

profile of v0, /device:TPU:0, one launch (start us, length us, event | category | flops | bytes accessed | tf_op | source)
XLA Modules:
  0.0 244.6 jit_solution(2086551908232233764)
XLA Ops:
  11.7 5.2 %all-to-all-start.3 = ((bf16[8,1,64]{2,1,0:T(2,128)(2,1)}), bf16[8,1,64]{2,1,0:T(2,128)(2,1)S(1)}, u32[]{:S(2)}, u32[]{:S(2)}) async-start(bf16[8,1,64]{2,1,0:T(2,128)(2,1)} %convert_element_type.136), calls=%async_computation.3 | async-start | bytes 8192 | tf_op jit(solution)/shard_map/all_to_all | solution.py:81
  20.9 3.3 %select_bitcast_fusion.3 = (bf16[256,2048]{1,0:T(8,128)(2,1)}, bf16[256,2048]{1,0:T(8,128)(2,1)}, bf16[256,2048]{1,0:T(8,128)(2,1)}, bf16[256,2048]{1,0:T(8,128)(2,1)}) fusion(bf16[1,1,256,2048]{3,2,1,0:T(8,128)(2,1)} %param.14, pred[]{:T(512)S(6)} %eq.78, pred[]{:T(512)S(6)} %eq.81, pred[]{:T(512)S(6)} %eq.83, pred[]{:T(512)S(6)} %eq.82), kind=kLoop, calls=%fused_computation.117 | loop fusion | flops 2097152 | bytes 5242884 | tf_op jit(solution)/shard_map/jit(_where)/select_n | solution.py:15
  26.5 4.1 %all-to-all-start.1 = ((s32[8,1,64]{2,1,0:T(1,128)}), s32[8,1,64]{2,1,0:T(1,128)S(1)}, u32[]{:S(2)}, u32[]{:S(2)}) async-start(s32[8,1,64]{2,1,0:T(1,128)} %all_to_all.21), calls=%async_computation.1 | async-start | bytes 8192 | tf_op jit(solution)/shard_map/all_to_all | solution.py:67
  30.6 35.4 %cosine_multiply_fusion = (f32[1024,2048]{1,0:T(8,128)}, f32[1024,2048]{1,0:T(8,128)}) fusion(f32[1024]{0:T(1024)S(1)} %fusion.75), kind=kLoop, calls=%fused_computation.25 | loop fusion | flops 35651584 | bytes 16781312 | tf_op jit(solution)/shard_map/mul | solution.py:37
  68.3 4.2 %all-to-all-start = ((s32[8,1,64]{2,1,0:T(1,128)}), s32[8,1,64]{2,1,0:T(1,128)S(1)}, u32[]{:S(2)}, u32[]{:S(2)}) async-start(s32[8,1,64]{2,1,0:T(1,128)} %all_to_all.19), calls=%async_computation | async-start | bytes 8192 | tf_op jit(solution)/shard_map/all_to_all | solution.py:74
  72.5 34.5 %sine_negate_fusion = (f32[2048,1024]{1,0:T(8,128)}, f32[2048,1024]{1,0:T(8,128)}) fusion(), kind=kLoop, calls=%fused_computation.28 | loop fusion | flops 31457280 | bytes 16777216 | tf_op jit(solution)/shard_map/neg | solution.py:32
  106.9 4.4 %scatter_custom_fusion.2 = bf16[512,2048]{1,0:T(8,128)(2,1)} fusion(s32[256]{0:T(256)S(1)} %bitcast.57, bf16[256,2048]{1,0:T(8,128)(2,1)} %param.9, bf16[]{:T(256)} %constant.33.clone.1), kind=kCustom, calls=%fused_computation.115 | custom fusion | bytes 2097664 | tf_op jit(solution)/shard_map/scatter | solution.py:58
  111.4 4.2 %all-to-all-start.2 = ((bf16[8,64,2048]{2,1,0:T(8,128)(2,1)}), bf16[8,64,2048]{2,1,0:T(8,128)(2,1)S(1)}, u32[]{:S(2)}, u32[]{:S(2)}) async-start(bf16[8,64,2048]{2,1,0:T(8,128)(2,1)} %bitcast.8), calls=%async_computation.2 | async-start | bytes 4194304 | tf_op jit(solution)/shard_map/all_to_all | solution.py:60
  115.6 10.5 %fusion = bf16[2048,2048]{1,0:T(8,128)(2,1)} fusion(f32[2048,1024]{1,0:T(8,128)} %get-tuple-element.36, f32[2048,1024]{1,0:T(8,128)} %get-tuple-element.37), kind=kLoop, calls=%fused_computation.9 | loop fusion | flops 12582912 | bytes 25165824 | tf_op jit(solution)/shard_map/convert_element_type | solution.py:32
  129.3 4.8 %fusion.1 = bf16[2048,2048]{1,0:T(8,128)(2,1)} fusion(f32[1024,2048]{1,0:T(8,128)S(1)} %bitcast.49, f32[1024,2048]{1,0:T(8,128)S(1)} %bitcast.47), kind=kLoop, calls=%fused_computation.11 | loop fusion | flops 12582912 | bytes 25165824 | tf_op jit(solution)/shard_map/convert_element_type | solution.py:38
  136.3 6.0 %all-to-all-done.2 = bf16[8,64,2048]{2,1,0:T(8,128)(2,1)S(1)} async-done(((bf16[8,64,2048]{2,1,0:T(8,128)(2,1)}), bf16[8,64,2048]{2,1,0:T(8,128)(2,1)S(1)}, u32[]{:S(2)}, u32[]{:S(2)}) %all-to-all-start.2) | async-done | bytes 2097184 | tf_op jit(solution)/shard_map/all_to_all | solution.py:60
  142.2 9.1 %convolution_convert_fusion = bf16[512,2048]{1,0:T(8,128)(2,1)} fusion(bf16[512,2048]{1,0:T(8,128)(2,1)S(1)} %bitcast.50, bf16[2048,2048]{1,0:T(8,128)(2,1)} %fusion), kind=kOutput, calls=%fused_computation.50 | convolution fusion | flops 4296015872 | bytes 12582912 | tf_op jit(solution)/shard_map/dot_general | solution.py:89
  151.3 6.2 %convolution_convert_fusion.1 = bf16[256,2048]{1,0:T(8,128)(2,1)S(1)} fusion(bf16[256,2048]{1,0:T(8,128)(2,1)} %get-tuple-element.6, bf16[2048,2048]{1,0:T(8,128)(2,1)} %fusion), kind=kOutput, calls=%fused_computation.51 | convolution fusion | flops 2148007936 | bytes 10485760 | tf_op jit(solution)/shard_map/dot_general | solution.py:106
  157.5 3.5 %collective-permute-start.3 = (bf16[64,2048]{1,0:T(8,128)(2,1)S(1)}, bf16[64,2048]{1,0:T(8,128)(2,1)S(1)}, u32[]{:S(2)}, u32[]{:S(2)}) collective-permute-start(bf16[64,2048]{1,0:T(8,128)(2,1)S(1)} %slice.84), channel_id=1, source_target_pairs={{0,8},{8,16},{16,24},{1,9},{9,17},{17,25},{2,10},{10,18},{18,26},{... | collective-permute-start | bytes 786440 | tf_op jit(solution)/shard_map/ppermute | solution.py:22
  163.5 3.5 %collective-permute-start.2 = (bf16[64,2048]{1,0:T(8,128)(2,1)S(1)}, bf16[64,2048]{1,0:T(8,128)(2,1)S(1)}, u32[]{:S(2)}, u32[]{:S(2)}) collective-permute-start(bf16[64,2048]{1,0:T(8,128)(2,1)S(1)} %slice.81), channel_id=1, source_target_pairs={{0,8},{8,16},{16,24},{1,9},{9,17},{17,25},{2,10},{10,18},{18,26},{... | collective-permute-start | bytes 786440 | tf_op jit(solution)/shard_map/ppermute | solution.py:22
  169.4 3.5 %collective-permute-start.1 = (bf16[64,2048]{1,0:T(8,128)(2,1)S(1)}, bf16[64,2048]{1,0:T(8,128)(2,1)S(1)}, u32[]{:S(2)}, u32[]{:S(2)}) collective-permute-start(bf16[64,2048]{1,0:T(8,128)(2,1)S(1)} %slice.78), channel_id=1, source_target_pairs={{0,8},{8,16},{16,24},{1,9},{9,17},{17,25},{2,10},{10,18},{18,26},{... | collective-permute-start | bytes 786440 | tf_op jit(solution)/shard_map/ppermute | solution.py:22
  181.7 3.3 %gather_fusion.2 = bf16[512,2048]{1,0:T(8,128)(2,1)} fusion(bf16[320,2048]{1,0:T(8,128)(2,1)S(1)} %pad_maximum_fusion.2, s32[1024]{0:T(1024)S(1)} %pad_clamp_fusion), kind=kCustom, calls=%fused_computation.2.clone | custom fusion | bytes 4196352 | tf_op jit(solution)/shard_map/jit(_take)/gather | solution.py:111
  193.2 8.4 %select_convert_fusion.3 = (f32[512,2048]{1,0:T(8,128)S(1)}, f32[512,2048]{1,0:T(8,128)}, f32[512,2048]{1,0:T(8,128)}, f32[512,2048]{1,0:T(8,128)}) fusion(bf16[512,2048]{1,0:T(8,128)(2,1)} %gather_fusion, pred[512]{0:T(512)(128)(4,1)S(1)} %compare_and_fusion, bf16[512,2048]{1,0:T(8,128)(2,1)} %gather_fusion.1, bf16[512,2048]{1,0:T(8,128)(2,1)} %gather_fusion.2, ...), kind=kLoop, calls=%fused_computation.106 | loop fusion | flops 8388608 | bytes 25166336 | tf_op jit(solution)/shard_map/convert_element_type | solution.py:111
  201.6 5.1 %fusion.21 = (bf16[512,1024]{1,0:T(8,128)(2,1)}, bf16[512,1024]{1,0:T(8,128)(2,1)}, bf16[512,1024]{1,0:T(8,128)(2,1)}, bf16[512,1024]{1,0:T(8,128)(2,1)}) fusion(f32[512,2048]{1,0:T(8,128)S(1)} %get-tuple-element.32, f32[512]{0:T(512)S(1)} %reshape.86, bf16[512,2048]{1,0:T(8,128)(2,1)S(1)} %copy-done.1, f32[512,2048]{1,0:T(8,128)} %get-tuple-element.33), kind=kLoop, calls=%fused_computation.69 | loop fusion | flops 11534336 | bytes 14682112 | tf_op jit(solution)/shard_map/convert.7
  206.6 6.0 %fusion.15 = bf16[1,64,2048]{2,1,0:T(8,128)(2,1)S(1)} fusion(bf16[2048,2048]{1,0:T(8,128)(2,1)} %fusion.1, bf16[512,1024]{1,0:T(8,128)(2,1)} %get-tuple-element.11, bf16[512,1024]{1,0:T(8,128)(2,1)} %get-tuple-element.10, s32[512]{0:T(512)S(1)} %eq.74), kind=kOutput, calls=%fused_computation.63 | convolution fusion | flops 675577856 | bytes 10749952 | tf_op jit(solution)/shard_map/dot_general | solution.py:125
  212.6 6.7 %fusion.16 = bf16[1,64,2048]{2,1,0:T(8,128)(2,1)} fusion(bf16[2048,2048]{1,0:T(8,128)(2,1)} %fusion.1, bf16[512,1024]{1,0:T(8,128)(2,1)} %get-tuple-element.18, bf16[512,1024]{1,0:T(8,128)(2,1)} %get-tuple-element.19, s32[512]{0:T(512)S(1)} %eq.74), kind=kOutput, calls=%fused_computation.64 | convolution fusion | flops 675577856 | bytes 10749952 | tf_op jit(solution)/shard_map/dot_general | solution.py:125
  219.3 5.8 %fusion.33 = (bf16[512,1024]{1,0:T(8,128)(2,1)}, bf16[512,1024]{1,0:T(8,128)(2,1)}, bf16[512,1024]{1,0:T(8,128)(2,1)}, bf16[512,1024]{1,0:T(8,128)(2,1)}) fusion(f32[512,2048]{1,0:T(8,128)} %get-tuple-element.34, f32[512]{0:T(512)S(1)} %reshape.86, bf16[512,2048]{1,0:T(8,128)(2,1)S(1)} %copy-done.1, f32[512,2048]{1,0:T(8,128)} %get-tuple-element.35), kind=kLoop, calls=%fused_computation.81 | loop fusion | flops 11534336 | bytes 14682112 | tf_op jit(solution)/shard_map/convert.3
  225.1 6.1 %fusion.17 = bf16[1,64,2048]{2,1,0:T(8,128)(2,1)S(1)} fusion(bf16[2048,2048]{1,0:T(8,128)(2,1)} %fusion.1, bf16[512,1024]{1,0:T(8,128)(2,1)} %get-tuple-element.15, bf16[512,1024]{1,0:T(8,128)(2,1)} %get-tuple-element.14, s32[512]{0:T(512)S(1)} %eq.74), kind=kOutput, calls=%fused_computation.65 | convolution fusion | flops 675577856 | bytes 10749952 | tf_op jit(solution)/shard_map/dot_general | solution.py:125
  231.2 5.4 %fusion.18 = bf16[1,64,2048]{2,1,0:T(8,128)(2,1)S(1)} fusion(bf16[2048,2048]{1,0:T(8,128)(2,1)} %fusion.1, bf16[512,1024]{1,0:T(8,128)(2,1)S(1)} %copy-done.2, bf16[512,1024]{1,0:T(8,128)(2,1)S(1)} %copy-done.3, s32[512]{0:T(512)S(1)} %eq.74), kind=kOutput, calls=%fused_computation.66 | convolution fusion | flops 675577856 | bytes 10749952 | tf_op jit(solution)/shard_map/dot_general | solution.py:125
  (84 shorter events, 39.3 us)
Async XLA Ops:
  11.7 14.8 %all-to-all-start.3 = ((bf16[8,1,64]{2,1,0:T(2,128)(2,1)}), bf16[8,1,64]{2,1,0:T(2,128)(2,1)S(1)}, u32[]{:S(2)}, u32[]{:S(2)}) async-start(bf16[8,1,64]{2,1,0:T(2,128)(2,1)} %convert_element_type.136), calls=%async_computation.3 | async-start | bytes 8192 | tf_op jit(solution)/shard_map/all_to_all | solution.py:81
  16.9 134.4 %all-reduce.3.cloned.1.call-start = ((), (), s32[]{:S(2)}) async-start(), calls=%async_computation.4 | async-start | bytes 8388608 | tf_op jit(solution)/shard_map/psum | solution.py:16
  26.5 41.8 %all-to-all-start.1 = ((s32[8,1,64]{2,1,0:T(1,128)}), s32[8,1,64]{2,1,0:T(1,128)S(1)}, u32[]{:S(2)}, u32[]{:S(2)}) async-start(s32[8,1,64]{2,1,0:T(1,128)} %all_to_all.21), calls=%async_computation.1 | async-start | bytes 8192 | tf_op jit(solution)/shard_map/all_to_all | solution.py:67
  68.3 43.1 %all-to-all-start = ((s32[8,1,64]{2,1,0:T(1,128)}), s32[8,1,64]{2,1,0:T(1,128)S(1)}, u32[]{:S(2)}, u32[]{:S(2)}) async-start(s32[8,1,64]{2,1,0:T(1,128)} %all_to_all.19), calls=%async_computation | async-start | bytes 8192 | tf_op jit(solution)/shard_map/all_to_all | solution.py:74
  111.4 30.8 %all-to-all-start.2 = ((bf16[8,64,2048]{2,1,0:T(8,128)(2,1)}), bf16[8,64,2048]{2,1,0:T(8,128)(2,1)S(1)}, u32[]{:S(2)}, u32[]{:S(2)}) async-start(bf16[8,64,2048]{2,1,0:T(8,128)(2,1)} %bitcast.8), calls=%async_computation.2 | async-start | bytes 4194304 | tf_op jit(solution)/shard_map/all_to_all | solution.py:60
  115.6 10.5 %slice-start = ((s8[8388608]{0:T(1024)(128)(4,1)}), s8[4194304]{0:T(1024)(128)(4,1)S(1)}, s32[]{:S(2)}) async-start(s8[8388608]{0:T(1024)(128)(4,1)} %bitcast.46), calls=%async_computation.5 | async-start | bytes 8388608
  115.6 11.4 %slice-start.2 = ((s8[8388608]{0:T(1024)(128)(4,1)}), s8[4194304]{0:T(1024)(128)(4,1)S(1)}, s32[]{:S(2)}) async-start(s8[8388608]{0:T(1024)(128)(4,1)} %bitcast.48), calls=%async_computation.7 | async-start | bytes 8388608
  115.6 12.5 %slice-start.1 = ((s8[8388608]{0:T(1024)(128)(4,1)}), s8[4194304]{0:T(1024)(128)(4,1)S(1)}, s32[]{:S(2)}) async-start(s8[8388608]{0:T(1024)(128)(4,1)} %bitcast.46), calls=%async_computation.6 | async-start | bytes 8388608
  115.6 13.7 %slice-start.3 = ((s8[8388608]{0:T(1024)(128)(4,1)}), s8[4194304]{0:T(1024)(128)(4,1)S(1)}, s32[]{:S(2)}) async-start(s8[8388608]{0:T(1024)(128)(4,1)} %bitcast.48), calls=%async_computation.8 | async-start | bytes 8388608
  151.3 9.7 %copy-start = (bf16[2048,2048]{1,0:T(8,128)(2,1)S(1)}, bf16[2048,2048]{1,0:T(8,128)(2,1)}, u32[]{:S(2)}) copy-start(bf16[2048,2048]{1,0:T(8,128)(2,1)} %fusion) | copy-start | bytes 25165828
  151.3 9.7 %copy-start.10 = (bf16[256,2048]{1,0:T(8,128)(2,1)S(1)}, bf16[256,2048]{1,0:T(8,128)(2,1)}, u32[]{:S(2)}) copy-start(bf16[256,2048]{1,0:T(8,128)(2,1)} %get-tuple-element.7) | copy-start | bytes 3145732
  157.5 20.8 %collective-permute-start.3 = (bf16[64,2048]{1,0:T(8,128)(2,1)S(1)}, bf16[64,2048]{1,0:T(8,128)(2,1)S(1)}, u32[]{:S(2)}, u32[]{:S(2)}) collective-permute-start(bf16[64,2048]{1,0:T(8,128)(2,1)S(1)} %slice.84), channel_id=1, source_target_pairs={{0,8},{8,16},{16,24},{1,9},{9,17},{17,25},{2,10},{10,18},{18,26},{... | collective-permute-start | bytes 786440 | tf_op jit(solution)/shard_map/ppermute | solution.py:22
  161.0 5.9 %copy-start.9 = (bf16[256,2048]{1,0:T(8,128)(2,1)S(1)}, bf16[256,2048]{1,0:T(8,128)(2,1)}, u32[]{:S(2)}) copy-start(bf16[256,2048]{1,0:T(8,128)(2,1)} %get-tuple-element.8) | copy-start | bytes 3145732
  163.5 14.9 %collective-permute-start.2 = (bf16[64,2048]{1,0:T(8,128)(2,1)S(1)}, bf16[64,2048]{1,0:T(8,128)(2,1)S(1)}, u32[]{:S(2)}, u32[]{:S(2)}) collective-permute-start(bf16[64,2048]{1,0:T(8,128)(2,1)S(1)} %slice.81), channel_id=1, source_target_pairs={{0,8},{8,16},{16,24},{1,9},{9,17},{17,25},{2,10},{10,18},{18,26},{... | collective-permute-start | bytes 786440 | tf_op jit(solution)/shard_map/ppermute | solution.py:22
  167.0 6.0 %copy-start.8 = (bf16[256,2048]{1,0:T(8,128)(2,1)S(1)}, bf16[256,2048]{1,0:T(8,128)(2,1)}, u32[]{:S(2)}) copy-start(bf16[256,2048]{1,0:T(8,128)(2,1)} %get-tuple-element.9) | copy-start | bytes 3145732
  169.4 3.5 %copy-start.6 = (bf16[256,2048]{1,0:T(8,128)(2,1)}, bf16[256,2048]{1,0:T(8,128)(2,1)S(1)}, u32[]{:S(2)}) copy-start(bf16[256,2048]{1,0:T(8,128)(2,1)S(1)} %convolution_convert_fusion.3) | copy-start | bytes 3145732
  169.4 15.6 %collective-permute-start.1 = (bf16[64,2048]{1,0:T(8,128)(2,1)S(1)}, bf16[64,2048]{1,0:T(8,128)(2,1)S(1)}, u32[]{:S(2)}, u32[]{:S(2)}) collective-permute-start(bf16[64,2048]{1,0:T(8,128)(2,1)S(1)} %slice.78), channel_id=1, source_target_pairs={{0,8},{8,16},{16,24},{1,9},{9,17},{17,25},{2,10},{10,18},{18,26},{... | collective-permute-start | bytes 786440 | tf_op jit(solution)/shard_map/ppermute | solution.py:22
  175.4 3.0 %copy-start.4 = (bf16[256,2048]{1,0:T(8,128)(2,1)}, bf16[256,2048]{1,0:T(8,128)(2,1)S(1)}, u32[]{:S(2)}) copy-start(bf16[256,2048]{1,0:T(8,128)(2,1)S(1)} %convolution_convert_fusion.4) | copy-start | bytes 3145732
  176.1 13.6 %collective-permute-start = (bf16[64,2048]{1,0:T(8,128)(2,1)}, bf16[64,2048]{1,0:T(8,128)(2,1)S(1)}, u32[]{:S(2)}, u32[]{:S(2)}) collective-permute-start(bf16[64,2048]{1,0:T(8,128)(2,1)} %slice.73), channel_id=1, source_target_pairs={{0,8},{8,16},{16,24},{1,9},{9,17},{17,25},{2,10},{10,18},{18,26},{... | collective-permute-start | bytes 786440 | tf_op jit(solution)/shard_map/ppermute | solution.py:22
  186.4 3.3 %copy-start.5 = (bf16[256,2048]{1,0:T(8,128)(2,1)S(1)}, bf16[256,2048]{1,0:T(8,128)(2,1)}, u32[]{:S(2)}) copy-start(bf16[256,2048]{1,0:T(8,128)(2,1)} %copy-done.4) | copy-start | bytes 3145732
  193.2 8.4 %copy-start.1 = (bf16[512,2048]{1,0:T(8,128)(2,1)S(1)}, bf16[512,2048]{1,0:T(8,128)(2,1)}, u32[]{:S(2)}) copy-start(bf16[512,2048]{1,0:T(8,128)(2,1)} %convolution_convert_fusion) | copy-start | bytes 6291460
  225.1 6.1 %copy-start.2 = (bf16[512,1024]{1,0:T(8,128)(2,1)S(1)}, bf16[512,1024]{1,0:T(8,128)(2,1)}, u32[]{:S(2)}) copy-start(bf16[512,1024]{1,0:T(8,128)(2,1)} %get-tuple-element.20) | copy-start | bytes 3145732
  225.1 6.1 %copy-start.3 = (bf16[512,1024]{1,0:T(8,128)(2,1)S(1)}, bf16[512,1024]{1,0:T(8,128)(2,1)}, u32[]{:S(2)}) copy-start(bf16[512,1024]{1,0:T(8,128)(2,1)} %get-tuple-element.21) | copy-start | bytes 3145732
  231.2 5.4 %copy-start.7 = (bf16[1,64,2048]{2,1,0:T(8,128)(2,1)S(1)}, bf16[1,64,2048]{2,1,0:T(8,128)(2,1)}, u32[]{:S(2)}) copy-start(bf16[1,64,2048]{2,1,0:T(8,128)(2,1)} %fusion.16) | copy-start | bytes 786436
Sparse Core Ops, SparseCore 0:
  24.4 83.3 all-reduce.2
where the time goes:
time: 245 us
  other arithmetic  115 us (47%)
  matrix products  46.6 us (19%)
  local copies, waits for them, and re-layouts  30.8 us (13%)
  starting transfers between devices  30.4 us (12%)
  between operations  16.3 us (7%)
  waiting for transfers between devices  5.99 us (2%)
    mul x1, other arithmetic, make_tables(): jnp.cos(phases).T * weights  35.4 us
    neg x1, other arithmetic, make_tables(): -jnp.sin(phases)  34.5 us
    dot_general x4, matrix products, local(): jnp.dot(receiver_spectra, inverse, preferred_element_type=jnp.float32)  24.1 us
    dot_general x4, matrix products, local(): jnp.dot(panel_now, forward, preferred_element_type=jnp.float32)  13.4 us
    gather x4, local copies, waits for them, and re-layouts, local(): picked = jnp.take(extended, got_index, axis=0).astype(jnp.float32)  13.2 us
    ppermute x4, starting transfers between devices, from_behind(): return lax.ppermute(block, axis, route)  12.6 us
    another operation x4, other arithmetic  11.4 us
    convert_element_type x1, other arithmetic, make_tables(): (jnp.concatenate([jnp.cos(phases), -jnp.sin(phases)], 1) * scaling).astyp...  10.5 us
  transfers between devices with their start and end apart: 9, of which 1 were waited for; matrix products, arithmetic and copies ran while one was open for 52% of the time, Pallas kernels for 0%

commit v1 on v0

v1 whole, which is shorter than its diff:
```python
import functools
import math

import jax
import jax.numpy as jnp
import ml_dtypes
import numpy as np
from jax import lax
from jax.experimental import pallas as pl
from jax.experimental.pallas import tpu as pltpu
from jax.sharding import PartitionSpec as P

NF = 1024
EDGE = 64
STEPS = 4
RECV_DEV = 64
META = 16
ITEMS = 4
BASE = 64
F32 = jnp.float32
BF16 = jnp.bfloat16


def vmem():
    return pl.BlockSpec(memory_space=pltpu.VMEM)


def smem():
    return pl.BlockSpec(memory_space=pltpu.SMEM)


@functools.lru_cache(maxsize=None)
def make_tables(samples, bins, owners):
    ids = np.arange(samples)[:, None] * np.arange(bins)[None, :] % samples
    phases = ids * (2.0 * math.pi / samples)
    scaling = 1.0 / math.sqrt(samples)
    each = bins // owners

    def blocks(real, imag):
        both = np.stack([real.reshape(samples, owners, each), imag.reshape(samples, owners, each)], 2)
        return both.reshape(samples, owners, 2 * each)

    forward = blocks(np.cos(phases), -np.sin(phases)) * scaling
    doubled = np.where(np.arange(bins) == 0, 1.0, 2.0)[None, :] * scaling
    inverse = blocks(np.cos(phases) * doubled, -np.sin(phases) * doubled)
    forward = np.ascontiguousarray(forward.transpose(1, 0, 2)).astype(ml_dtypes.bfloat16)
    inverse = np.ascontiguousarray(inverse.transpose(1, 2, 0)).astype(ml_dtypes.bfloat16)
    return forward, inverse


def transform_kernel(x_ref, table_ref, out_ref):
    out_ref[0] = jnp.dot(x_ref[...], table_ref[0], preferred_element_type=F32).astype(BF16)


def transform_panel(panel, table):
    rows, samples = panel.shape
    owners, _, cols = table.shape
    return pl.pallas_call(
        transform_kernel,
        grid=(owners,),
        out_shape=jax.ShapeDtypeStruct((owners, rows, cols), BF16),
        in_specs=[
            pl.BlockSpec((rows, samples), lambda j: (0, 0)),
            pl.BlockSpec((1, samples, cols), lambda j: (j, 0, 0)),
        ],
        out_specs=pl.BlockSpec((1, rows, cols), lambda j: (j, 0, 0)),
        cost_estimate=pl.CostEstimate(
            flops=2 * rows * samples * cols * owners,
            bytes_accessed=2 * (samples * cols * owners + rows * samples * 2),
            transcendentals=0,
        ),
        compiler_params=pltpu.CompilerParams(vmem_limit_bytes=16 << 20),
        name="panel_dft",
    )(panel, table)


def traces_kernel(x_ref, weight_ref, meta_ref, table_ref, out_ref):
    rows = x_ref.shape[0]
    spectra = jnp.dot(x_ref[...], table_ref[0], preferred_element_type=F32)
    out_ref[0, :rows, :] = (spectra * weight_ref[...]).astype(BF16)
    out_ref[0, rows:, :] = meta_ref[...]


def transform_traces(traces, weight, meta, table):
    rows, samples = traces.shape
    owners, _, cols = table.shape
    return pl.pallas_call(
        traces_kernel,
        grid=(owners,),
        out_shape=jax.ShapeDtypeStruct((owners, rows + META, cols), BF16),
        in_specs=[
            pl.BlockSpec((rows, samples), lambda j: (0, 0)),
            pl.BlockSpec((rows, 1), lambda j: (0, 0)),
            pl.BlockSpec((META, cols), lambda j: (0, 0)),
            pl.BlockSpec((1, samples, cols), lambda j: (j, 0, 0)),
        ],
        out_specs=pl.BlockSpec((1, rows + META, cols), lambda j: (j, 0, 0)),
        cost_estimate=pl.CostEstimate(
            flops=2 * rows * samples * cols * owners,
            bytes_accessed=2 * (samples * cols * owners + rows * samples * 2),
            transcendentals=0,
        ),
        compiler_params=pltpu.CompilerParams(vmem_limit_bytes=16 << 20),
        name="trace_dft",
    )(traces, weight, meta, table)


def product_kernel(plan_ref, got_ref, panels_ref, border_ref, out_ref, gather_ref, summer_ref):
    owners, rows_meta, cols = got_ref.shape
    rows = rows_meta - META
    half = cols // 2
    panel_rows = panels_ref.shape[1]
    per_item = rows // cols
    receivers = summer_ref.shape[0]
    step = pl.program_id(0)

    @pl.when(step == 0)
    def _():
        square = (cols, cols)
        eye = (
            lax.broadcasted_iota(jnp.int32, square, 0) == lax.broadcasted_iota(jnp.int32, square, 1)
        ).astype(BF16)
        for src in range(owners):
            meta = got_ref[src, rows:, :]
            wide = meta.astype(F32)
            turned = lax.dot_general(eye, meta, (((1,), (1,)), ((), ())), preferred_element_type=F32)
            for part in range(per_item):
                at = src * rows + part * cols
                owner = wide[part : part + 1]
                slot = wide[per_item + part : per_item + part + 1]
                number = (owner * RECV_DEV + slot).astype(jnp.int32)
                ids = lax.broadcasted_iota(jnp.int32, (receivers, cols), 0)
                summer_ref[:, at : at + cols] = (ids == number).astype(BF16)
                high = turned[:, 2 * per_item + part : 2 * per_item + part + 1]
                low = turned[:, 3 * per_item + part : 3 * per_item + part + 1]
                index = (high * BASE + low).astype(jnp.int32)
                ids = lax.broadcasted_iota(jnp.int32, (cols, panel_rows + EDGE), 1)
                gather_ref[at : at + cols, :] = (ids == index).astype(BF16)

    extended = jnp.concatenate([panels_ref[plan_ref[step]], border_ref[step]], 0)
    total = jnp.zeros((receivers, cols), F32)
    for src in range(owners):
        at = src * rows
        picked = jnp.dot(gather_ref[at : at + rows, :], extended, preferred_element_type=F32)
        spectra = got_ref[src, :rows, :].astype(F32)
        real_p, imag_p = picked[:, :half], picked[:, half:]
        real_d, imag_d = spectra[:, :half], spectra[:, half:]
        product = jnp.concatenate(
            [real_p * real_d - imag_p * imag_d, real_p * imag_d + imag_p * real_d], 1
        ).astype(BF16)
        total += jnp.dot(summer_ref[:, at : at + rows], product, preferred_element_type=F32)
    result = total.astype(BF16)
    for owner in range(owners):
        out_ref[owner, 0] = result[owner * RECV_DEV : (owner + 1) * RECV_DEV]


def receivers_of(plan_row, got, panels, border):
    owners, rows_meta, cols = got.shape
    rows = rows_meta - META
    panel_rows = panels.shape[1]
    receivers = owners * RECV_DEV
    extent = panel_rows + EDGE
    return pl.pallas_call(
        product_kernel,
        grid=(STEPS,),
        out_shape=jax.ShapeDtypeStruct((owners, STEPS, RECV_DEV, cols), BF16),
        in_specs=[smem(), vmem(), vmem(), vmem()],
        out_specs=pl.BlockSpec((owners, 1, RECV_DEV, cols), lambda k: (0, k, 0, 0)),
        scratch_shapes=[
            pltpu.VMEM((owners * rows, extent), BF16),
            pltpu.VMEM((receivers, owners * rows), BF16),
        ],
        cost_estimate=pl.CostEstimate(
            flops=2 * STEPS * owners * rows * cols * (extent + receivers),
            bytes_accessed=2 * cols * owners * (rows + panel_rows + STEPS * RECV_DEV),
            transcendentals=0,
        ),
        compiler_params=pltpu.CompilerParams(vmem_limit_bytes=40 << 20),
        name="receiver_sums",
    )(plan_row, got, panels, border)


def inverse_kernel(x_ref, table_ref, out_ref):
    owners = x_ref.shape[0]
    steps, receivers, width = out_ref.shape
    total = jnp.zeros((steps * receivers, width), F32)
    for owner in range(owners):
        total += jnp.dot(x_ref[owner], table_ref[owner], preferred_element_type=F32)
    out_ref[...] = total.astype(BF16).reshape(steps, receivers, width)


def inverse_of(spectra, table):
    owners, steps, receivers, cols = spectra.shape
    samples = table.shape[2]
    width = min(samples, 512)
    return pl.pallas_call(
        inverse_kernel,
        grid=(samples // width,),
        out_shape=jax.ShapeDtypeStruct((steps, receivers, samples), BF16),
        in_specs=[
            pl.BlockSpec((owners, steps * receivers, cols), lambda j: (0, 0, 0)),
            pl.BlockSpec((owners, cols, width), lambda j: (0, 0, j)),
        ],
        out_specs=pl.BlockSpec((steps, receivers, width), lambda j: (0, 0, j)),
        cost_estimate=pl.CostEstimate(
            flops=2 * owners * steps * receivers * cols * samples,
            bytes_accessed=2 * owners * cols * samples,
            transcendentals=0,
        ),
        compiler_params=pltpu.CompilerParams(vmem_limit_bytes=24 << 20),
        name="inverse_dft",
    )(spectra.reshape(owners, steps * receivers, cols), table)


def exchange(blocks):
    return lax.all_to_all(blocks, "line", split_axis=0, concat_axis=0, tiled=True)


def local(traces, owner, panel_index, receiver_slot, aperture_weight, panels, plan):
    owners = lax.axis_size("line")
    areas = lax.axis_size("area")
    rows, samples = traces.shape
    cols = 2 * NF // owners
    forward, inverse = make_tables(samples, NF, owners)
    forward = jnp.asarray(forward)
    inverse = jnp.asarray(inverse)
    plan_row = plan[lax.axis_index("area")]

    panel_blocks = exchange(transform_panel(panels[0, 0], forward))
    edges = jnp.stack([panel_blocks[plan_row[k], -EDGE:] for k in range(STEPS)], 0)
    border = lax.ppermute(edges, "area", [(i, i + 1) for i in range(areas - 1)])

    items = [owner[:, 0], receiver_slot, panel_index // BASE, panel_index % BASE]
    meta = jnp.stack(items, 0).reshape(-1, cols).astype(BF16)
    meta = jnp.pad(meta, ((0, META - meta.shape[0]), (0, 0)))
    got = exchange(transform_traces(traces, aperture_weight[:, None], meta, forward))

    sums = exchange(receivers_of(plan_row, got, panel_blocks, border))
    return inverse_of(sums, inverse)


def solution(mesh):
    in_specs = (
        P(("area", "line"), None),
        P(("area", "line"), None),
        P(("area", "line")),
        P(("area", "line")),
        P(("area", "line")),
        P("area", "line", None, None),
        P(),
    )
    out_specs = P(None, ("area", "line"), None)
    return jax.shard_map(local, mesh=mesh, in_specs=in_specs, out_specs=out_specs, check_vma=False)
```

time: 245 us -> 84.6 us (0.35)
  other arithmetic: 115 us -> 0.06 us
  matrix products: 46.6 us -> 0 us
  Pallas kernels: 0 us -> 22.8 us
  local copies, waits for them, and re-layouts: 30.8 us -> 12.3 us
  starting transfers between devices: 30.4 us -> 12.2 us
  blocking collectives: 0 us -> 18 us
  between operations: 16.3 us -> 7.67 us
  waiting for transfers between devices: 5.99 us -> 11.1 us
    dot_general x9 -> x0, matrix products: 46.6 us -> none  [the longest x4 24.1 us: local(): jnp.dot(receiver_spectra, inverse, preferred_element_type=jnp.float32)]
    mul x1 -> x0, other arithmetic: 35.4 us -> none  [make_tables(): jnp.cos(phases).T * weights]
    neg x1 -> x0, other arithmetic: 34.5 us -> none  [make_tables(): -jnp.sin(phases)]
    convert_element_type x6 -> x0, other arithmetic: 24.4 us -> none  [the longest x1 10.5 us: make_tables(): (jnp.concatenate([jnp.cos(phases), -jnp.sin(phases)], 1) * scaling).astyp...]
    pallas_call x0 -> x4, Pallas kernels: none -> 22.8 us  [the longest x1 8.75 us: receivers_of(): pl.pallas_call(product_kernel, grid=(STEPS,), out_shape=jax.ShapeDtypeStr...]
    all_to_all x0 -> x1, blocking collectives: none -> 18 us  [exchange(): lax.all_to_all(blocks, 'line', split_axis=0, concat_axis=0, tiled=True)]
    gather x4 -> x0, local copies, waits for them, and re-layouts: 13.2 us -> none  [local(): picked = jnp.take(extended, got_index, axis=0).astype(jnp.float32)]
    another operation x5, other arithmetic: 12.5 us -> 0.06 us  [the longest x1 0.02 us: local(): jnp.stack([panel_blocks[plan_row[k], -EDGE:] for k in range(STEPS)], 0)]
  transfers between devices with their start and end apart: 9 -> 3, of which waited for: 1 -> 2; matrix products, arithmetic and copies ran while one was open for 52% -> 1% of each run, Pallas kernels for 0% -> 6%
where the time goes in v1:
time: 84.6 us; the launch traced here: 84.1 us
  Pallas kernels  22.8 us (27%)
  blocking collectives  18 us (21%)
  local copies, waits for them, and re-layouts  12.3 us (15%)
  starting transfers between devices  12.2 us (14%)
  waiting for transfers between devices  11.1 us (13%)
  between operations  7.67 us (9%)
    all_to_all x1, blocking collectives, exchange(): lax.all_to_all(blocks, 'line', split_axis=0, concat_axis=0, tiled=True)  18 us
    unnamed x20, local copies, waits for them, and re-layouts  11.4 us
    all_to_all x2, waiting for transfers between devices, exchange(): lax.all_to_all(blocks, 'line', split_axis=0, concat_axis=0, tiled=True)  11.1 us
    pallas_call x1, Pallas kernels, receivers_of(): pl.pallas_call(product_kernel, grid=(STEPS,), out_shape=jax.ShapeDtypeStr...  8.75 us
    all_to_all x2, starting transfers between devices, exchange(): lax.all_to_all(blocks, 'line', split_axis=0, concat_axis=0, tiled=True)  8.73 us
    pallas_call x1, Pallas kernels, transform_traces(): pl.pallas_call(traces_kernel, grid=(owners,), out_shape=jax.ShapeDtypeStr...  4.92 us
    pallas_call x1, Pallas kernels, transform_panel(): pl.pallas_call(transform_kernel, grid=(owners,), out_shape=jax.ShapeDtype...  4.87 us
    pallas_call x1, Pallas kernels, inverse_of(): pl.pallas_call(inverse_kernel, grid=(samples // width,), out_shape=jax.Sh...  4.24 us
  transfers between devices with their start and end apart: 3, of which 2 were waited for; matrix products, arithmetic and copies ran while one was open for 1% of the time, Pallas kernels for 6%

profile of v1, /device:TPU:0, one launch (start us, length us, event | category | flops | bytes accessed | tf_op | source)
XLA Modules:
  0.0 84.1 jit_solution(16378686185735093902)
XLA Ops:
  0.0 0.0 copy-start
  0.0 3.4 %copy-done.1 = bf16[8,2048,256]{2,1,0:T(8,128)(2,1)S(1)} copy-done((bf16[8,2048,256]{2,1,0:T(8,128)(2,1)S(1)}, bf16[8,2048,256]{2,1,0:T(8,128)(2,1)}, u32[]{:S(2)}) %copy-start.1) | copy-done | bytes 8388632
  3.4 1.2 %copy-done.4 = bf16[1,1,256,2048]{3,2,1,0:T(8,128)(2,1)S(1)} copy-done((bf16[1,1,256,2048]{3,2,1,0:T(8,128)(2,1)S(1)}, bf16[1,1,256,2048]{3,2,1,0:T(8,128)(2,1)}, u32[]{:S(2)}) %copy-start.4) | copy-done | bytes 1048600
  4.7 4.9 %panel_dft.1 = bf16[8,256,256]{2,1,0:T(8,128)(2,1)} custom-call(bf16[256,2048]{1,0:T(8,128)(2,1)S(1)} %bitcast.12, bf16[8,2048,256]{2,1,0:T(8,128)(2,1)S(1)} %copy-done.1), custom_call_target="tpu_custom_call" | custom-call | flops 2147483648 | bytes 10485760 | tf_op jit(solution)/shard_map/panel_dft/pallas_call | solution.py:58
  9.5 5.2 %all-to-all-start.1 = ((bf16[8,256,256]{2,1,0:T(8,128)(2,1)}), bf16[8,256,256]{2,1,0:T(8,128)(2,1)S(1)}, u32[]{:S(2)}, u32[]{:S(2)}) async-start(bf16[8,256,256]{2,1,0:T(8,128)(2,1)} %panel_dft.1), calls=%async_computation.1 | async-start | bytes 2097152 | tf_op jit(solution)/shard_map/all_to_all | solution.py:216
  14.7 0.0 copy-done.9
  14.7 0.0 copy-done.7
  14.8 0.0 copy-done.6
  14.8 0.1 copy.10.weight_ref
  14.9 0.0 copy-done.8
  15.0 0.0 copy-done.5
  15.0 0.0 copy-start.2
  15.0 3.4 %copy-done.2 = bf16[8,2048,256]{2,1,0:T(8,128)(2,1)S(1)} copy-done((bf16[8,2048,256]{2,1,0:T(8,128)(2,1)S(1)}, bf16[8,2048,256]{2,1,0:T(8,128)(2,1)}, u32[]{:S(2)}) %copy-start.2) | copy-done | bytes 8388632
  18.4 4.9 %trace_dft.1 = bf16[8,272,256]{2,1,0:T(8,128)(2,1)} custom-call(bf16[256,2048]{1,0:T(8,128)(2,1)S(1)} %copy-done.5, f32[256,1]{1,0:T(8,128)S(1)} %copy.10.weight_ref, bf16[16,256]{1,0:T(8,128)(2,1)S(1)} %fusion.6.meta_ref, bf16[8,2048,256]{2,1,0:T(8,128)(2,1)S(1)} %copy-done.2), custom_call_target="tpu_custom_call" | custom-call | flops 2147483648 | bytes 10485760 | tf_op jit(solution)/shard_map/trace_dft/pallas_call | solution.py:87
  23.3 6.8 %all-to-all-done.1.panels_ref = bf16[8,256,256]{2,1,0:T(8,128)(2,1)S(1)} async-done(((bf16[8,256,256]{2,1,0:T(8,128)(2,1)}), bf16[8,256,256]{2,1,0:T(8,128)(2,1)S(1)}, u32[]{:S(2)}, u32[]{:S(2)}) %all-to-all-start.1) | async-done | bytes 1048608 | tf_op jit(solution)/shard_map/all_to_all | solution.py:216
  30.1 3.6 %all-to-all-start = ((bf16[8,272,256]{2,1,0:T(8,128)(2,1)}), bf16[8,272,256]{2,1,0:T(8,128)(2,1)S(1)}, u32[]{:S(2)}, u32[]{:S(2)}) async-start(bf16[8,272,256]{2,1,0:T(8,128)(2,1)} %trace_dft.1), calls=%async_computation | async-start | bytes 2228224 | tf_op jit(solution)/shard_map/all_to_all | solution.py:216
  33.7 0.7 fusion.9
  41.9 3.5 %collective-permute-start = (bf16[4,64,256]{2,1,0:T(8,128)(2,1)S(1)}, bf16[4,64,256]{2,1,0:T(8,128)(2,1)S(1)}, u32[]{:S(2)}, u32[]{:S(2)}) collective-permute-start(bf16[4,64,256]{2,1,0:T(8,128)(2,1)S(1)} %pad_maximum_fusion), channel_id=1, source_target_pairs={{0,8},{8,16},{16,24},{1,9},{9,17},{17,25},{2,10},{10,18},{18,26},{... | collective-permute-start | bytes 393224 | tf_op jit(solution)/shard_map/ppermute | solution.py:231
  45.5 4.3 %all-to-all-done.got_ref = bf16[8,272,256]{2,1,0:T(8,128)(2,1)S(1)} async-done(((bf16[8,272,256]{2,1,0:T(8,128)(2,1)}), bf16[8,272,256]{2,1,0:T(8,128)(2,1)S(1)}, u32[]{:S(2)}, u32[]{:S(2)}) %all-to-all-start) | async-done | bytes 1114144 | tf_op jit(solution)/shard_map/all_to_all | solution.py:216
  49.7 0.0 collective-permute-done.border_ref
  49.7 8.7 %receiver_sums.1 = bf16[8,4,64,256]{3,2,1,0:T(8,128)(2,1)S(1)} custom-call(s32[4]{0:T(128)S(1)} %fusion.10.plan_ref, bf16[8,272,256]{2,1,0:T(8,128)(2,1)S(1)} %all-to-all-done.got_ref, bf16[8,256,256]{2,1,0:T(8,128)(2,1)S(1)} %all-to-all-done.1.panels_ref, bf16[4,64,256]{2,1,0:T(8,128)(2,1)S(1)} %collective-permute-done.border_ref), custom_call_target="tpu_custom_call" | custom-call | flops 3489660928 | bytes 3145728 | tf_op jit(solution)/shard_map/receiver_sums/pallas_call | solution.py:163
  58.5 18.0 %all_to_all.15 = bf16[8,4,64,256]{3,2,1,0:T(8,128)(2,1)S(1)} all-to-all(bf16[8,4,64,256]{3,2,1,0:T(8,128)(2,1)S(1)} %receiver_sums.1), channel_id=1, replica_groups=mesh['area'=4,'line'=8] {'line'}, dimensions={0} | all-to-all | bytes 2097152 | tf_op jit(solution)/shard_map/all_to_all | solution.py:216
  76.5 3.4 %copy-done.3 = bf16[8,256,2048]{2,1,0:T(8,128)(2,1)S(1)} copy-done((bf16[8,256,2048]{2,1,0:T(8,128)(2,1)S(1)}, bf16[8,256,2048]{2,1,0:T(8,128)(2,1)}, u32[]{:S(2)}) %copy-start.3) | copy-done | bytes 8388632
  79.9 4.2 %inverse_dft.1 = bf16[4,64,2048]{2,1,0:T(8,128)(2,1)} custom-call(bf16[8,256,256]{2,1,0:T(8,128)(2,1)S(1)} %bitcast.11, bf16[8,256,2048]{2,1,0:T(8,128)(2,1)S(1)} %copy-done.3), custom_call_target="tpu_custom_call" | custom-call | flops 2147483648 | bytes 8388608 | tf_op jit(solution)/shard_map/inverse_dft/pallas_call | solution.py:196
  (20 shorter events, 0.1 us)
Async XLA Ops:
  0.0 33.7 %copy-start = (s32[4,4]{1,0:T(4,128)S(1)}, s32[4,4]{1,0:T(4,128)}, u32[]{:S(2)}) copy-start(s32[4,4]{1,0:T(4,128)} %param.15) | copy-start | bytes 196
  0.0 14.8 %copy-start.6 = (f32[256]{0:T(256)S(1)}, f32[256]{0:T(256)}, u32[]{:S(2)}) copy-start(f32[256]{0:T(256)} %param.13) | copy-start | bytes 3076
  0.0 3.4 %copy-start.1 = (bf16[8,2048,256]{2,1,0:T(8,128)(2,1)S(1)}, bf16[8,2048,256]{2,1,0:T(8,128)(2,1)}, u32[]{:S(2)}) copy-start(bf16[8,2048,256]{2,1,0:T(8,128)(2,1)} %constant.46.clone.table_ref) | copy-start | bytes 25165828
  3.4 1.2 %copy-start.4 = (bf16[1,1,256,2048]{3,2,1,0:T(8,128)(2,1)S(1)}, bf16[1,1,256,2048]{3,2,1,0:T(8,128)(2,1)}, u32[]{:S(2)}) copy-start(bf16[1,1,256,2048]{3,2,1,0:T(8,128)(2,1)} %param.14) | copy-start | bytes 3145732
  4.6 10.1 %copy-start.9 = (s32[256]{0:T(256)S(1)}, s32[256]{0:T(256)}, u32[]{:S(2)}) copy-start(s32[256]{0:T(256)} %param.12) | copy-start | bytes 3076
  4.6 10.1 %copy-start.7 = (s32[256]{0:T(256)S(1)}, s32[256]{0:T(256)}, u32[]{:S(2)}) copy-start(s32[256]{0:T(256)} %param.11) | copy-start | bytes 3076
  4.6 10.3 %copy-start.8 = (s32[256,1]{0,1:T(1,128)S(1)}, s32[256,1]{0,1:T(1,128)}, u32[]{:S(2)}) copy-start(s32[256,1]{0,1:T(1,128)} %param.10) | copy-start | bytes 3076
  4.6 10.3 %copy-start.5 = (bf16[256,2048]{1,0:T(8,128)(2,1)S(1)}, bf16[256,2048]{1,0:T(8,128)(2,1)}, u32[]{:S(2)}) copy-start(bf16[256,2048]{1,0:T(8,128)(2,1)} %x_ref.1) | copy-start | bytes 3145732
  9.5 20.6 %all-to-all-start.1 = ((bf16[8,256,256]{2,1,0:T(8,128)(2,1)}), bf16[8,256,256]{2,1,0:T(8,128)(2,1)S(1)}, u32[]{:S(2)}, u32[]{:S(2)}) async-start(bf16[8,256,256]{2,1,0:T(8,128)(2,1)} %panel_dft.1), calls=%async_computation.1 | async-start | bytes 2097152 | tf_op jit(solution)/shard_map/all_to_all | solution.py:216
  15.0 3.4 %copy-start.2 = (bf16[8,2048,256]{2,1,0:T(8,128)(2,1)S(1)}, bf16[8,2048,256]{2,1,0:T(8,128)(2,1)}, u32[]{:S(2)}) copy-start(bf16[8,2048,256]{2,1,0:T(8,128)(2,1)} %constant.46.clone.table_ref) | copy-start | bytes 25165828
  30.1 19.6 %all-to-all-start = ((bf16[8,272,256]{2,1,0:T(8,128)(2,1)}), bf16[8,272,256]{2,1,0:T(8,128)(2,1)S(1)}, u32[]{:S(2)}, u32[]{:S(2)}) async-start(bf16[8,272,256]{2,1,0:T(8,128)(2,1)} %trace_dft.1), calls=%async_computation | async-start | bytes 2228224 | tf_op jit(solution)/shard_map/all_to_all | solution.py:216
  41.9 7.8 %collective-permute-start = (bf16[4,64,256]{2,1,0:T(8,128)(2,1)S(1)}, bf16[4,64,256]{2,1,0:T(8,128)(2,1)S(1)}, u32[]{:S(2)}, u32[]{:S(2)}) collective-permute-start(bf16[4,64,256]{2,1,0:T(8,128)(2,1)S(1)} %pad_maximum_fusion), channel_id=1, source_target_pairs={{0,8},{8,16},{16,24},{1,9},{9,17},{17,25},{2,10},{10,18},{18,26},{... | collective-permute-start | bytes 393224 | tf_op jit(solution)/shard_map/ppermute | solution.py:231
  76.5 3.4 %copy-start.3 = (bf16[8,256,2048]{2,1,0:T(8,128)(2,1)S(1)}, bf16[8,256,2048]{2,1,0:T(8,128)(2,1)}, u32[]{:S(2)}) copy-start(bf16[8,256,2048]{2,1,0:T(8,128)(2,1)} %constant.47.clone.table_ref) | copy-start | bytes 25165828

commit v2 on v0

v2 whole, which is shorter than its diff:
```python
import functools
import math

import jax
import jax.numpy as jnp
import ml_dtypes
import numpy as np
from jax import lax
from jax.experimental import pallas as pl
from jax.experimental.pallas import tpu as pltpu
from jax.sharding import PartitionSpec as P

NF = 1024
EDGE = 64
STEPS = 4
RECV_DEV = 64
CHUNK = 2
INDEX_SPAN = 512
F32 = jnp.float32
BF16 = jnp.bfloat16
I32 = jnp.int32


def vmem():
    return pl.BlockSpec(memory_space=pltpu.VMEM)


def smem():
    return pl.BlockSpec(memory_space=pltpu.SMEM)


def params(mib):
    return pltpu.CompilerParams(vmem_limit_bytes=mib << 20)


@functools.lru_cache(maxsize=None)
def make_tables(samples, bins, owners):
    half = samples // 2
    each = bins // owners
    of_bins = np.arange(bins).reshape(bins // 2, 2).T.reshape(owners, each)
    ids = np.arange(half)[None, :, None] * of_bins[:, None, :] % samples
    phases = ids * (2.0 * math.pi / samples)
    scaling = 1.0 / math.sqrt(samples)
    both = np.concatenate([np.cos(phases), -np.sin(phases)], 2) * scaling
    doubled = np.where(of_bins == 0, 1.0, 2.0)
    forward = both.astype(ml_dtypes.bfloat16)
    inverse = both * np.concatenate([doubled, doubled], 1)[:, None, :]
    inverse = np.ascontiguousarray(inverse.transpose(0, 2, 1)).astype(ml_dtypes.bfloat16)
    return forward, inverse


def forward_kernel(chips, count, ids_ref, *refs):
    inputs, tables, outs = refs[:count], refs[count : count + chips], refs[count + chips :]
    sign = ids_ref[chips].astype(F32)
    for number, x_ref in enumerate(inputs):
        rows, samples = x_ref.shape
        low = x_ref[:, : samples // 2].astype(F32)
        high = x_ref[:, samples // 2 :].astype(F32) * sign
        folded = ((low + high).astype(BF16), (low - high).astype(BF16))
        for distance in range(chips):
            spectra = jnp.dot(
                folded[2 * distance // chips],
                tables[distance][0],
                preferred_element_type=F32,
            )
            outs[distance][number * rows : (number + 1) * rows, :] = spectra.astype(BF16)


def forward_of(ids, arrays, table, name):
    rows, samples = arrays[0].shape
    owners, half, cols = table.shape
    chips = owners // 2
    count = len(arrays)

    def table_spec(distance):
        return pl.BlockSpec((1, half, cols), lambda i, ids_ref: (ids_ref[distance], 0, 0))

    whole = pl.BlockSpec((rows, samples), lambda i, ids_ref: (0, 0))
    out = pl.BlockSpec((count * rows, cols), lambda i, ids_ref: (0, 0))
    return pl.pallas_call(
        functools.partial(forward_kernel, chips, count),
        grid_spec=pltpu.PrefetchScalarGridSpec(
            num_scalar_prefetch=1,
            grid=(1,),
            in_specs=[whole] * count + [table_spec(d) for d in range(chips)],
            out_specs=[out] * chips,
        ),
        out_shape=[jax.ShapeDtypeStruct((count * rows, cols), BF16)] * chips,
        cost_estimate=pl.CostEstimate(
            flops=2 * count * rows * half * cols * chips,
            bytes_accessed=2 * (half * cols * chips + count * rows * samples * 2),
            transcendentals=0,
        ),
        compiler_params=params(48),
        name=name,
    )(ids, *arrays, *[table] * chips)


def masks_kernel(ids_ref, facts_ref, gather_ref, summer_ref, weight_ref, rows_ref):
    owners, _, rows = facts_ref.shape
    chips = owners // 2
    chip, core = ids_ref[chips + 1], ids_ref[chips + 2]
    receivers = summer_ref.shape[0]
    extent = gather_ref.shape[1]
    for block in range(owners):
        line = (chip ^ (block // 2)) * 2 + (core ^ (block % 2))
        facts = facts_ref[line]
        packed = facts[0:1].astype(I32)
        index = packed % INDEX_SPAN
        slot = packed // INDEX_SPAN % RECV_DEV
        owner = packed // (INDEX_SPAN * RECV_DEV)
        place = (((owner // 2) ^ chip) * 2 + ((owner % 2) ^ core)) * RECV_DEV + slot
        ids = lax.broadcasted_iota(I32, (receivers, rows), 0)
        summer_ref[:, block * rows : (block + 1) * rows] = (ids == place).astype(BF16)
        rows_ref[block : block + 1, :] = index.astype(F32)
        rows_ref[owners + block : owners + block + 1, :] = facts[1:2]
    square = (rows, rows)
    eye = (
        lax.broadcasted_iota(I32, square, 0) == lax.broadcasted_iota(I32, square, 1)
    ).astype(F32)
    turned = lax.dot_general(
        eye,
        rows_ref[...],
        (((1,), (1,)), ((), ())),
        precision=lax.Precision.HIGHEST,
        preferred_element_type=F32,
    )
    weight_ref[...] = turned[:, owners:]
    ids = lax.broadcasted_iota(I32, (rows, extent), 1)
    for block in range(owners):
        index = turned[:, block : block + 1].astype(I32)
        gather_ref[block * rows : (block + 1) * rows, :] = (ids == index).astype(BF16)


def masks_of(ids, facts, extent):
    owners, _, rows = facts.shape
    return pl.pallas_call(
        masks_kernel,
        out_shape=[
            jax.ShapeDtypeStruct((owners * rows, extent), BF16),
            jax.ShapeDtypeStruct((owners * RECV_DEV, owners * rows), BF16),
            jax.ShapeDtypeStruct((rows, owners), F32),
        ],
        in_specs=[smem(), vmem()],
        out_specs=[vmem()] * 3,
        scratch_shapes=[pltpu.VMEM((2 * owners, rows), F32)],
        cost_estimate=pl.CostEstimate(
            flops=6 * owners * rows * (extent + owners * RECV_DEV),
            bytes_accessed=2 * owners * rows * (extent + owners * RECV_DEV),
            transcendentals=0,
        ),
        compiler_params=params(48),
        name="masks",
    )(ids, facts)


def choose_kernel(chosen_ref, *refs):
    blocks, main_ref, edges_ref = refs[:-2], refs[-2], refs[-1]
    for step in range(STEPS):
        for number, block in enumerate(blocks):

            @pl.when(chosen_ref[step] == number)
            def _():
                main_ref[step] = block[...]
                edges_ref[step] = block[block.shape[0] - EDGE :, :]


def choose(chosen, blocks):
    rows, cols = blocks[0].shape
    return pl.pallas_call(
        choose_kernel,
        out_shape=[
            jax.ShapeDtypeStruct((STEPS, rows, cols), BF16),
            jax.ShapeDtypeStruct((STEPS, EDGE, cols), BF16),
        ],
        in_specs=[smem()] + [vmem()] * len(blocks),
        out_specs=[vmem()] * 2,
        cost_estimate=pl.CostEstimate(
            flops=STEPS * rows * cols,
            bytes_accessed=2 * (len(blocks) + STEPS) * rows * cols,
            transcendentals=0,
        ),
        compiler_params=params(48),
        name="choose_panels",
    )(chosen, *blocks)


def product_kernel(first, chips, *refs):
    main_ref, border_ref, gather_ref, summer_ref, weight_ref = refs[:5]
    spectra_refs, outs = refs[5 : 5 + chips], refs[5 + chips :]
    cols = main_ref.shape[2]
    half = cols // 2
    rows = weight_ref.shape[0]
    receivers = summer_ref.shape[0]
    extended = [
        jnp.concatenate([main_ref[first + step], border_ref[first + step]], 0)
        for step in range(CHUNK)
    ]
    totals = [jnp.zeros((receivers, cols), F32) for _ in range(CHUNK)]
    for block in range(2 * chips):
        at = block * rows
        mine = block % 2 * rows
        spectra = spectra_refs[block // 2][mine : mine + rows, :].astype(F32)
        spectra = spectra * weight_ref[:, block : block + 1]
        real_d, imag_d = spectra[:, :half], spectra[:, half:]
        for step in range(CHUNK):
            picked = jnp.dot(
                gather_ref[at : at + rows, :], extended[step], preferred_element_type=F32
            )
            real_p, imag_p = picked[:, :half], picked[:, half:]
            product = jnp.concatenate(
                [real_p * real_d - imag_p * imag_d, real_p * imag_d + imag_p * real_d], 1
            ).astype(BF16)
            totals[step] += jnp.dot(
                summer_ref[:, at : at + rows], product, preferred_element_type=F32
            )
    for step in range(CHUNK):
        result = totals[step].astype(BF16)
        for place in range(2 * chips):
            rows_of = result[place * RECV_DEV : (place + 1) * RECV_DEV]
            outs[place // 2][place % 2, step] = rows_of


def receivers_of(first, main, border, gather, summer, weight, spectra):
    chips = len(spectra)
    cols = main.shape[2]
    return pl.pallas_call(
        functools.partial(product_kernel, first, chips),
        out_shape=[jax.ShapeDtypeStruct((2, CHUNK, RECV_DEV, cols), BF16)] * chips,
        in_specs=[vmem()] * (5 + chips),
        out_specs=[vmem()] * chips,
        cost_estimate=pl.CostEstimate(
            flops=2 * CHUNK * cols * gather.shape[0] * (gather.shape[1] + summer.shape[0]),
            bytes_accessed=2 * (gather.size + summer.size + gather.shape[0] * cols),
            transcendentals=0,
        ),
        compiler_params=params(48),
        name="receiver_sums",
    )(main, border, gather, summer, weight, *spectra)


def inverse_kernel(chips, ids_ref, *refs):
    per_chunk = chips + 1
    chunks = STEPS // CHUNK
    groups = [refs[i * per_chunk : (i + 1) * per_chunk] for i in range(chunks)]
    tables = refs[chunks * per_chunk : -1]
    out_ref = refs[-1]
    samples = out_ref.shape[2]
    width = tables[0].shape[2]
    cols = tables[0].shape[1]
    sign = ids_ref[2 * chips].astype(F32)
    sums = [None, None]
    for distance in range(chips):
        for across in range(2):
            parts = []
            for group in groups:
                part = group[distance][0] if across == 0 else group[chips][distance]
                parts.append(part.reshape(CHUNK * RECV_DEV, cols))
            term = jnp.dot(
                jnp.concatenate(parts, 0),
                tables[2 * distance + across][0],
                preferred_element_type=F32,
            )
            which = 2 * distance // chips
            sums[which] = term if sums[which] is None else sums[which] + term
    shape = (STEPS, RECV_DEV, width)
    at = pl.multiple_of(pl.program_id(0) * width, width)
    out_ref[:, :, pl.ds(at, width)] = (sums[0] + sums[1]).astype(BF16).reshape(shape)
    at = pl.multiple_of(pl.program_id(0) * width + samples // 2, width)
    out_ref[:, :, pl.ds(at, width)] = ((sums[0] - sums[1]) * sign).astype(BF16).reshape(shape)


def inverse_of(ids, groups, table):
    owners, cols, half = table.shape
    chips = owners // 2
    width = min(half, 256)
    arrays = [array for group in groups for array in group]

    def table_spec(block):
        return pl.BlockSpec((1, cols, width), lambda i, ids_ref: (ids_ref[block], 0, i))

    def whole(array):
        rank = array.ndim
        return pl.BlockSpec(array.shape, lambda i, ids_ref: (0,) * rank)

    return pl.pallas_call(
        functools.partial(inverse_kernel, chips),
        grid_spec=pltpu.PrefetchScalarGridSpec(
            num_scalar_prefetch=1,
            grid=(half // width,),
            in_specs=[whole(a) for a in arrays] + [table_spec(b) for b in range(owners)],
            out_specs=pl.BlockSpec((STEPS, RECV_DEV, 2 * half), lambda i, ids_ref: (0, 0, 0)),
        ),
        out_shape=jax.ShapeDtypeStruct((STEPS, RECV_DEV, 2 * half), BF16),
        cost_estimate=pl.CostEstimate(
            flops=2 * STEPS * RECV_DEV * owners * cols * half,
            bytes_accessed=2 * owners * cols * half,
            transcendentals=0,
        ),
        compiler_params=params(48),
        name="inverse_dft",
    )(ids, *arrays, *[table] * owners)


def swap(array, distance):
    devices = range(lax.axis_size("line"))
    return lax.ppermute(array, "line", [(i, i ^ distance) for i in devices])


def send_blocks(blocks):
    chips = len(blocks)
    sent = {d: swap(blocks[d], 2 * d) for d in range(chips - 1, 0, -1)}
    return [blocks[0]] + [sent[d] for d in range(1, chips)]


def local(traces, owner, panel_index, receiver_slot, aperture_weight, panels, plan):
    owners = lax.axis_size("line")
    areas = lax.axis_size("area")
    chips = owners // 2
    samples = traces.shape[1]
    panel = panels[0, 0]
    forward, inverse = make_tables(samples, NF, owners)
    forward = jnp.asarray(forward)
    inverse = jnp.asarray(inverse)

    line = lax.axis_index("line")
    chip, core = line // 2, line % 2
    sign = jnp.where(2 * chip < chips, 1, -1)
    near = [(chip ^ d) * 2 + core for d in range(chips)]
    near_ids = jnp.stack(near + [sign, chip, core]).astype(I32)
    all_ids = [(chip ^ (b // 2)) * 2 + (core ^ (b % 2)) for b in range(owners)]
    all_ids = jnp.stack(all_ids + [sign]).astype(I32)
    plan_row = plan[lax.axis_index("area")]
    chosen = ((plan_row // 2) ^ chip) * 2 + ((plan_row % 2) ^ core)

    panel_across = swap(panel, 1)
    traces_across = swap(traces, 1)
    packed = (owner[:, 0] * RECV_DEV + receiver_slot) * INDEX_SPAN + panel_index
    facts = jnp.stack([packed.astype(F32), aperture_weight], 0)
    facts = lax.all_gather(facts, "line")

    near_panels = send_blocks(forward_of(near_ids, [panel], forward, "panel_dft"))
    far_panels = send_blocks(forward_of(near_ids, [panel_across], forward, "panel_dft"))
    spectra = send_blocks(forward_of(near_ids, [traces, traces_across], forward, "trace_dft"))

    blocks = [block for pair in zip(near_panels, far_panels) for block in pair]
    main, edges = choose(chosen, blocks)
    border = lax.ppermute(edges, "area", [(i, i + 1) for i in range(areas - 1)])
    gather, summer, weight = masks_of(near_ids, facts, panel.shape[0] + EDGE)

    groups = []
    for first in range(0, STEPS, CHUNK):
        sums = receivers_of(first, main, border, gather, summer, weight, spectra)
        sums = send_blocks(sums)
        across = swap(jnp.stack([block[1] for block in sums]), 1)
        groups.append(sums + [across])
    return inverse_of(all_ids, groups, inverse)


def solution(mesh):
    in_specs = (
        P(("area", "line"), None),
        P(("area", "line"), None),
        P(("area", "line")),
        P(("area", "line")),
        P(("area", "line")),
        P("area", "line", None, None),
        P(),
    )
    out_specs = P(None, ("area", "line"), None)
    return jax.shard_map(local, mesh=mesh, in_specs=in_specs, out_specs=out_specs, check_vma=False)
```

time: 245 us -> 68.3 us (0.28)
  other arithmetic: 115 us -> 0.79 us
  matrix products: 46.6 us -> 0 us
  local copies, waits for them, and re-layouts: 30.8 us -> 8.03 us
  Pallas kernels: 0 us -> 19.5 us
  between operations: 16.3 us -> 0.31 us
  blocking collectives: 0 us -> 9.53 us
  starting transfers between devices: 30.4 us -> 23.3 us
    dot_general x9 -> x0, matrix products: 46.6 us -> none  [the longest x4 24.1 us: local(): jnp.dot(receiver_spectra, inverse, preferred_element_type=jnp.float32)]
    mul x1, other arithmetic: 35.4 us -> 0.01 us  [local(): packed = (owner[:, 0] * RECV_DEV + receiver_slot) * INDEX_SPAN + panel_index]
    neg x1 -> x0, other arithmetic: 34.5 us -> none  [make_tables(): -jnp.sin(phases)]
    convert_element_type x6 -> x1, other arithmetic: 24.4 us -> 0.01 us  [local(): facts = jnp.stack([packed.astype(F32), aperture_weight], 0)]
    pallas_call x0 -> x8, Pallas kernels: none -> 19.5 us  [the longest x2 6.61 us: receivers_of(): pl.pallas_call(functools.partial(product_kernel, first, chips), out_shape...]
    all_to_all x4 -> x0, starting transfers between devices: 17.7 us -> none  [the longest x1 5.17 us: local(): lax.all_to_all(moved_weight.reshape(line_count, capacity).astype(jnp.bflo...]
    gather x4 -> x0, local copies, waits for them, and re-layouts: 13.2 us -> none  [local(): picked = jnp.take(extended, got_index, axis=0).astype(jnp.float32)]
    another operation x5 -> x2, other arithmetic: 12.5 us -> 0.07 us  [local(): across = swap(jnp.stack([block[1] for block in sums]), 1)]
  transfers between devices with their start and end apart: 9 -> 20, of which waited for: 1 -> 3; matrix products, arithmetic and copies ran while one was open for 52% -> 1% of each run, Pallas kernels for 0% -> 18%
where the time goes in v2:
time: 68.3 us; the launch traced here: 67.9 us
  starting transfers between devices  23.3 us (34%)
  Pallas kernels  19.5 us (29%)
  blocking collectives  9.53 us (14%)
  local copies, waits for them, and re-layouts  8.03 us (12%)
  waiting for transfers between devices  6.41 us (9%)
  other arithmetic  0.79 us (1%)
    ppermute x19, starting transfers between devices, swap(): return lax.ppermute(array, 'line', [(i, i ^ distance) for i in devices])  19.4 us
    all_gather x1, blocking collectives, local(): facts = lax.all_gather(facts, 'line')  9.53 us
    unnamed x18, local copies, waits for them, and re-layouts  7.81 us
    pallas_call x2, Pallas kernels, receivers_of(): pl.pallas_call(functools.partial(product_kernel, first, chips), out_shape...  6.61 us
    ppermute x19, waiting for transfers between devices, swap(): return lax.ppermute(array, 'line', [(i, i ^ distance) for i in devices])  6.4 us
    pallas_call x3, Pallas kernels, forward_of(): pl.pallas_call(functools.partial(forward_kernel, chips, count), grid_spec...  5.9 us
    pallas_call x1, Pallas kernels, inverse_of(): pl.pallas_call(functools.partial(inverse_kernel, chips), grid_spec=pltpu....  4.19 us
    ppermute x1, starting transfers between devices, local(): border = lax.ppermute(edges, 'area', [(i, i + 1) for i in range(areas - 1)])  3.92 us
  transfers between devices with their start and end apart: 20, of which 3 were waited for; matrix products, arithmetic and copies ran while one was open for 1% of the time, Pallas kernels for 18%

profile of v2, /device:TPU:0, one launch (start us, length us, event | category | flops | bytes accessed | tf_op | source)
XLA Modules:
  0.0 67.9 jit_solution(6935150663432265789)
XLA Ops:
  0.6 2.2 %copy-done = bf16[8,1024,256]{2,1,0:T(8,128)(2,1)S(1)} copy-done((bf16[8,1024,256]{2,1,0:T(8,128)(2,1)S(1)}, bf16[8,1024,256]{2,1,0:T(8,128)(2,1)}, u32[]{:S(2)}) %copy-start) | copy-done | bytes 4194328
  2.8 1.2 %copy-done.3 = bf16[1,1,256,2048]{3,2,1,0:T(8,128)(2,1)S(1)} copy-done((bf16[1,1,256,2048]{3,2,1,0:T(8,128)(2,1)S(1)}, bf16[1,1,256,2048]{3,2,1,0:T(8,128)(2,1)}, u32[]{:S(2)}) %copy-start.3) | copy-done | bytes 1048600
  4.0 1.3 %panel_dft.2 = (bf16[256,256]{1,0:T(8,128)(2,1)S(1)}, bf16[256,256]{1,0:T(8,128)(2,1)S(1)}, bf16[256,256]{1,0:T(8,128)(2,1)S(1)}, bf16[256,256]{1,0:T(8,128)(2,1)S(1)}) custom-call(s32[7]{0:T(128)S(1)} %stack.71.ids_ref, bf16[256,2048]{1,0:T(8,128)(2,1)S(1)} %bitcast.31, bf16[8,1024,256]{2,1,0:T(8,128)(2,1)S(1)} %copy-done, ...), custom_call_target="tpu_custom_call" | custom-call | flops 536870912 | bytes 4194304 | tf_op jit(solution)/shard_map/panel_dft/pallas_call | solution.py:80
  5.3 3.0 %collective-permute-start.1 = (bf16[256,256]{1,0:T(8,128)(2,1)S(1)}, bf16[256,256]{1,0:T(8,128)(2,1)S(1)}, u32[]{:S(2)}, u32[]{:S(2)}) collective-permute-start(bf16[256,256]{1,0:T(8,128)(2,1)S(1)} %get-tuple-element.32), channel_id=1, source_target_pairs={{0,2},{1,3},{2,0},{3,1},{4,6},{5,7},{6,4},{7,5},{8,10},{9,11},{10,... | collective-permute-start | bytes 393224 | tf_op jit(solution)/shard_map/ppermute | solution.py:307
  8.3 1.5 %collective-permute-start.3 = (bf16[256,256]{1,0:T(8,128)(2,1)S(1)}, bf16[256,256]{1,0:T(8,128)(2,1)S(1)}, u32[]{:S(2)}, u32[]{:S(2)}) collective-permute-start(bf16[256,256]{1,0:T(8,128)(2,1)S(1)} %get-tuple-element.34), channel_id=1, source_target_pairs={{0,4},{1,5},{2,6},{3,7},{4,0},{5,1},{6,2},{7,3},{8,12},{9,13},{10,... | collective-permute-start | bytes 393224 | tf_op jit(solution)/shard_map/ppermute | solution.py:307
  9.9 2.2 %copy-done.1 = bf16[8,1024,256]{2,1,0:T(8,128)(2,1)S(1)} copy-done((bf16[8,1024,256]{2,1,0:T(8,128)(2,1)S(1)}, bf16[8,1024,256]{2,1,0:T(8,128)(2,1)}, u32[]{:S(2)}) %copy-start.1) | copy-done | bytes 4194328
  12.0 1.3 %panel_dft.3 = (bf16[256,256]{1,0:T(8,128)(2,1)S(1)}, bf16[256,256]{1,0:T(8,128)(2,1)S(1)}, bf16[256,256]{1,0:T(8,128)(2,1)S(1)}, bf16[256,256]{1,0:T(8,128)(2,1)S(1)}) custom-call(s32[7]{0:T(128)S(1)} %stack.71.ids_ref, bf16[256,2048]{1,0:T(8,128)(2,1)S(1)} %collective-permute-done.refs_0_, bf16[8,1024,256]{2,1,0:T(8,128)(2,1)S(1)} %copy-done.1, ...), custom_call_target="tpu_custom_call" | custom-call | flops 536870912 | bytes 4194304 | tf_op jit(solution)/shard_map/panel_dft/pallas_call | solution.py:80
  13.3 2.0 %collective-permute-start.2 = (bf16[256,256]{1,0:T(8,128)(2,1)S(1)}, bf16[256,256]{1,0:T(8,128)(2,1)S(1)}, u32[]{:S(2)}, u32[]{:S(2)}) collective-permute-start(bf16[256,256]{1,0:T(8,128)(2,1)S(1)} %get-tuple-element.33), channel_id=1, source_target_pairs={{0,2},{1,3},{2,0},{3,1},{4,6},{5,7},{6,4},{7,5},{8,10},{9,11},{10,... | collective-permute-start | bytes 393224 | tf_op jit(solution)/shard_map/ppermute | solution.py:307
  15.4 1.5 %collective-permute-start.4 = (bf16[256,256]{1,0:T(8,128)(2,1)S(1)}, bf16[256,256]{1,0:T(8,128)(2,1)S(1)}, u32[]{:S(2)}, u32[]{:S(2)}) collective-permute-start(bf16[256,256]{1,0:T(8,128)(2,1)S(1)} %get-tuple-element.35), channel_id=1, source_target_pairs={{0,4},{1,5},{2,6},{3,7},{4,0},{5,1},{6,2},{7,3},{8,12},{9,13},{10,... | collective-permute-start | bytes 393224 | tf_op jit(solution)/shard_map/ppermute | solution.py:307
  17.7 3.3 %trace_dft.1 = (bf16[512,256]{1,0:T(8,128)(2,1)S(1)}, bf16[512,256]{1,0:T(8,128)(2,1)S(1)}, bf16[512,256]{1,0:T(8,128)(2,1)S(1)}, bf16[512,256]{1,0:T(8,128)(2,1)S(1)}) custom-call(s32[7]{0:T(128)S(1)} %stack.71.ids_ref, bf16[256,2048]{1,0:T(8,128)(2,1)S(1)} %copy-done.4, bf16[256,2048]{1,0:T(8,128)(2,1)S(1)} %collective-permute-done.8.refs_1_, ...), custom_call_target="tpu_custom_call" | custom-call | flops 1073741824 | bytes 6291456 | tf_op jit(solution)/shard_map/trace_dft/pallas_call | solution.py:80
  21.0 2.0 %collective-permute-start.9 = (bf16[512,256]{1,0:T(8,128)(2,1)S(1)}, bf16[512,256]{1,0:T(8,128)(2,1)S(1)}, u32[]{:S(2)}, u32[]{:S(2)}) collective-permute-start(bf16[512,256]{1,0:T(8,128)(2,1)S(1)} %get-tuple-element.44), channel_id=1, source_target_pairs={{0,2},{1,3},{2,0},{3,1},{4,6},{5,7},{6,4},{7,5},{8,10},{9,11},{10,... | collective-permute-start | bytes 786440 | tf_op jit(solution)/shard_map/ppermute | solution.py:307
  23.0 1.5 %collective-permute-start.10 = (bf16[512,256]{1,0:T(8,128)(2,1)S(1)}, bf16[512,256]{1,0:T(8,128)(2,1)S(1)}, u32[]{:S(2)}, u32[]{:S(2)}) collective-permute-start(bf16[512,256]{1,0:T(8,128)(2,1)S(1)} %get-tuple-element.45), channel_id=1, source_target_pairs={{0,4},{1,5},{2,6},{3,7},{4,0},{5,1},{6,2},{7,3},{8,12},{9,13},{10,... | collective-permute-start | bytes 786440 | tf_op jit(solution)/shard_map/ppermute | solution.py:307
  25.4 3.9 %collective-permute-start.7 = (bf16[4,64,256]{2,1,0:T(8,128)(2,1)S(1)}, bf16[4,64,256]{2,1,0:T(8,128)(2,1)S(1)}, u32[]{:S(2)}, u32[]{:S(2)}) collective-permute-start(bf16[4,64,256]{2,1,0:T(8,128)(2,1)S(1)} %get-tuple-element.39), channel_id=1, source_target_pairs={{0,8},{8,16},{16,24},{1,9},{9,17},{17,25},{2,10},{10,18},{18,26},{... | collective-permute-start | bytes 393224 | tf_op jit(solution)/shard_map/ppermute | solution.py:348
  29.4 9.5 %all-gather.1.facts_ref = f32[8,2,256]{2,1,0:T(2,128)S(1)} all-gather(f32[1,2,256]{2,1,0:T(2,128)S(1)} %maximum_bitcast_fusion), channel_id=2, replica_groups=mesh['area'=4,'line'=8] {'line'}, dimensions={0}, use_global_device_ids=true | all-gather | bytes 18432 | tf_op jit(solution)/shard_map/all_gather | solution.py:340
  38.9 2.0 %masks.1 = (bf16[2048,320]{1,0:T(8,128)(2,1)S(1)}, bf16[512,2048]{1,0:T(8,128)(2,1)S(1)}, f32[256,8]{1,0:T(8,128)S(1)}) custom-call(s32[7]{0:T(128)S(1)} %stack.71.ids_ref, f32[8,2,256]{2,1,0:T(2,128)S(1)} %all-gather.1.facts_ref), custom_call_target="tpu_custom_call" | custom-call | flops 10223616 | bytes 3407872 | tf_op jit(solution)/shard_map/masks/pallas_call | solution.py:137
  41.0 3.3 %receiver_sums.2 = (bf16[2,2,64,256]{3,2,1,0:T(8,128)(2,1)S(1)}, bf16[2,2,64,256]{3,2,1,0:T(8,128)(2,1)S(1)}, bf16[2,2,64,256]{3,2,1,0:T(8,128)(2,1)S(1)}, bf16[2,2,64,256]{3,2,1,0:T(8,128)(2,1)S(1)}) custom-call(bf16[4,256,256]{2,1,0:T(8,128)(2,1)S(1)} %get-tuple-element.38.refs_0_, bf16[4,64,256]{2,1,0:T(8,128)(2,1)S(1)} %collective-permute-done.7.refs_1_, ...), custom_call_target="tpu_custom_call" | custom-call | flops 1744830464 | bytes 4456448 | tf_op jit(solution)/shard_map/receiver_sums/pallas_call | solution.py:227
  46.4 1.5 %collective-permute-start.14 = (bf16[2,2,64,256]{3,2,1,0:T(8,128)(2,1)S(1)}, bf16[2,2,64,256]{3,2,1,0:T(8,128)(2,1)S(1)}, u32[]{:S(2)}, u32[]{:S(2)}) collective-permute-start(bf16[2,2,64,256]{3,2,1,0:T(8,128)(2,1)S(1)} %get-tuple-element.50), channel_id=1, source_target_pairs={{0,6},{1,7},{2,4},{3,5},{4,2},{5,3},{6,0},{7,1},{8,14},{9,15},{10,... | collective-permute-start | bytes 393224 | tf_op jit(solution)/shard_map/ppermute | solution.py:307
  47.9 3.3 %receiver_sums.3 = (bf16[2,2,64,256]{3,2,1,0:T(8,128)(2,1)S(1)}, bf16[2,2,64,256]{3,2,1,0:T(8,128)(2,1)S(1)}, bf16[2,2,64,256]{3,2,1,0:T(8,128)(2,1)S(1)}, bf16[2,2,64,256]{3,2,1,0:T(8,128)(2,1)S(1)}) custom-call(bf16[4,256,256]{2,1,0:T(8,128)(2,1)S(1)} %get-tuple-element.38.refs_0_, bf16[4,64,256]{2,1,0:T(8,128)(2,1)S(1)} %collective-permute-done.7.refs_1_, ...), custom_call_target="tpu_custom_call" | custom-call | flops 1744830464 | bytes 4456448 | tf_op jit(solution)/shard_map/receiver_sums/pallas_call | solution.py:227
  53.3 1.5 %collective-permute-start.18 = (bf16[2,2,64,256]{3,2,1,0:T(8,128)(2,1)S(1)}, bf16[2,2,64,256]{3,2,1,0:T(8,128)(2,1)S(1)}, u32[]{:S(2)}, u32[]{:S(2)}) collective-permute-start(bf16[2,2,64,256]{3,2,1,0:T(8,128)(2,1)S(1)} %get-tuple-element.54), channel_id=1, source_target_pairs={{0,6},{1,7},{2,4},{3,5},{4,2},{5,3},{6,0},{7,1},{8,14},{9,15},{10,... | collective-permute-start | bytes 393224 | tf_op jit(solution)/shard_map/ppermute | solution.py:307
  54.9 2.4 %collective-permute-done.16.refs_6_ = bf16[2,2,64,256]{3,2,1,0:T(8,128)(2,1)S(1)} collective-permute-done((bf16[2,2,64,256]{3,2,1,0:T(8,128)(2,1)S(1)}, bf16[2,2,64,256]{3,2,1,0:T(8,128)(2,1)S(1)}, u32[]{:S(2)}, u32[]{:S(2)}) %collective-permute-start.16) | collective-permute-done | bytes 131104 | tf_op jit(solution)/shard_map/ppermute | solution.py:307
  57.3 2.6 %collective-permute-done.17.refs_7_ = bf16[2,2,64,256]{3,2,1,0:T(8,128)(2,1)S(1)} collective-permute-done((bf16[2,2,64,256]{3,2,1,0:T(8,128)(2,1)S(1)}, bf16[2,2,64,256]{3,2,1,0:T(8,128)(2,1)S(1)}, u32[]{:S(2)}, u32[]{:S(2)}) %collective-permute-start.17) | collective-permute-done | bytes 131104 | tf_op jit(solution)/shard_map/ppermute | solution.py:307
  60.1 1.4 %collective-permute-done.19.refs_9_ = bf16[4,2,64,256]{3,2,1,0:T(8,128)(2,1)S(1)} collective-permute-done((bf16[4,2,64,256]{3,2,1,0:T(8,128)(2,1)S(1)}, bf16[4,2,64,256]{3,2,1,0:T(8,128)(2,1)S(1)}, u32[]{:S(2)}, u32[]{:S(2)}) %collective-permute-start.19) | collective-permute-done | bytes 262176 | tf_op jit(solution)/shard_map/ppermute | solution.py:307
  61.6 2.2 %copy-done.2 = bf16[8,256,1024]{2,1,0:T(8,128)(2,1)S(1)} copy-done((bf16[8,256,1024]{2,1,0:T(8,128)(2,1)S(1)}, bf16[8,256,1024]{2,1,0:T(8,128)(2,1)}, u32[]{:S(2)}) %copy-start.2) | copy-done | bytes 4194328
  63.7 4.2 %inverse_dft.1 = bf16[4,64,2048]{2,1,0:T(8,128)(2,1)} custom-call(s32[9]{0:T(128)S(1)} %stack.68.ids_ref, bf16[2,2,64,256]{3,2,1,0:T(8,128)(2,1)S(1)} %get-tuple-element.47.refs_0_, bf16[2,2,64,256]{3,2,1,0:T(8,128)(2,1)S(1)} %collective-permute-done.12.refs_1_, bf16[2,2,64,256]{3,2,1,0:T(8,128)(2,1)S(1)} %collective-permute-done.13.refs_2_, ...), custom_call_target="tpu_custom_call" | custom-call | flops 1073741824 | bytes 4194304 | tf_op jit(solution)/shard_map/inverse_dft/pallas_call | solution.py:286
  (59 shorter events, 6.9 us)
Async XLA Ops:
  0.0 9.8 %collective-permute-start = (bf16[256,2048]{1,0:T(8,128)(2,1)}, bf16[256,2048]{1,0:T(8,128)(2,1)S(1)}, u32[]{:S(2)}, u32[]{:S(2)}) collective-permute-start(bf16[256,2048]{1,0:T(8,128)(2,1)} %bitcast.30), channel_id=1, source_target_pairs={{0,1},{1,0},{2,3},{3,2},{4,5},{5,4},{6,7},{7,6},{8,9},{9,8},{10,11... | collective-permute-start | bytes 3145736 | tf_op jit(solution)/shard_map/ppermute | solution.py:307
  0.5 16.4 %collective-permute-start.8 = (bf16[256,2048]{1,0:T(8,128)(2,1)}, bf16[256,2048]{1,0:T(8,128)(2,1)S(1)}, u32[]{:S(2)}, u32[]{:S(2)}) collective-permute-start(bf16[256,2048]{1,0:T(8,128)(2,1)} %refs_0_.1), channel_id=1, source_target_pairs={{0,1},{1,0},{2,3},{3,2},{4,5},{5,4},{6,7},{7,6},{8,9},{9,8},{10,11... | collective-permute-start | bytes 3145736 | tf_op jit(solution)/shard_map/ppermute | solution.py:307
  4.0 5.8 %copy-start.5 = (s32[256,1]{0,1:T(1,128)S(1)}, s32[256,1]{0,1:T(1,128)}, u32[]{:S(2)}) copy-start(s32[256,1]{0,1:T(1,128)} %param.10) | copy-start | bytes 3076
  5.3 10.1 %collective-permute-start.1 = (bf16[256,256]{1,0:T(8,128)(2,1)S(1)}, bf16[256,256]{1,0:T(8,128)(2,1)S(1)}, u32[]{:S(2)}, u32[]{:S(2)}) collective-permute-start(bf16[256,256]{1,0:T(8,128)(2,1)S(1)} %get-tuple-element.32), channel_id=1, source_target_pairs={{0,2},{1,3},{2,0},{3,1},{4,6},{5,7},{6,4},{7,5},{8,10},{9,11},{10,... | collective-permute-start | bytes 393224 | tf_op jit(solution)/shard_map/ppermute | solution.py:307
  8.3 12.7 %collective-permute-start.3 = (bf16[256,256]{1,0:T(8,128)(2,1)S(1)}, bf16[256,256]{1,0:T(8,128)(2,1)S(1)}, u32[]{:S(2)}, u32[]{:S(2)}) collective-permute-start(bf16[256,256]{1,0:T(8,128)(2,1)S(1)} %get-tuple-element.34), channel_id=1, source_target_pairs={{0,4},{1,5},{2,6},{3,7},{4,0},{5,1},{6,2},{7,3},{8,12},{9,13},{10,... | collective-permute-start | bytes 393224 | tf_op jit(solution)/shard_map/ppermute | solution.py:307
  9.8 13.2 %collective-permute-start.5 = (bf16[256,256]{1,0:T(8,128)(2,1)S(1)}, bf16[256,256]{1,0:T(8,128)(2,1)S(1)}, u32[]{:S(2)}, u32[]{:S(2)}) collective-permute-start(bf16[256,256]{1,0:T(8,128)(2,1)S(1)} %get-tuple-element.36), channel_id=1, source_target_pairs={{0,6},{1,7},{2,4},{3,5},{4,2},{5,3},{6,0},{7,1},{8,14},{9,15},{10,... | collective-permute-start | bytes 393224 | tf_op jit(solution)/shard_map/ppermute | solution.py:307
  13.3 11.2 %collective-permute-start.2 = (bf16[256,256]{1,0:T(8,128)(2,1)S(1)}, bf16[256,256]{1,0:T(8,128)(2,1)S(1)}, u32[]{:S(2)}, u32[]{:S(2)}) collective-permute-start(bf16[256,256]{1,0:T(8,128)(2,1)S(1)} %get-tuple-element.33), channel_id=1, source_target_pairs={{0,2},{1,3},{2,0},{3,1},{4,6},{5,7},{6,4},{7,5},{8,10},{9,11},{10,... | collective-permute-start | bytes 393224 | tf_op jit(solution)/shard_map/ppermute | solution.py:307
  15.4 9.2 %collective-permute-start.4 = (bf16[256,256]{1,0:T(8,128)(2,1)S(1)}, bf16[256,256]{1,0:T(8,128)(2,1)S(1)}, u32[]{:S(2)}, u32[]{:S(2)}) collective-permute-start(bf16[256,256]{1,0:T(8,128)(2,1)S(1)} %get-tuple-element.35), channel_id=1, source_target_pairs={{0,4},{1,5},{2,6},{3,7},{4,0},{5,1},{6,2},{7,3},{8,12},{9,13},{10,... | collective-permute-start | bytes 393224 | tf_op jit(solution)/shard_map/ppermute | solution.py:307
  16.9 7.7 %collective-permute-start.6 = (bf16[256,256]{1,0:T(8,128)(2,1)S(1)}, bf16[256,256]{1,0:T(8,128)(2,1)S(1)}, u32[]{:S(2)}, u32[]{:S(2)}) collective-permute-start(bf16[256,256]{1,0:T(8,128)(2,1)S(1)} %get-tuple-element.37), channel_id=1, source_target_pairs={{0,6},{1,7},{2,4},{3,5},{4,2},{5,3},{6,0},{7,1},{8,14},{9,15},{10,... | collective-permute-start | bytes 393224 | tf_op jit(solution)/shard_map/ppermute | solution.py:307
  17.6 11.7 %copy-start.6 = (s32[256]{0:T(256)S(1)}, s32[256]{0:T(256)}, u32[]{:S(2)}) copy-start(s32[256]{0:T(256)} %param.11) | copy-start | bytes 3076
  17.6 11.7 %copy-start.7 = (s32[256]{0:T(256)S(1)}, s32[256]{0:T(256)}, u32[]{:S(2)}) copy-start(s32[256]{0:T(256)} %param.12) | copy-start | bytes 3076
  17.6 11.7 %copy-start.8 = (f32[256]{0:T(256)S(1)}, f32[256]{0:T(256)}, u32[]{:S(2)}) copy-start(f32[256]{0:T(256)} %param.13) | copy-start | bytes 3076
  21.0 19.9 %collective-permute-start.9 = (bf16[512,256]{1,0:T(8,128)(2,1)S(1)}, bf16[512,256]{1,0:T(8,128)(2,1)S(1)}, u32[]{:S(2)}, u32[]{:S(2)}) collective-permute-start(bf16[512,256]{1,0:T(8,128)(2,1)S(1)} %get-tuple-element.44), channel_id=1, source_target_pairs={{0,2},{1,3},{2,0},{3,1},{4,6},{5,7},{6,4},{7,5},{8,10},{9,11},{10,... | collective-permute-start | bytes 786440 | tf_op jit(solution)/shard_map/ppermute | solution.py:307
  23.0 18.0 %collective-permute-start.10 = (bf16[512,256]{1,0:T(8,128)(2,1)S(1)}, bf16[512,256]{1,0:T(8,128)(2,1)S(1)}, u32[]{:S(2)}, u32[]{:S(2)}) collective-permute-start(bf16[512,256]{1,0:T(8,128)(2,1)S(1)} %get-tuple-element.45), channel_id=1, source_target_pairs={{0,4},{1,5},{2,6},{3,7},{4,0},{5,1},{6,2},{7,3},{8,12},{9,13},{10,... | collective-permute-start | bytes 786440 | tf_op jit(solution)/shard_map/ppermute | solution.py:307
  24.5 16.5 %collective-permute-start.11 = (bf16[512,256]{1,0:T(8,128)(2,1)S(1)}, bf16[512,256]{1,0:T(8,128)(2,1)S(1)}, u32[]{:S(2)}, u32[]{:S(2)}) collective-permute-start(bf16[512,256]{1,0:T(8,128)(2,1)S(1)} %get-tuple-element.46), channel_id=1, source_target_pairs={{0,6},{1,7},{2,4},{3,5},{4,2},{5,3},{6,0},{7,1},{8,14},{9,15},{10,... | collective-permute-start | bytes 786440 | tf_op jit(solution)/shard_map/ppermute | solution.py:307
  25.4 15.5 %collective-permute-start.7 = (bf16[4,64,256]{2,1,0:T(8,128)(2,1)S(1)}, bf16[4,64,256]{2,1,0:T(8,128)(2,1)S(1)}, u32[]{:S(2)}, u32[]{:S(2)}) collective-permute-start(bf16[4,64,256]{2,1,0:T(8,128)(2,1)S(1)} %get-tuple-element.39), channel_id=1, source_target_pairs={{0,8},{8,16},{16,24},{1,9},{9,17},{17,25},{2,10},{10,18},{18,26},{... | collective-permute-start | bytes 393224 | tf_op jit(solution)/shard_map/ppermute | solution.py:348
  44.3 9.0 %collective-permute-start.12 = (bf16[2,2,64,256]{3,2,1,0:T(8,128)(2,1)S(1)}, bf16[2,2,64,256]{3,2,1,0:T(8,128)(2,1)S(1)}, u32[]{:S(2)}, u32[]{:S(2)}) collective-permute-start(bf16[2,2,64,256]{3,2,1,0:T(8,128)(2,1)S(1)} %get-tuple-element.48), channel_id=1, source_target_pairs={{0,2},{1,3},{2,0},{3,1},{4,6},{5,7},{6,4},{7,5},{8,10},{9,11},{10,... | collective-permute-start | bytes 393224 | tf_op jit(solution)/shard_map/ppermute | solution.py:307
  45.2 9.5 %collective-permute-start.13 = (bf16[2,2,64,256]{3,2,1,0:T(8,128)(2,1)S(1)}, bf16[2,2,64,256]{3,2,1,0:T(8,128)(2,1)S(1)}, u32[]{:S(2)}, u32[]{:S(2)}) collective-permute-start(bf16[2,2,64,256]{3,2,1,0:T(8,128)(2,1)S(1)} %get-tuple-element.49), channel_id=1, source_target_pairs={{0,4},{1,5},{2,6},{3,7},{4,0},{5,1},{6,2},{7,3},{8,12},{9,13},{10,... | collective-permute-start | bytes 393224 | tf_op jit(solution)/shard_map/ppermute | solution.py:307
  46.4 8.4 %collective-permute-start.14 = (bf16[2,2,64,256]{3,2,1,0:T(8,128)(2,1)S(1)}, bf16[2,2,64,256]{3,2,1,0:T(8,128)(2,1)S(1)}, u32[]{:S(2)}, u32[]{:S(2)}) collective-permute-start(bf16[2,2,64,256]{3,2,1,0:T(8,128)(2,1)S(1)} %get-tuple-element.50), channel_id=1, source_target_pairs={{0,6},{1,7},{2,4},{3,5},{4,2},{5,3},{6,0},{7,1},{8,14},{9,15},{10,... | collective-permute-start | bytes 393224 | tf_op jit(solution)/shard_map/ppermute | solution.py:307
  51.2 6.1 %collective-permute-start.16 = (bf16[2,2,64,256]{3,2,1,0:T(8,128)(2,1)S(1)}, bf16[2,2,64,256]{3,2,1,0:T(8,128)(2,1)S(1)}, u32[]{:S(2)}, u32[]{:S(2)}) collective-permute-start(bf16[2,2,64,256]{3,2,1,0:T(8,128)(2,1)S(1)} %get-tuple-element.52), channel_id=1, source_target_pairs={{0,2},{1,3},{2,0},{3,1},{4,6},{5,7},{6,4},{7,5},{8,10},{9,11},{10,... | collective-permute-start | bytes 393224 | tf_op jit(solution)/shard_map/ppermute | solution.py:307
  52.1 7.8 %collective-permute-start.17 = (bf16[2,2,64,256]{3,2,1,0:T(8,128)(2,1)S(1)}, bf16[2,2,64,256]{3,2,1,0:T(8,128)(2,1)S(1)}, u32[]{:S(2)}, u32[]{:S(2)}) collective-permute-start(bf16[2,2,64,256]{3,2,1,0:T(8,128)(2,1)S(1)} %get-tuple-element.53), channel_id=1, source_target_pairs={{0,4},{1,5},{2,6},{3,7},{4,0},{5,1},{6,2},{7,3},{8,12},{9,13},{10,... | collective-permute-start | bytes 393224 | tf_op jit(solution)/shard_map/ppermute | solution.py:307
  53.3 6.6 %collective-permute-start.18 = (bf16[2,2,64,256]{3,2,1,0:T(8,128)(2,1)S(1)}, bf16[2,2,64,256]{3,2,1,0:T(8,128)(2,1)S(1)}, u32[]{:S(2)}, u32[]{:S(2)}) collective-permute-start(bf16[2,2,64,256]{3,2,1,0:T(8,128)(2,1)S(1)} %get-tuple-element.54), channel_id=1, source_target_pairs={{0,6},{1,7},{2,4},{3,5},{4,2},{5,3},{6,0},{7,1},{8,14},{9,15},{10,... | collective-permute-start | bytes 393224 | tf_op jit(solution)/shard_map/ppermute | solution.py:307
  54.8 5.3 %collective-permute-start.15 = (bf16[4,2,64,256]{3,2,1,0:T(8,128)(2,1)S(1)}, bf16[4,2,64,256]{3,2,1,0:T(8,128)(2,1)S(1)}, u32[]{:S(2)}, u32[]{:S(2)}) collective-permute-start(bf16[4,2,64,256]{3,2,1,0:T(8,128)(2,1)S(1)} %pad_maximum_fusion), channel_id=1, source_target_pairs={{0,1},{1,0},{2,3},{3,2},{4,5},{5,4},{6,7},{7,6},{8,9},{9,8},{10,11... | collective-permute-start | bytes 786440 | tf_op jit(solution)/shard_map/ppermute | solution.py:307
  60.0 1.6 %collective-permute-start.19 = (bf16[4,2,64,256]{3,2,1,0:T(8,128)(2,1)S(1)}, bf16[4,2,64,256]{3,2,1,0:T(8,128)(2,1)S(1)}, u32[]{:S(2)}, u32[]{:S(2)}) collective-permute-start(bf16[4,2,64,256]{3,2,1,0:T(8,128)(2,1)S(1)} %pad_maximum_fusion.1), channel_id=1, source_target_pairs={{0,1},{1,0},{2,3},{3,2},{4,5},{5,4},{6,7},{7,6},{8,9},{9,8},{10,11... | collective-permute-start | bytes 786440 | tf_op jit(solution)/shard_map/ppermute | solution.py:307
  (5 other events, 13.4 us)

commit v3 on v2

v3 whole, which is shorter than its diff:
```python
import functools
import math

import jax
import jax.numpy as jnp
import ml_dtypes
import numpy as np
from jax import lax
from jax.experimental import pallas as pl
from jax.experimental.pallas import tpu as pltpu
from jax.sharding import PartitionSpec as P

NF = 1024
EDGE = 64
STEPS = 4
RECV_DEV = 64
CHUNK = 2
BASE = 64
FACTS = 8
ROWS = 16
LANES = 128
F32 = jnp.float32
BF16 = jnp.bfloat16
I32 = jnp.int32


def vmem():
    return pl.BlockSpec(memory_space=pltpu.VMEM)


def hbm():
    return pl.BlockSpec(memory_space=pltpu.HBM)


def in_hbm(array):
    return pltpu.with_memory_space_constraint(array, pltpu.HBM)


def smem():
    return pl.BlockSpec(memory_space=pltpu.SMEM)


def params(mib):
    return pltpu.CompilerParams(vmem_limit_bytes=mib << 20)


@functools.lru_cache(maxsize=None)
def make_tables(samples, bins, owners):
    scaling = 1.0 / math.sqrt(samples)
    half, period, each = samples // 2, samples // owners, bins // owners
    of_bins = np.arange(bins).reshape(each, owners).T
    ids = np.arange(half)[None, :, None] * of_bins[:, None, :] % samples
    phases = ids * (2.0 * math.pi / samples)
    forward = np.concatenate([np.cos(phases), -np.sin(phases)], 2) * scaling
    phases = np.outer(np.arange(each), np.arange(period)) % period * (2.0 * math.pi / period)
    real, imag = np.cos(phases) * scaling, np.sin(phases) * scaling
    inverse = np.concatenate(
        [np.concatenate([real, imag], 1), np.concatenate([-imag, real], 1)], 0
    )
    inverse = np.stack([inverse, 2.0 * inverse])
    inverse[0, 1:each] *= 2.0
    inverse[0, each + 1 :] *= 2.0
    phases = np.outer(np.arange(owners), np.arange(period)) * (2.0 * math.pi / samples)
    turns = np.stack([np.cos(phases), np.sin(phases)], 1).astype(np.float32)
    return forward.astype(ml_dtypes.bfloat16), inverse.astype(ml_dtypes.bfloat16), turns


def facts_message(facts, height, cols):
    index, slot, owner, weight = [ref[...].astype(F32)[None, :] for ref in facts]
    high = index.astype(I32) // BASE
    first = weight.astype(BF16).astype(F32)
    second = (weight - first).astype(BF16).astype(F32)
    lines = [high.astype(F32), index - (high * BASE).astype(F32), slot, owner]
    lines += [first, second, weight - first - second, jnp.zeros_like(weight)]
    block = jnp.concatenate(lines, 0)
    parts = [block[:, at : at + cols] for at in range(0, block.shape[1], cols)]
    parts += [jnp.zeros((height - FACTS * len(parts), cols), F32)] * (height > FACTS * len(parts))
    return jnp.concatenate(parts, 0).astype(BF16)


def fold(x_ref, sign):
    half = x_ref.shape[1] // 2
    return (x_ref[:, :half].astype(F32) + x_ref[:, half:].astype(F32) * sign).astype(BF16)


def first_kernel(chips, ids_ref, table_ref, x_ref, *refs):
    given, (out_ref, folded_ref, held, message_ref) = refs[:4], refs[4:8]
    ready, taken, sems = refs[8], refs[9:13], refs[13]
    rows = x_ref.shape[0]
    far = chips - 1
    copies = [
        pltpu.make_async_copy(x_ref, ready, sems.at[0]),
        pltpu.make_async_copy(table_ref.at[ids_ref[far]], held.at[0], sems.at[1]),
    ]
    copies += [
        pltpu.make_async_copy(source, target, sems.at[2 + i])
        for i, (source, target) in enumerate(zip(given, taken))
    ]
    for copy in copies:
        copy.start()
    copies[0].wait()
    folded = fold(ready, ids_ref[chips].astype(F32))
    folded_ref[...] = folded
    for copy in copies[1:]:
        copy.wait()
    spectra = jnp.dot(folded, held[0], preferred_element_type=F32)
    out_ref[:rows, :] = spectra.astype(BF16)
    message = facts_message(taken, *message_ref.shape)
    message_ref[...] = message
    out_ref[rows:, :] = message


def second_kernel(chips, ids_ref, table_ref, folded_ref, message_ref, *refs):
    outs, held, sems = refs[: chips - 1], refs[chips - 1], refs[chips]
    rows = folded_ref.shape[0]
    copies = [
        pltpu.make_async_copy(table_ref.at[ids_ref[d]], held.at[d], sems.at[d])
        for d in range(chips - 1)
    ]
    for copy in copies[::-1]:
        copy.start()
    for out_ref in outs:
        out_ref[rows:, :] = message_ref[...]
    for d in range(chips - 2, -1, -1):
        copies[d].wait()
        spectra = jnp.dot(folded_ref[...], held[d], preferred_element_type=F32)
        outs[d][:rows, :] = spectra.astype(BF16)


def near_of(ids, panel, table, facts):
    rows, samples = panel.shape
    owners, half, cols = table.shape
    chips = owners // 2
    height = 2 * FACTS * -(-rows // (2 * cols))
    block = jax.ShapeDtypeStruct((rows + height, cols), BF16)
    table = in_hbm(table)

    def cost(count):
        return pl.CostEstimate(
            flops=2 * rows * half * cols * count,
            bytes_accessed=2 * (half * cols * count + rows * samples),
            transcendentals=0,
        )

    last, folded, held_last, message = pl.pallas_call(
        functools.partial(first_kernel, chips),
        out_shape=[
            block,
            jax.ShapeDtypeStruct((rows, half), BF16),
            jax.ShapeDtypeStruct((1, half, cols), BF16),
            jax.ShapeDtypeStruct((height, cols), BF16),
        ],
        in_specs=[smem()] + [hbm()] * 6,
        out_specs=[vmem()] * 4,
        scratch_shapes=[pltpu.VMEM((rows, samples), BF16)]
        + [pltpu.VMEM(fact.shape, fact.dtype) for fact in facts]
        + [pltpu.SemaphoreType.DMA((6,))],
        cost_estimate=cost(1),
        compiler_params=params(24),
        name="first_panel_dft",
    )(ids, table, in_hbm(panel), *[in_hbm(fact) for fact in facts])
    *blocks, held = pl.pallas_call(
        functools.partial(second_kernel, chips),
        out_shape=[block] * (chips - 1) + [jax.ShapeDtypeStruct((chips - 1, half, cols), BF16)],
        in_specs=[smem(), hbm(), vmem(), vmem()],
        out_specs=[vmem()] * chips,
        scratch_shapes=[pltpu.SemaphoreType.DMA((chips - 1,))],
        cost_estimate=cost(chips - 1),
        compiler_params=params(24),
        name="near_panel_dft",
    )(ids, table, folded, message)
    return blocks + [last], [held, held_last]


def forward_kernel(chips, count, ids_ref, table_ref, last_ref, *refs):
    inputs, outs = refs[:count], refs[count:]
    for number, x_ref in enumerate(inputs):
        rows = x_ref.shape[0]
        folded = fold(x_ref, ids_ref[chips].astype(F32))
        for d in range(chips - 1, -1, -1):
            table = last_ref[0] if d == chips - 1 else table_ref[d]
            spectra = jnp.dot(folded, table, preferred_element_type=F32)
            outs[d][number * rows : (number + 1) * rows, :] = spectra.astype(BF16)


def forward_of(ids, arrays, tables, name):
    rows, samples = arrays[0].shape
    half, cols = tables[0].shape[1:]
    chips = tables[0].shape[0] + 1
    count = len(arrays)
    return pl.pallas_call(
        functools.partial(forward_kernel, chips, count),
        out_shape=[jax.ShapeDtypeStruct((count * rows, cols), BF16)] * chips,
        in_specs=[smem()] + [vmem()] * (count + 2),
        out_specs=[vmem()] * chips,
        cost_estimate=pl.CostEstimate(
            flops=2 * count * rows * half * cols * chips,
            bytes_accessed=2 * count * rows * samples * 2,
            transcendentals=0,
        ),
        compiler_params=params(24),
        name=name,
    )(ids, *tables, *arrays)


def masks_kernel(rows, ids_ref, *refs):
    facts, (gather_ref, summer_ref, weight_ref) = refs[:2], refs[2:]
    chips, height, cols = facts[0].shape
    chip, core = ids_ref[chips + 1], ids_ref[chips + 2]
    receivers = summer_ref.shape[0]
    extent = gather_ref.shape[1]
    square = (cols, cols)
    eye = (
        lax.broadcasted_iota(I32, square, 0) == lax.broadcasted_iota(I32, square, 1)
    ).astype(BF16)
    places = lax.broadcasted_iota(I32, (receivers, cols), 0)
    indices = lax.broadcasted_iota(I32, (cols, extent), 1)
    stacked = jnp.concatenate(
        [facts[across][distance] for distance in range(chips) for across in range(2)], 0
    )
    every = lax.dot_general(eye, stacked, (((1,), (1,)), ((), ())), preferred_element_type=F32)
    for distance in range(chips):
        for across in range(2):
            wide = facts[across][distance].astype(F32).astype(I32)
            where = 2 * distance + across
            turned = every[:, where * height : (where + 1) * height]
            for part in range(rows // cols):
                line = part * FACTS
                at = where * rows + part * cols
                slot, owner = wide[line + 2 : line + 3], wide[line + 3 : line + 4]
                place = (((owner >> 1) ^ chip) * 2 + ((owner & 1) ^ core)) * RECV_DEV + slot
                summer_ref[:, at : at + cols] = (places == place).astype(BF16)
                column = [turned[:, line + i : line + i + 1] for i in range(7)]
                index = (column[0] * BASE + column[1]).astype(I32)
                gather_ref[at : at + cols, :] = (indices == index).astype(BF16)
                weight = column[4] + column[5] + column[6]
                weight_ref[part * cols : (part + 1) * cols, where : where + 1] = weight


def masks_of(ids, facts, rows, extent):
    chips = facts[0].shape[0]
    traces = 2 * chips * rows
    receivers = 2 * chips * RECV_DEV
    return pl.pallas_call(
        functools.partial(masks_kernel, rows),
        out_shape=[
            jax.ShapeDtypeStruct((traces, extent), BF16),
            jax.ShapeDtypeStruct((receivers, traces), BF16),
            jax.ShapeDtypeStruct((rows, 2 * chips), F32),
        ],
        in_specs=[smem()] + [vmem()] * 2,
        out_specs=[vmem()] * 3,
        cost_estimate=pl.CostEstimate(
            flops=6 * traces * (extent + receivers),
            bytes_accessed=2 * traces * (extent + receivers),
            transcendentals=0,
        ),
        compiler_params=params(24),
        name="masks",
    )(ids, *facts)


def choose_kernel(rows, ids_ref, plan_ref, *refs):
    blocks, (main_ref, edges_ref, facts_ref) = refs[:-3], refs[-3:]
    chips = len(blocks) // 2
    for number in range(chips):
        facts_ref[number] = blocks[2 * number][rows:, :]
    for step in range(STEPS):
        planned = plan_ref[ids_ref[chips + 3], step]
        chosen = ((planned >> 1) ^ ids_ref[chips + 1]) * 2 + ((planned & 1) ^ ids_ref[chips + 2])
        for number, block in enumerate(blocks):

            @pl.when(chosen == number)
            def _():
                main_ref[step] = block[:rows, :]
                edges_ref[step] = block[rows - EDGE : rows, :]


def choose(ids, plan, blocks):
    rows, cols = blocks[1].shape
    height = blocks[0].shape[0] - rows
    return pl.pallas_call(
        functools.partial(choose_kernel, rows),
        out_shape=[
            jax.ShapeDtypeStruct((STEPS, rows, cols), BF16),
            jax.ShapeDtypeStruct((STEPS, EDGE, cols), BF16),
            jax.ShapeDtypeStruct((len(blocks) // 2, height, cols), BF16),
        ],
        in_specs=[smem(), smem()] + [vmem()] * len(blocks),
        out_specs=[vmem()] * 3,
        cost_estimate=pl.CostEstimate(
            flops=STEPS * rows * cols,
            bytes_accessed=2 * STEPS * rows * cols,
            transcendentals=0,
        ),
        compiler_params=params(24),
        name="choose_panels",
    )(ids, plan, *blocks)


def product_kernel(first, chips, *refs):
    main_ref, border_ref, gather_ref, summer_ref, weight_ref = refs[:5]
    spectra_refs, outs = refs[5 : 5 + chips], refs[5 + chips :]
    cols = main_ref.shape[2]
    half = cols // 2
    rows = weight_ref.shape[0]
    receivers = summer_ref.shape[0]
    extended = [
        jnp.concatenate([main_ref[first + step], border_ref[first + step]], 0)
        for step in range(CHUNK)
    ]
    totals = [jnp.zeros((receivers, cols), F32) for _ in range(CHUNK)]
    for block in range(2 * chips):
        at = block * rows
        mine = block % 2 * rows
        spectra = spectra_refs[block // 2][mine : mine + rows, :].astype(F32)
        spectra = spectra * weight_ref[:, block : block + 1]
        real_d, imag_d = spectra[:, :half], spectra[:, half:]
        for step in range(CHUNK):
            picked = jnp.dot(
                gather_ref[at : at + rows, :], extended[step], preferred_element_type=F32
            )
            real_p, imag_p = picked[:, :half], picked[:, half:]
            product = jnp.concatenate(
                [real_p * real_d - imag_p * imag_d, real_p * imag_d + imag_p * real_d], 1
            ).astype(BF16)
            totals[step] += jnp.dot(
                summer_ref[:, at : at + rows], product, preferred_element_type=F32
            )
    for step in range(CHUNK):
        result = totals[step].astype(BF16)
        for place in range(2 * chips):
            rows_of = result[place * RECV_DEV : (place + 1) * RECV_DEV]
            outs[place // 2][place % 2, step] = rows_of


def receivers_of(first, main, border, gather, summer, weight, spectra):
    chips = len(spectra)
    cols = main.shape[2]
    return pl.pallas_call(
        functools.partial(product_kernel, first, chips),
        out_shape=[jax.ShapeDtypeStruct((2, CHUNK, RECV_DEV, cols), BF16)] * chips,
        in_specs=[vmem()] * (5 + chips),
        out_specs=[vmem()] * chips,
        cost_estimate=pl.CostEstimate(
            flops=2 * CHUNK * cols * gather.shape[0] * (gather.shape[1] + summer.shape[0]),
            bytes_accessed=2 * (gather.size + summer.size + gather.shape[0] * cols),
            transcendentals=0,
        ),
        compiler_params=params(24),
        name="receiver_sums",
    )(main, border, gather, summer, weight, *spectra)


def weighted_sum(terms):
    by_size = {}
    for coefficient, term in terms:
        size = round(abs(coefficient), 12)
        if size == 0.0:
            continue
        before = by_size.get(size)
        if before is None:
            by_size[size] = (term, coefficient)
        elif (before[1] < 0) == (coefficient < 0):
            by_size[size] = (before[0] + term, before[1])
        else:
            by_size[size] = (before[0] - term, before[1])
    total = None
    for term, coefficient in by_size.values():
        if abs(abs(coefficient) - 1.0) > 1e-9:
            term = term * coefficient
        elif coefficient < 0:
            term = -term
        total = term if total is None else total + term
    return total


def inverse_kernel(chips, ids_ref, table_ref, turns_ref, *refs):
    out_ref, real_ref, imag_ref = refs[-3:]
    owners, _, period = turns_ref.shape
    cols = table_ref.shape[1]
    per_chunk = chips + 1
    groups = [refs[i * per_chunk : (i + 1) * per_chunk] for i in range(STEPS // CHUNK)]
    for distance in range(chips):
        for across in range(2):
            parts = []
            for group in groups:
                part = group[distance][0] if across == 0 else group[chips][distance]
                parts.append(part.reshape(CHUNK * RECV_DEV, cols))
            line = ids_ref[2 * distance + across]
            spread = jnp.dot(
                jnp.concatenate(parts, 0),
                table_ref[jnp.minimum(line, 1)],
                preferred_element_type=F32,
            )
            real, imag = spread[:, :period], spread[:, period:]
            turn = turns_ref[line]
            real_ref[line] = real * turn[0:1] - imag * turn[1:2]
            imag_ref[line] = real * turn[1:2] + imag * turn[0:1]

    angles = [[2.0 * math.pi * (r * q % owners) / owners for r in range(owners)] for q in range(owners)]

    @pl.loop(0, STEPS * RECV_DEV // ROWS)
    def _(chunk):
        at = pl.multiple_of(chunk * ROWS, ROWS)
        step = at // RECV_DEV
        row = pl.multiple_of(at % RECV_DEV, ROWS)
        for lane in range(0, period, LANES):
            lanes = slice(lane, min(lane + LANES, period))
            real = [real_ref[r, pl.ds(at, ROWS), lanes] for r in range(owners)]
            imag = [imag_ref[r, pl.ds(at, ROWS), lanes] for r in range(owners)]
            for q in range(owners // 2):
                sums = []
                for parity in range(2):
                    terms = []
                    for r in range(parity, owners, 2):
                        terms += [(math.cos(angles[q][r]), real[r])]
                        terms += [(-math.sin(angles[q][r]), imag[r])]
                    sums.append(weighted_sum(terms))
                for value, place in ((sums[0] + sums[1], q), (sums[0] - sums[1], q + owners // 2)):
                    start = place * period + lane
                    out_ref[step, pl.ds(row, ROWS), start : start + lanes.stop - lane] = (
                        value.astype(BF16)
                    )


def inverse_of(ids, groups, table, turns):
    owners, _, period = turns.shape
    arrays = [array for group in groups for array in group]
    rows = STEPS * RECV_DEV
    return pl.pallas_call(
        functools.partial(inverse_kernel, owners // 2),
        in_specs=[smem()] + [vmem()] * (2 + len(arrays)),
        out_specs=vmem(),
        out_shape=jax.ShapeDtypeStruct((STEPS, RECV_DEV, owners * period), BF16),
        scratch_shapes=[pltpu.VMEM((owners, rows, period), F32)] * 2,
        cost_estimate=pl.CostEstimate(
            flops=2 * rows * owners * table[0].size,
            bytes_accessed=2 * rows * owners * period,
            transcendentals=0,
        ),
        compiler_params=params(24),
        name="inverse_dft",
    )(ids, table, turns, *arrays)


def swap(array, distance):
    devices = range(lax.axis_size("line"))
    return lax.ppermute(array, "line", [(i, i ^ distance) for i in devices])


def send_blocks(blocks):
    chips = len(blocks)
    sent = {d: swap(blocks[d], 2 * d) for d in range(chips - 1, 0, -1)}
    return [blocks[0]] + [sent[d] for d in range(1, chips)]


def local(traces, owner, panel_index, receiver_slot, aperture_weight, panels, plan):
    owners = lax.axis_size("line")
    areas = lax.axis_size("area")
    chips = owners // 2
    samples = traces.shape[1]
    panel = panels[0, 0]
    forward, inverse, turns = make_tables(samples, NF, owners)
    forward = jnp.asarray(forward)
    inverse = jnp.asarray(inverse)
    turns = jnp.asarray(turns)

    line = lax.axis_index("line")
    chip, core = lax.shift_right_logical(line, 1), line & 1
    sign = 1 - 2 * core
    near = [(chip ^ d) * 2 + core for d in range(chips)]
    near_ids = jnp.stack(near + [sign, chip, core, lax.axis_index("area")]).astype(I32)
    all_ids = [(chip ^ (b // 2)) * 2 + (core ^ (b % 2)) for b in range(owners)]
    all_ids = jnp.stack(all_ids).astype(I32)

    panel_across = swap(panel, 1)
    traces_across = swap(traces, 1)
    facts = [panel_index, receiver_slot, owner.reshape(-1), aperture_weight]
    near_panels, tables = near_of(near_ids, panel, forward, facts)
    near_panels = send_blocks(near_panels)
    far_panels = forward_of(near_ids, [panel_across], tables, "far_panel_dft")
    far_panels = send_blocks(far_panels)
    spectra = forward_of(near_ids, [traces, traces_across], tables, "trace_dft")
    spectra = send_blocks(spectra)

    blocks = [block for pair in zip(near_panels, far_panels) for block in pair]
    main, edges, near_facts = choose(near_ids, plan, blocks)
    facts = [near_facts, swap(near_facts, 1)]
    border = lax.ppermute(edges, "area", [(i, i + 1) for i in range(areas - 1)])
    gather, summer, weight = masks_of(near_ids, facts, panel.shape[0], panel.shape[0] + EDGE)

    groups = []
    for first in range(0, STEPS, CHUNK):
        sums = receivers_of(first, main, border, gather, summer, weight, spectra)
        sums = send_blocks(sums)
        across = swap(jnp.stack([block[1] for block in sums]), 1)
        groups.append(sums + [across])
    return inverse_of(all_ids, groups, inverse, turns)


def solution(mesh):
    in_specs = (
        P(("area", "line"), None),
        P(("area", "line"), None),
        P(("area", "line")),
        P(("area", "line")),
        P(("area", "line")),
        P("area", "line", None, None),
        P(),
    )
    out_specs = P(None, ("area", "line"), None)
    return jax.shard_map(local, mesh=mesh, in_specs=in_specs, out_specs=out_specs, check_vma=False)
```

time: 68.3 us -> 55.5 us (0.81)
  blocking collectives: 9.53 us -> 0 us
  local copies, waits for them, and re-layouts: 8.03 us -> 0.24 us
  waiting for transfers between devices: 6.41 us -> 11.1 us
  Pallas kernels: 19.5 us -> 20.4 us
  other arithmetic: 0.79 us -> 0.07 us
    all_gather x1 -> x0, blocking collectives: 9.53 us -> none  [local(): facts = lax.all_gather(facts, 'line')]
    unnamed x18 -> x8, local copies, waits for them, and re-layouts: 7.81 us -> 0.02 us
    ppermute x19 -> x20, waiting for transfers between devices: 6.4 us -> 11.1 us  [swap(): return lax.ppermute(array, 'line', [(i, i ^ distance) for i in devices])]
    pallas_call x6 -> x7, Pallas kernels: 12.9 us -> 13.8 us  [the longest x2 3.07 us: forward_of(): pl.pallas_call(functools.partial(forward_kernel, chips, count), out_shape...]
    add x1 -> x0, other arithmetic: 0.7 us -> none  [local(): chosen = (plan_row // 2 ^ chip) * 2 + (plan_row % 2 ^ core)]
    ppermute x19 -> x20, starting transfers between devices: 19.4 us -> 19.6 us  [swap(): return lax.ppermute(array, 'line', [(i, i ^ distance) for i in devices])]
  transfers between devices with their start and end apart: 20 -> 21, of which waited for: 3 -> 7; matrix products, arithmetic and copies ran while one was open for 1% -> 1% of each run, Pallas kernels for 18% -> 26%
where the time goes in v3:
time: 55.5 us; the launch traced here: 55.4 us
  starting transfers between devices  23.3 us (42%)
  Pallas kernels  20.4 us (37%)
  waiting for transfers between devices  11.1 us (20%)
    ppermute x20, starting transfers between devices, swap(): return lax.ppermute(array, 'line', [(i, i ^ distance) for i in devices])  19.6 us
    ppermute x20, waiting for transfers between devices, swap(): return lax.ppermute(array, 'line', [(i, i ^ distance) for i in devices])  11.1 us
    pallas_call x2, Pallas kernels, receivers_of(): pl.pallas_call(functools.partial(product_kernel, first, chips), out_shape...  6.64 us
    ppermute x1, starting transfers between devices, local(): border = lax.ppermute(edges, 'area', [(i, i + 1) for i in range(areas - 1)])  3.67 us
    pallas_call x2, Pallas kernels, forward_of(): pl.pallas_call(functools.partial(forward_kernel, chips, count), out_shape...  3.07 us
    pallas_call x1, Pallas kernels, inverse_of(): pl.pallas_call(functools.partial(inverse_kernel, owners // 2), in_specs=[...  2.89 us
    pallas_call x1, Pallas kernels, near_of(): pl.pallas_call(functools.partial(second_kernel, chips), out_shape=[block]...  2.75 us
    pallas_call x1, Pallas kernels, near_of(): pl.pallas_call(functools.partial(first_kernel, chips), out_shape=[block,...  2.29 us
  transfers between devices with their start and end apart: 21, of which 7 were waited for; matrix products, arithmetic and copies ran while one was open for 1% of the time, Pallas kernels for 26%

profile of v3, /device:TPU:0, one launch (start us, length us, event | category | flops | bytes accessed | tf_op | source)
XLA Modules:
  0.0 55.4 jit_solution(1291408587097732347)
XLA Ops:
  0.6 2.3 %first_panel_dft.1 = (bf16[272,256]{1,0:T(8,128)(2,1)S(1)}, bf16[256,1024]{1,0:T(8,128)(2,1)S(1)}, bf16[1,1024,256]{2,1,0:T(8,128)(2,1)S(1)}, bf16[16,256]{1,0:T(8,128)(2,1)S(1)}) custom-call(s32[8]{0:T(128)S(1)} %stack.65.ids_ref, bf16[8,1024,256]{2,1,0:T(8,128)(2,1)} %constant.20.clone.table_ref, bf16[256,2048]{1,0:T(8,128)(2,1)} %bitcast.15, s32[256]{0:T(256)} %refs_0_.2, ...), custom_call_target="tpu_custom_call" | custom-call | flops 134217728 | bytes 1572864 | tf_op jit(solution)/shard_map/first_panel_dft/pallas_call | solution.py:145
  2.9 4.0 %collective-permute-start.5 = (bf16[272,256]{1,0:T(8,128)(2,1)S(1)}, bf16[272,256]{1,0:T(8,128)(2,1)S(1)}, u32[]{:S(2)}, u32[]{:S(2)}) collective-permute-start(bf16[272,256]{1,0:T(8,128)(2,1)S(1)} %get-tuple-element.45), channel_id=1, source_target_pairs={{0,6},{1,7},{2,4},{3,5},{4,2},{5,3},{6,0},{7,1},{8,14},{9,15},{10,... | collective-permute-start | bytes 417800 | tf_op jit(solution)/shard_map/ppermute | solution.py:449
  6.9 2.8 %near_panel_dft.1 = (bf16[272,256]{1,0:T(8,128)(2,1)S(1)}, bf16[272,256]{1,0:T(8,128)(2,1)S(1)}, bf16[272,256]{1,0:T(8,128)(2,1)S(1)}, bf16[3,1024,256]{2,1,0:T(8,128)(2,1)S(1)}) custom-call(s32[8]{0:T(128)S(1)} %stack.65.ids_ref, bf16[8,1024,256]{2,1,0:T(8,128)(2,1)} %constant.20.clone.table_ref, bf16[256,1024]{1,0:T(8,128)(2,1)S(1)} %get-tuple-element.35.folded_ref, ...), custom_call_target="tpu_custom_call" | custom-call | flops 402653184 | bytes 2621440 | tf_op jit(solution)/shard_map/near_panel_dft/pallas_call | solution.py:162
  10.3 1.3 %far_panel_dft.1 = (bf16[256,256]{1,0:T(8,128)(2,1)S(1)}, bf16[256,256]{1,0:T(8,128)(2,1)S(1)}, bf16[256,256]{1,0:T(8,128)(2,1)S(1)}, bf16[256,256]{1,0:T(8,128)(2,1)S(1)}) custom-call(s32[8]{0:T(128)S(1)} %stack.65.ids_ref, bf16[3,1024,256]{2,1,0:T(8,128)(2,1)S(1)} %get-tuple-element.38.table_ref, bf16[1,1024,256]{2,1,0:T(8,128)(2,1)S(1)} %get-tuple-element.39.last_ref, ...), custom_call_target="tpu_custom_call" | custom-call | flops 536870912 | bytes 2097152 | tf_op jit(solution)/shard_map/far_panel_dft/pallas_call | solution.py:191
  11.6 2.0 %collective-permute-start.2 = (bf16[256,256]{1,0:T(8,128)(2,1)S(1)}, bf16[256,256]{1,0:T(8,128)(2,1)S(1)}, u32[]{:S(2)}, u32[]{:S(2)}) collective-permute-start(bf16[256,256]{1,0:T(8,128)(2,1)S(1)} %get-tuple-element.42), channel_id=1, source_target_pairs={{0,2},{1,3},{2,0},{3,1},{4,6},{5,7},{6,4},{7,5},{8,10},{9,11},{10,... | collective-permute-start | bytes 393224 | tf_op jit(solution)/shard_map/ppermute | solution.py:449
  13.6 1.5 %collective-permute-start.4 = (bf16[256,256]{1,0:T(8,128)(2,1)S(1)}, bf16[256,256]{1,0:T(8,128)(2,1)S(1)}, u32[]{:S(2)}, u32[]{:S(2)}) collective-permute-start(bf16[256,256]{1,0:T(8,128)(2,1)S(1)} %get-tuple-element.44), channel_id=1, source_target_pairs={{0,4},{1,5},{2,6},{3,7},{4,0},{5,1},{6,2},{7,3},{8,12},{9,13},{10,... | collective-permute-start | bytes 393224 | tf_op jit(solution)/shard_map/ppermute | solution.py:449
  15.1 1.8 %trace_dft.1 = (bf16[512,256]{1,0:T(8,128)(2,1)S(1)}, bf16[512,256]{1,0:T(8,128)(2,1)S(1)}, bf16[512,256]{1,0:T(8,128)(2,1)S(1)}, bf16[512,256]{1,0:T(8,128)(2,1)S(1)}) custom-call(s32[8]{0:T(128)S(1)} %stack.65.ids_ref, bf16[3,1024,256]{2,1,0:T(8,128)(2,1)S(1)} %get-tuple-element.38.table_ref, bf16[1,1024,256]{2,1,0:T(8,128)(2,1)S(1)} %get-tuple-element.39.last_ref, ...), custom_call_target="tpu_custom_call" | custom-call | flops 1073741824 | bytes 4194304 | tf_op jit(solution)/shard_map/trace_dft/pallas_call | solution.py:191
  17.0 1.9 %collective-permute-start.10 = (bf16[512,256]{1,0:T(8,128)(2,1)S(1)}, bf16[512,256]{1,0:T(8,128)(2,1)S(1)}, u32[]{:S(2)}, u32[]{:S(2)}) collective-permute-start(bf16[512,256]{1,0:T(8,128)(2,1)S(1)} %get-tuple-element.54), channel_id=1, source_target_pairs={{0,2},{1,3},{2,0},{3,1},{4,6},{5,7},{6,4},{7,5},{8,10},{9,11},{10,... | collective-permute-start | bytes 786440 | tf_op jit(solution)/shard_map/ppermute | solution.py:449
  19.0 1.5 %collective-permute-start.11 = (bf16[512,256]{1,0:T(8,128)(2,1)S(1)}, bf16[512,256]{1,0:T(8,128)(2,1)S(1)}, u32[]{:S(2)}, u32[]{:S(2)}) collective-permute-start(bf16[512,256]{1,0:T(8,128)(2,1)S(1)} %get-tuple-element.55), channel_id=1, source_target_pairs={{0,4},{1,5},{2,6},{3,7},{4,0},{5,1},{6,2},{7,3},{8,12},{9,13},{10,... | collective-permute-start | bytes 786440 | tf_op jit(solution)/shard_map/ppermute | solution.py:449
  20.6 3.7 %collective-permute-done.6.refs_7_ = bf16[256,256]{1,0:T(8,128)(2,1)S(1)} collective-permute-done((bf16[256,256]{1,0:T(8,128)(2,1)S(1)}, bf16[256,256]{1,0:T(8,128)(2,1)S(1)}, u32[]{:S(2)}, u32[]{:S(2)}) %collective-permute-start.6) | collective-permute-done | bytes 131104 | tf_op jit(solution)/shard_map/ppermute | solution.py:449
  25.1 3.7 %collective-permute-start.7 = (bf16[4,64,256]{2,1,0:T(8,128)(2,1)S(1)}, bf16[4,64,256]{2,1,0:T(8,128)(2,1)S(1)}, u32[]{:S(2)}, u32[]{:S(2)}) collective-permute-start(bf16[4,64,256]{2,1,0:T(8,128)(2,1)S(1)} %get-tuple-element.48), channel_id=1, source_target_pairs={{0,8},{8,16},{16,24},{1,9},{9,17},{17,25},{2,10},{10,18},{18,26},{... | collective-permute-start | bytes 393224 | tf_op jit(solution)/shard_map/ppermute | solution.py:490
  28.9 1.2 %collective-permute-done.8.refs_1_ = bf16[4,16,256]{2,1,0:T(8,128)(2,1)S(1)} collective-permute-done((bf16[4,16,256]{2,1,0:T(8,128)(2,1)S(1)}, bf16[4,16,256]{2,1,0:T(8,128)(2,1)S(1)}, u32[]{:S(2)}, u32[]{:S(2)}) %collective-permute-start.8) | collective-permute-done | bytes 32800 | tf_op jit(solution)/shard_map/ppermute | solution.py:449
  30.1 2.0 %masks.1 = (bf16[2048,320]{1,0:T(8,128)(2,1)S(1)}, bf16[512,2048]{1,0:T(8,128)(2,1)S(1)}, f32[256,8]{1,0:T(8,128)S(1)}) custom-call(s32[8]{0:T(128)S(1)} %stack.65.ids_ref, bf16[4,16,256]{2,1,0:T(8,128)(2,1)S(1)} %get-tuple-element.49.refs_0_, bf16[4,16,256]{2,1,0:T(8,128)(2,1)S(1)} %collective-permute-done.8.refs_1_), custom_call_target="tpu_custom_call" | custom-call | flops 10223616 | bytes 3407872 | tf_op jit(solution)/shard_map/masks/pallas_call | solution.py:244
  32.1 1.0 %collective-permute-done.12.refs_8_ = bf16[512,256]{1,0:T(8,128)(2,1)S(1)} collective-permute-done((bf16[512,256]{1,0:T(8,128)(2,1)S(1)}, bf16[512,256]{1,0:T(8,128)(2,1)S(1)}, u32[]{:S(2)}, u32[]{:S(2)}) %collective-permute-start.12) | collective-permute-done | bytes 262176 | tf_op jit(solution)/shard_map/ppermute | solution.py:449
  33.1 3.3 %receiver_sums.2 = (bf16[2,2,64,256]{3,2,1,0:T(8,128)(2,1)S(1)}, bf16[2,2,64,256]{3,2,1,0:T(8,128)(2,1)S(1)}, bf16[2,2,64,256]{3,2,1,0:T(8,128)(2,1)S(1)}, bf16[2,2,64,256]{3,2,1,0:T(8,128)(2,1)S(1)}) custom-call(bf16[4,256,256]{2,1,0:T(8,128)(2,1)S(1)} %get-tuple-element.47.refs_0_, bf16[4,64,256]{2,1,0:T(8,128)(2,1)S(1)} %collective-permute-done.7.refs_1_, ...), custom_call_target="tpu_custom_call" | custom-call | flops 1744830464 | bytes 4456448 | tf_op jit(solution)/shard_map/receiver_sums/pallas_call | solution.py:340
  37.1 1.0 %collective-permute-start.14 = (bf16[2,2,64,256]{3,2,1,0:T(8,128)(2,1)S(1)}, bf16[2,2,64,256]{3,2,1,0:T(8,128)(2,1)S(1)}, u32[]{:S(2)}, u32[]{:S(2)}) collective-permute-start(bf16[2,2,64,256]{3,2,1,0:T(8,128)(2,1)S(1)} %get-tuple-element.59), channel_id=1, source_target_pairs={{0,4},{1,5},{2,6},{3,7},{4,0},{5,1},{6,2},{7,3},{8,12},{9,13},{10,... | collective-permute-start | bytes 393224 | tf_op jit(solution)/shard_map/ppermute | solution.py:449
  38.0 2.0 %collective-permute-start.15 = (bf16[2,2,64,256]{3,2,1,0:T(8,128)(2,1)S(1)}, bf16[2,2,64,256]{3,2,1,0:T(8,128)(2,1)S(1)}, u32[]{:S(2)}, u32[]{:S(2)}) collective-permute-start(bf16[2,2,64,256]{3,2,1,0:T(8,128)(2,1)S(1)} %get-tuple-element.60), channel_id=1, source_target_pairs={{0,6},{1,7},{2,4},{3,5},{4,2},{5,3},{6,0},{7,1},{8,14},{9,15},{10,... | collective-permute-start | bytes 393224 | tf_op jit(solution)/shard_map/ppermute | solution.py:449
  40.0 3.3 %receiver_sums.3 = (bf16[2,2,64,256]{3,2,1,0:T(8,128)(2,1)S(1)}, bf16[2,2,64,256]{3,2,1,0:T(8,128)(2,1)S(1)}, bf16[2,2,64,256]{3,2,1,0:T(8,128)(2,1)S(1)}, bf16[2,2,64,256]{3,2,1,0:T(8,128)(2,1)S(1)}) custom-call(bf16[4,256,256]{2,1,0:T(8,128)(2,1)S(1)} %get-tuple-element.47.refs_0_, bf16[4,64,256]{2,1,0:T(8,128)(2,1)S(1)} %collective-permute-done.7.refs_1_, ...), custom_call_target="tpu_custom_call" | custom-call | flops 1744830464 | bytes 4456448 | tf_op jit(solution)/shard_map/receiver_sums/pallas_call | solution.py:340
  44.0 1.0 %collective-permute-start.18 = (bf16[2,2,64,256]{3,2,1,0:T(8,128)(2,1)S(1)}, bf16[2,2,64,256]{3,2,1,0:T(8,128)(2,1)S(1)}, u32[]{:S(2)}, u32[]{:S(2)}) collective-permute-start(bf16[2,2,64,256]{3,2,1,0:T(8,128)(2,1)S(1)} %get-tuple-element.63), channel_id=1, source_target_pairs={{0,4},{1,5},{2,6},{3,7},{4,0},{5,1},{6,2},{7,3},{8,12},{9,13},{10,... | collective-permute-start | bytes 393224 | tf_op jit(solution)/shard_map/ppermute | solution.py:449
  45.0 2.0 %collective-permute-start.19 = (bf16[2,2,64,256]{3,2,1,0:T(8,128)(2,1)S(1)}, bf16[2,2,64,256]{3,2,1,0:T(8,128)(2,1)S(1)}, u32[]{:S(2)}, u32[]{:S(2)}) collective-permute-start(bf16[2,2,64,256]{3,2,1,0:T(8,128)(2,1)S(1)} %get-tuple-element.64), channel_id=1, source_target_pairs={{0,6},{1,7},{2,4},{3,5},{4,2},{5,3},{6,0},{7,1},{8,14},{9,15},{10,... | collective-permute-start | bytes 393224 | tf_op jit(solution)/shard_map/ppermute | solution.py:449
  47.1 1.5 %collective-permute-done.17.refs_6_ = bf16[2,2,64,256]{3,2,1,0:T(8,128)(2,1)S(1)} collective-permute-done((bf16[2,2,64,256]{3,2,1,0:T(8,128)(2,1)S(1)}, bf16[2,2,64,256]{3,2,1,0:T(8,128)(2,1)S(1)}, u32[]{:S(2)}, u32[]{:S(2)}) %collective-permute-start.17) | collective-permute-done | bytes 131104 | tf_op jit(solution)/shard_map/ppermute | solution.py:449
  48.9 1.9 %collective-permute-done.19.refs_8_ = bf16[2,2,64,256]{3,2,1,0:T(8,128)(2,1)S(1)} collective-permute-done((bf16[2,2,64,256]{3,2,1,0:T(8,128)(2,1)S(1)}, bf16[2,2,64,256]{3,2,1,0:T(8,128)(2,1)S(1)}, u32[]{:S(2)}, u32[]{:S(2)}) %collective-permute-start.19) | collective-permute-done | bytes 131104 | tf_op jit(solution)/shard_map/ppermute | solution.py:449
  51.1 1.4 %collective-permute-done.20.refs_9_ = bf16[4,2,64,256]{3,2,1,0:T(8,128)(2,1)S(1)} collective-permute-done((bf16[4,2,64,256]{3,2,1,0:T(8,128)(2,1)S(1)}, bf16[4,2,64,256]{3,2,1,0:T(8,128)(2,1)S(1)}, u32[]{:S(2)}, u32[]{:S(2)}) %collective-permute-start.20) | collective-permute-done | bytes 262176 | tf_op jit(solution)/shard_map/ppermute | solution.py:449
  52.5 2.9 %inverse_dft.1 = bf16[4,64,2048]{2,1,0:T(8,128)(2,1)} custom-call(s32[8]{0:T(128)S(1)} %stack.60.ids_ref, bf16[2,256,512]{2,1,0:T(8,128)(2,1)S(1)} %copy-done.1, f32[8,2,256]{2,1,0:T(2,128)S(1)} %copy-done.2, bf16[2,2,64,256]{3,2,1,0:T(8,128)(2,1)S(1)} %get-tuple-element.57.refs_0_, bf16[2,2,64,256]{3,2,1,0:T(8,128)(2,1)S(1)} %collective-permute-done.13.refs_1_, ...), custom_call_target="tpu_custom_call" | custom-call | flops 536870912 | bytes 1048576 | tf_op jit(solution)/shard_map/inverse_dft/pallas_call | solution.py:431
  (47 shorter events, 4.3 us)
Async XLA Ops:
  0.0 10.3 %collective-permute-start = (bf16[256,2048]{1,0:T(8,128)(2,1)}, bf16[256,2048]{1,0:T(8,128)(2,1)S(1)}, u32[]{:S(2)}, u32[]{:S(2)}) collective-permute-start(bf16[256,2048]{1,0:T(8,128)(2,1)} %bitcast.14), channel_id=1, source_target_pairs={{0,1},{1,0},{2,3},{3,2},{4,5},{5,4},{6,7},{7,6},{8,9},{9,8},{10,11... | collective-permute-start | bytes 3145736 | tf_op jit(solution)/shard_map/ppermute | solution.py:449
  0.5 13.1 %collective-permute-start.9 = (bf16[256,2048]{1,0:T(8,128)(2,1)}, bf16[256,2048]{1,0:T(8,128)(2,1)S(1)}, u32[]{:S(2)}, u32[]{:S(2)}) collective-permute-start(bf16[256,2048]{1,0:T(8,128)(2,1)} %refs_0_.3), channel_id=1, source_target_pairs={{0,1},{1,0},{2,3},{3,2},{4,5},{5,4},{6,7},{7,6},{8,9},{9,8},{10,11... | collective-permute-start | bytes 3145736 | tf_op jit(solution)/shard_map/ppermute | solution.py:449
  2.9 14.0 %collective-permute-start.5 = (bf16[272,256]{1,0:T(8,128)(2,1)S(1)}, bf16[272,256]{1,0:T(8,128)(2,1)S(1)}, u32[]{:S(2)}, u32[]{:S(2)}) collective-permute-start(bf16[272,256]{1,0:T(8,128)(2,1)S(1)} %get-tuple-element.45), channel_id=1, source_target_pairs={{0,6},{1,7},{2,4},{3,5},{4,2},{5,3},{6,0},{7,1},{8,14},{9,15},{10,... | collective-permute-start | bytes 417800 | tf_op jit(solution)/shard_map/ppermute | solution.py:449
  9.6 7.4 %collective-permute-start.1 = (bf16[272,256]{1,0:T(8,128)(2,1)S(1)}, bf16[272,256]{1,0:T(8,128)(2,1)S(1)}, u32[]{:S(2)}, u32[]{:S(2)}) collective-permute-start(bf16[272,256]{1,0:T(8,128)(2,1)S(1)} %get-tuple-element.41), channel_id=1, source_target_pairs={{0,2},{1,3},{2,0},{3,1},{4,6},{5,7},{6,4},{7,5},{8,10},{9,11},{10,... | collective-permute-start | bytes 417800 | tf_op jit(solution)/shard_map/ppermute | solution.py:449
  10.2 8.7 %collective-permute-start.3 = (bf16[272,256]{1,0:T(8,128)(2,1)S(1)}, bf16[272,256]{1,0:T(8,128)(2,1)S(1)}, u32[]{:S(2)}, u32[]{:S(2)}) collective-permute-start(bf16[272,256]{1,0:T(8,128)(2,1)S(1)} %get-tuple-element.43), channel_id=1, source_target_pairs={{0,4},{1,5},{2,6},{3,7},{4,0},{5,1},{6,2},{7,3},{8,12},{9,13},{10,... | collective-permute-start | bytes 417800 | tf_op jit(solution)/shard_map/ppermute | solution.py:449
  11.6 8.9 %collective-permute-start.2 = (bf16[256,256]{1,0:T(8,128)(2,1)S(1)}, bf16[256,256]{1,0:T(8,128)(2,1)S(1)}, u32[]{:S(2)}, u32[]{:S(2)}) collective-permute-start(bf16[256,256]{1,0:T(8,128)(2,1)S(1)} %get-tuple-element.42), channel_id=1, source_target_pairs={{0,2},{1,3},{2,0},{3,1},{4,6},{5,7},{6,4},{7,5},{8,10},{9,11},{10,... | collective-permute-start | bytes 393224 | tf_op jit(solution)/shard_map/ppermute | solution.py:449
  13.6 10.8 %copy-start.3 = (s32[4,4]{1,0:T(4,128)S(1)}, s32[4,4]{1,0:T(4,128)}, u32[]{:S(2)}) copy-start(s32[4,4]{1,0:T(4,128)} %plan_ref.1) | copy-start | bytes 196
  13.6 7.0 %collective-permute-start.4 = (bf16[256,256]{1,0:T(8,128)(2,1)S(1)}, bf16[256,256]{1,0:T(8,128)(2,1)S(1)}, u32[]{:S(2)}, u32[]{:S(2)}) collective-permute-start(bf16[256,256]{1,0:T(8,128)(2,1)S(1)} %get-tuple-element.44), channel_id=1, source_target_pairs={{0,4},{1,5},{2,6},{3,7},{4,0},{5,1},{6,2},{7,3},{8,12},{9,13},{10,... | collective-permute-start | bytes 393224 | tf_op jit(solution)/shard_map/ppermute | solution.py:449
  16.9 7.4 %collective-permute-start.6 = (bf16[256,256]{1,0:T(8,128)(2,1)S(1)}, bf16[256,256]{1,0:T(8,128)(2,1)S(1)}, u32[]{:S(2)}, u32[]{:S(2)}) collective-permute-start(bf16[256,256]{1,0:T(8,128)(2,1)S(1)} %get-tuple-element.46), channel_id=1, source_target_pairs={{0,6},{1,7},{2,4},{3,5},{4,2},{5,3},{6,0},{7,1},{8,14},{9,15},{10,... | collective-permute-start | bytes 393224 | tf_op jit(solution)/shard_map/ppermute | solution.py:449
  17.0 15.0 %collective-permute-start.10 = (bf16[512,256]{1,0:T(8,128)(2,1)S(1)}, bf16[512,256]{1,0:T(8,128)(2,1)S(1)}, u32[]{:S(2)}, u32[]{:S(2)}) collective-permute-start(bf16[512,256]{1,0:T(8,128)(2,1)S(1)} %get-tuple-element.54), channel_id=1, source_target_pairs={{0,2},{1,3},{2,0},{3,1},{4,6},{5,7},{6,4},{7,5},{8,10},{9,11},{10,... | collective-permute-start | bytes 786440 | tf_op jit(solution)/shard_map/ppermute | solution.py:449
  19.0 13.1 %collective-permute-start.11 = (bf16[512,256]{1,0:T(8,128)(2,1)S(1)}, bf16[512,256]{1,0:T(8,128)(2,1)S(1)}, u32[]{:S(2)}, u32[]{:S(2)}) collective-permute-start(bf16[512,256]{1,0:T(8,128)(2,1)S(1)} %get-tuple-element.55), channel_id=1, source_target_pairs={{0,4},{1,5},{2,6},{3,7},{4,0},{5,1},{6,2},{7,3},{8,12},{9,13},{10,... | collective-permute-start | bytes 786440 | tf_op jit(solution)/shard_map/ppermute | solution.py:449
  20.5 12.6 %collective-permute-start.12 = (bf16[512,256]{1,0:T(8,128)(2,1)S(1)}, bf16[512,256]{1,0:T(8,128)(2,1)S(1)}, u32[]{:S(2)}, u32[]{:S(2)}) collective-permute-start(bf16[512,256]{1,0:T(8,128)(2,1)S(1)} %get-tuple-element.56), channel_id=1, source_target_pairs={{0,6},{1,7},{2,4},{3,5},{4,2},{5,3},{6,0},{7,1},{8,14},{9,15},{10,... | collective-permute-start | bytes 786440 | tf_op jit(solution)/shard_map/ppermute | solution.py:449
  25.1 6.9 %collective-permute-start.7 = (bf16[4,64,256]{2,1,0:T(8,128)(2,1)S(1)}, bf16[4,64,256]{2,1,0:T(8,128)(2,1)S(1)}, u32[]{:S(2)}, u32[]{:S(2)}) collective-permute-start(bf16[4,64,256]{2,1,0:T(8,128)(2,1)S(1)} %get-tuple-element.48), channel_id=1, source_target_pairs={{0,8},{8,16},{16,24},{1,9},{9,17},{17,25},{2,10},{10,18},{18,26},{... | collective-permute-start | bytes 393224 | tf_op jit(solution)/shard_map/ppermute | solution.py:490
  28.8 1.3 %collective-permute-start.8 = (bf16[4,16,256]{2,1,0:T(8,128)(2,1)S(1)}, bf16[4,16,256]{2,1,0:T(8,128)(2,1)S(1)}, u32[]{:S(2)}, u32[]{:S(2)}) collective-permute-start(bf16[4,16,256]{2,1,0:T(8,128)(2,1)S(1)} %get-tuple-element.49.refs_0_), channel_id=1, source_target_pairs={{0,1},{1,0},{2,3},{3,2},{4,5},{5,4},{6,7},{7,6},{8,9},{9,8},{10,11... | collective-permute-start | bytes 98312 | tf_op jit(solution)/shard_map/ppermute | solution.py:449
  36.5 8.5 %collective-permute-start.13 = (bf16[2,2,64,256]{3,2,1,0:T(8,128)(2,1)S(1)}, bf16[2,2,64,256]{3,2,1,0:T(8,128)(2,1)S(1)}, u32[]{:S(2)}, u32[]{:S(2)}) collective-permute-start(bf16[2,2,64,256]{3,2,1,0:T(8,128)(2,1)S(1)} %get-tuple-element.58), channel_id=1, source_target_pairs={{0,2},{1,3},{2,0},{3,1},{4,6},{5,7},{6,4},{7,5},{8,10},{9,11},{10,... | collective-permute-start | bytes 393224 | tf_op jit(solution)/shard_map/ppermute | solution.py:449
  37.1 9.9 %collective-permute-start.14 = (bf16[2,2,64,256]{3,2,1,0:T(8,128)(2,1)S(1)}, bf16[2,2,64,256]{3,2,1,0:T(8,128)(2,1)S(1)}, u32[]{:S(2)}, u32[]{:S(2)}) collective-permute-start(bf16[2,2,64,256]{3,2,1,0:T(8,128)(2,1)S(1)} %get-tuple-element.59), channel_id=1, source_target_pairs={{0,4},{1,5},{2,6},{3,7},{4,0},{5,1},{6,2},{7,3},{8,12},{9,13},{10,... | collective-permute-start | bytes 393224 | tf_op jit(solution)/shard_map/ppermute | solution.py:449
  38.0 8.9 %collective-permute-start.15 = (bf16[2,2,64,256]{3,2,1,0:T(8,128)(2,1)S(1)}, bf16[2,2,64,256]{3,2,1,0:T(8,128)(2,1)S(1)}, u32[]{:S(2)}, u32[]{:S(2)}) collective-permute-start(bf16[2,2,64,256]{3,2,1,0:T(8,128)(2,1)S(1)} %get-tuple-element.60), channel_id=1, source_target_pairs={{0,6},{1,7},{2,4},{3,5},{4,2},{5,3},{6,0},{7,1},{8,14},{9,15},{10,... | collective-permute-start | bytes 393224 | tf_op jit(solution)/shard_map/ppermute | solution.py:449
  43.3 9.1 %copy-start.1 = (bf16[2,256,512]{2,1,0:T(8,128)(2,1)S(1)}, bf16[2,256,512]{2,1,0:T(8,128)(2,1)}, u32[]{:S(2)}) copy-start(bf16[2,256,512]{2,1,0:T(8,128)(2,1)} %constant.21.clone.table_ref) | copy-start | bytes 1572868
  43.4 9.1 %copy-start.2 = (f32[8,2,256]{2,1,0:T(2,128)S(1)}, f32[8,2,256]{2,1,0:T(2,128)}, u32[]{:S(2)}) copy-start(f32[8,2,256]{2,1,0:T(2,128)} %constant.22.clone.turns_ref) | copy-start | bytes 49156
  43.4 5.2 %collective-permute-start.17 = (bf16[2,2,64,256]{3,2,1,0:T(8,128)(2,1)S(1)}, bf16[2,2,64,256]{3,2,1,0:T(8,128)(2,1)S(1)}, u32[]{:S(2)}, u32[]{:S(2)}) collective-permute-start(bf16[2,2,64,256]{3,2,1,0:T(8,128)(2,1)S(1)} %get-tuple-element.62), channel_id=1, source_target_pairs={{0,2},{1,3},{2,0},{3,1},{4,6},{5,7},{6,4},{7,5},{8,10},{9,11},{10,... | collective-permute-start | bytes 393224 | tf_op jit(solution)/shard_map/ppermute | solution.py:449
  44.0 5.0 %collective-permute-start.18 = (bf16[2,2,64,256]{3,2,1,0:T(8,128)(2,1)S(1)}, bf16[2,2,64,256]{3,2,1,0:T(8,128)(2,1)S(1)}, u32[]{:S(2)}, u32[]{:S(2)}) collective-permute-start(bf16[2,2,64,256]{3,2,1,0:T(8,128)(2,1)S(1)} %get-tuple-element.63), channel_id=1, source_target_pairs={{0,4},{1,5},{2,6},{3,7},{4,0},{5,1},{6,2},{7,3},{8,12},{9,13},{10,... | collective-permute-start | bytes 393224 | tf_op jit(solution)/shard_map/ppermute | solution.py:449
  45.0 5.9 %collective-permute-start.19 = (bf16[2,2,64,256]{3,2,1,0:T(8,128)(2,1)S(1)}, bf16[2,2,64,256]{3,2,1,0:T(8,128)(2,1)S(1)}, u32[]{:S(2)}, u32[]{:S(2)}) collective-permute-start(bf16[2,2,64,256]{3,2,1,0:T(8,128)(2,1)S(1)} %get-tuple-element.64), channel_id=1, source_target_pairs={{0,6},{1,7},{2,4},{3,5},{4,2},{5,3},{6,0},{7,1},{8,14},{9,15},{10,... | collective-permute-start | bytes 393224 | tf_op jit(solution)/shard_map/ppermute | solution.py:449
  47.0 4.0 %collective-permute-start.16 = (bf16[4,2,64,256]{3,2,1,0:T(8,128)(2,1)S(1)}, bf16[4,2,64,256]{3,2,1,0:T(8,128)(2,1)S(1)}, u32[]{:S(2)}, u32[]{:S(2)}) collective-permute-start(bf16[4,2,64,256]{3,2,1,0:T(8,128)(2,1)S(1)} %pad_maximum_fusion), channel_id=1, source_target_pairs={{0,1},{1,0},{2,3},{3,2},{4,5},{5,4},{6,7},{7,6},{8,9},{9,8},{10,11... | collective-permute-start | bytes 786440 | tf_op jit(solution)/shard_map/ppermute | solution.py:449
  50.9 1.6 %collective-permute-start.20 = (bf16[4,2,64,256]{3,2,1,0:T(8,128)(2,1)S(1)}, bf16[4,2,64,256]{3,2,1,0:T(8,128)(2,1)S(1)}, u32[]{:S(2)}, u32[]{:S(2)}) collective-permute-start(bf16[4,2,64,256]{3,2,1,0:T(8,128)(2,1)S(1)} %pad_maximum_fusion.1), channel_id=1, source_target_pairs={{0,1},{1,0},{2,3},{3,2},{4,5},{5,4},{6,7},{7,6},{8,9},{9,8},{10,11... | collective-permute-start | bytes 786440 | tf_op jit(solution)/shard_map/ppermute | solution.py:449
  (1 other events, 5.5 us)

commit v4 on v3

--- a/solution.py
+++ b/solution.py
@@ -48,21 +48,23 @@
 def make_tables(samples, bins, owners):
     scaling = 1.0 / math.sqrt(samples)
     half, period, each = samples // 2, samples // owners, bins // owners
-    of_bins = np.arange(bins).reshape(each, owners).T
-    ids = np.arange(half)[None, :, None] * of_bins[:, None, :] % samples
-    phases = ids * (2.0 * math.pi / samples)
-    forward = np.concatenate([np.cos(phases), -np.sin(phases)], 2) * scaling
+    ids = np.arange(half).reshape(1, half // period, period)
+    ids = ids * np.arange(owners)[:, None, None] % samples
+    forward_turns = ids * (2.0 * math.pi / samples)
+    forward_turns = np.concatenate([np.cos(forward_turns), -np.sin(forward_turns)], 1)
     phases = np.outer(np.arange(each), np.arange(period)) % period * (2.0 * math.pi / period)
     real, imag = np.cos(phases) * scaling, np.sin(phases) * scaling
     inverse = np.concatenate(
         [np.concatenate([real, imag], 1), np.concatenate([-imag, real], 1)], 0
     )
+    forward = inverse.T
     inverse = np.stack([inverse, 2.0 * inverse])
     inverse[0, 1:each] *= 2.0
     inverse[0, each + 1 :] *= 2.0
     phases = np.outer(np.arange(owners), np.arange(period)) * (2.0 * math.pi / samples)
     turns = np.stack([np.cos(phases), np.sin(phases)], 1).astype(np.float32)
-    return forward.astype(ml_dtypes.bfloat16), inverse.astype(ml_dtypes.bfloat16), turns
+    forward = np.ascontiguousarray(forward).astype(ml_dtypes.bfloat16)
+    return forward, forward_turns.astype(np.float32), inverse.astype(ml_dtypes.bfloat16), turns
 
 
 def facts_message(facts, height, cols):
@@ -78,129 +80,124 @@
     return jnp.concatenate(parts, 0).astype(BF16)
 
 
-def fold(x_ref, sign):
-    half = x_ref.shape[1] // 2
-    return (x_ref[:, :half].astype(F32) + x_ref[:, half:].astype(F32) * sign).astype(BF16)
-
-
-def first_kernel(chips, ids_ref, table_ref, x_ref, *refs):
-    given, (out_ref, folded_ref, held, message_ref) = refs[:4], refs[4:8]
-    ready, taken, sems = refs[8], refs[9:13], refs[13]
+def spread_turns(chips, ids_ref, turns_ref, wide_ref):
+    for d in range(chips):
+        turn = turns_ref[ids_ref[d]]
+        for number in range(turn.shape[0]):
+            wide_ref[d, number] = jnp.broadcast_to(turn[number : number + 1], wide_ref.shape[2:])
+
+
+def turn_rows(ids_ref, x_ref, base, count, wide_ref, y_ref, at):
+    chips, owners, _, period = wide_ref.shape
+    half = owners // 2
+    sign = ids_ref[chips].astype(F32)
+
+    @pl.loop(0, count // ROWS)
+    def _(chunk):
+        row = pl.multiple_of(base + chunk * ROWS, ROWS)
+        to = pl.multiple_of(at + chunk * ROWS, ROWS)
+        for lane in range(0, period, LANES):
+            stop = min(lane + LANES, period)
+            folded = []
+            for q in range(half):
+                low = x_ref[pl.ds(row, ROWS), q * period + lane : q * period + stop]
+                start = (q + half) * period
+                high = x_ref[pl.ds(row, ROWS), start + lane : start + stop]
+                folded.append(low.astype(F32) + high.astype(F32) * sign)
+            for d in range(chips):
+                for part in range(2):
+                    total = folded[0] * wide_ref[d, part * half, :, lane:stop]
+                    for q in range(1, half):
+                        total += folded[q] * wide_ref[d, part * half + q, :, lane:stop]
+                    start = part * period
+                    y_ref[d, pl.ds(to, ROWS), start + lane : start + stop] = total.astype(BF16)
+
+
+def first_kernel(chips, ids_ref, table_ref, turns_ref, x_ref, *refs):
+    given, outs, (table, wide), refs = refs[:4], refs[4:][:chips], refs[4 + chips :][:2], refs[6 + chips :]
+    turns, ready, taken, (y_ref, sems) = refs[0], refs[1], refs[2:6], refs[6:]
     rows = x_ref.shape[0]
-    far = chips - 1
+    part = rows // 2
+    pairs = [(turns_ref, turns)]
+    pairs += [(x_ref.at[pl.ds(at, part)], ready.at[pl.ds(at, part)]) for at in (0, part)]
+    pairs += [(table_ref, table), *zip(given, taken)]
     copies = [
-        pltpu.make_async_copy(x_ref, ready, sems.at[0]),
-        pltpu.make_async_copy(table_ref.at[ids_ref[far]], held.at[0], sems.at[1]),
-    ]
-    copies += [
-        pltpu.make_async_copy(source, target, sems.at[2 + i])
-        for i, (source, target) in enumerate(zip(given, taken))
+        pltpu.make_async_copy(source, target, sems.at[i]) for i, (source, target) in enumerate(pairs)
     ]
     for copy in copies:
         copy.start()
     copies[0].wait()
-    folded = fold(ready, ids_ref[chips].astype(F32))
-    folded_ref[...] = folded
-    for copy in copies[1:]:
+    spread_turns(chips, ids_ref, turns, wide)
+    for number in range(2):
+        copies[1 + number].wait()
+        turn_rows(ids_ref, ready, number * part, part, wide, y_ref, number * part)
+    for copy in copies[3:]:
         copy.wait()
-    spectra = jnp.dot(folded, held[0], preferred_element_type=F32)
-    out_ref[:rows, :] = spectra.astype(BF16)
-    message = facts_message(taken, *message_ref.shape)
-    message_ref[...] = message
-    out_ref[rows:, :] = message
-
-
-def second_kernel(chips, ids_ref, table_ref, folded_ref, message_ref, *refs):
-    outs, held, sems = refs[: chips - 1], refs[chips - 1], refs[chips]
-    rows = folded_ref.shape[0]
-    copies = [
-        pltpu.make_async_copy(table_ref.at[ids_ref[d]], held.at[d], sems.at[d])
-        for d in range(chips - 1)
-    ]
-    for copy in copies[::-1]:
-        copy.start()
-    for out_ref in outs:
-        out_ref[rows:, :] = message_ref[...]
-    for d in range(chips - 2, -1, -1):
-        copies[d].wait()
-        spectra = jnp.dot(folded_ref[...], held[d], preferred_element_type=F32)
+    message = facts_message(taken, outs[0].shape[0] - rows, outs[0].shape[1])
+    for d in range(chips - 1, -1, -1):
+        spectra = jnp.dot(y_ref[d], table[...], preferred_element_type=F32)
         outs[d][:rows, :] = spectra.astype(BF16)
-
-
-def near_of(ids, panel, table, facts):
+        outs[d][rows:, :] = message
+
+
+def cost_of(rows, table, turns):
+    return pl.CostEstimate(
+        flops=rows * turns.shape[0] * table.size,
+        bytes_accessed=4 * rows * table.size // 64,
+        transcendentals=0,
+    )
+
+
+def near_of(ids, panel, table, turns, facts):
     rows, samples = panel.shape
-    owners, half, cols = table.shape
-    chips = owners // 2
+    cols = table.shape[1]
+    chips = turns.shape[0] // 2
+    owners, _, period = turns.shape
     height = 2 * FACTS * -(-rows // (2 * cols))
-    block = jax.ShapeDtypeStruct((rows + height, cols), BF16)
-    table = in_hbm(table)
-
-    def cost(count):
-        return pl.CostEstimate(
-            flops=2 * rows * half * cols * count,
-            bytes_accessed=2 * (half * cols * count + rows * samples),
-            transcendentals=0,
-        )
-
-    last, folded, held_last, message = pl.pallas_call(
+    return pl.pallas_call(
         functools.partial(first_kernel, chips),
-        out_shape=[
-            block,
-            jax.ShapeDtypeStruct((rows, half), BF16),
-            jax.ShapeDtypeStruct((1, half, cols), BF16),
-            jax.ShapeDtypeStruct((height, cols), BF16),
+        out_shape=[jax.ShapeDtypeStruct((rows + height, cols), BF16)] * chips
+        + [
+            jax.ShapeDtypeStruct(table.shape, BF16),
+            jax.ShapeDtypeStruct((chips, owners, ROWS, period), F32),
         ],
-        in_specs=[smem()] + [hbm()] * 6,
-        out_specs=[vmem()] * 4,
-        scratch_shapes=[pltpu.VMEM((rows, samples), BF16)]
+        in_specs=[smem()] + [hbm()] * 7,
+        out_specs=[vmem()] * (chips + 2),
+        scratch_shapes=[pltpu.VMEM(turns.shape, F32), pltpu.VMEM((rows, samples), BF16)]
         + [pltpu.VMEM(fact.shape, fact.dtype) for fact in facts]
-        + [pltpu.SemaphoreType.DMA((6,))],
-        cost_estimate=cost(1),
-        compiler_params=params(24),
-        name="first_panel_dft",
-    )(ids, table, in_hbm(panel), *[in_hbm(fact) for fact in facts])
-    *blocks, held = pl.pallas_call(
-        functools.partial(second_kernel, chips),
-        out_shape=[block] * (chips - 1) + [jax.ShapeDtypeStruct((chips - 1, half, cols), BF16)],
-        in_specs=[smem(), hbm(), vmem(), vmem()],
-        out_specs=[vmem()] * chips,
-        scratch_shapes=[pltpu.SemaphoreType.DMA((chips - 1,))],
-        cost_estimate=cost(chips - 1),
+        + [pltpu.VMEM((chips, rows, 2 * period), BF16), pltpu.SemaphoreType.DMA((8,))],
+        cost_estimate=cost_of(rows, table, turns),
         compiler_params=params(24),
         name="near_panel_dft",
-    )(ids, table, folded, message)
-    return blocks + [last], [held, held_last]
-
-
-def forward_kernel(chips, count, ids_ref, table_ref, last_ref, *refs):
-    inputs, outs = refs[:count], refs[count:]
+    )(ids, *[in_hbm(array) for array in (table, turns, panel, *facts)])
+
+
+def forward_kernel(chips, count, ids_ref, table_ref, wide, *refs):
+    inputs, outs, y_ref = refs[:count], refs[count:-1], refs[-1]
     for number, x_ref in enumerate(inputs):
         rows = x_ref.shape[0]
-        folded = fold(x_ref, ids_ref[chips].astype(F32))
-        for d in range(chips - 1, -1, -1):
-            table = last_ref[0] if d == chips - 1 else table_ref[d]
-            spectra = jnp.dot(folded, table, preferred_element_type=F32)
-            outs[d][number * rows : (number + 1) * rows, :] = spectra.astype(BF16)
-
-
-def forward_of(ids, arrays, tables, name):
-    rows, samples = arrays[0].shape
-    half, cols = tables[0].shape[1:]
-    chips = tables[0].shape[0] + 1
+        turn_rows(ids_ref, x_ref, 0, rows, wide, y_ref, number * rows)
+    for d in range(chips - 1, -1, -1):
+        outs[d][...] = jnp.dot(
+            y_ref[d], table_ref[...], preferred_element_type=F32
+        ).astype(BF16)
+
+
+def forward_of(ids, arrays, table, wide, name):
+    rows = len(arrays) * arrays[0].shape[0]
+    cols = table.shape[1]
+    chips, _, _, period = wide.shape
     count = len(arrays)
     return pl.pallas_call(
         functools.partial(forward_kernel, chips, count),
-        out_shape=[jax.ShapeDtypeStruct((count * rows, cols), BF16)] * chips,
+        out_shape=[jax.ShapeDtypeStruct((rows, cols), BF16)] * chips,
         in_specs=[smem()] + [vmem()] * (count + 2),
         out_specs=[vmem()] * chips,
-        cost_estimate=pl.CostEstimate(
-            flops=2 * count * rows * half * cols * chips,
-            bytes_accessed=2 * count * rows * samples * 2,
-            transcendentals=0,
-        ),
+        scratch_shapes=[pltpu.VMEM((chips, rows, 2 * period), BF16)],
+        cost_estimate=cost_of(rows, table, wide),
         compiler_params=params(24),
         name=name,
-    )(ids, *tables, *arrays)
+    )(ids, table, wide, *arrays)
 
 
 def masks_kernel(rows, ids_ref, *refs):
@@ -298,58 +295,91 @@
     )(ids, plan, *blocks)
 
 
-def product_kernel(first, chips, *refs):
-    main_ref, border_ref, gather_ref, summer_ref, weight_ref = refs[:5]
-    spectra_refs, outs = refs[5 : 5 + chips], refs[5 + chips :]
-    cols = main_ref.shape[2]
-    half = cols // 2
+def add_products(steps, distances, main_ref, border_ref, masks, spectra_refs, totals):
+    gather_ref, summer_ref, weight_ref = masks
+    half = main_ref.shape[2] // 2
     rows = weight_ref.shape[0]
-    receivers = summer_ref.shape[0]
-    extended = [
-        jnp.concatenate([main_ref[first + step], border_ref[first + step]], 0)
-        for step in range(CHUNK)
-    ]
-    totals = [jnp.zeros((receivers, cols), F32) for _ in range(CHUNK)]
-    for block in range(2 * chips):
-        at = block * rows
-        mine = block % 2 * rows
-        spectra = spectra_refs[block // 2][mine : mine + rows, :].astype(F32)
-        spectra = spectra * weight_ref[:, block : block + 1]
-        real_d, imag_d = spectra[:, :half], spectra[:, half:]
-        for step in range(CHUNK):
-            picked = jnp.dot(
-                gather_ref[at : at + rows, :], extended[step], preferred_element_type=F32
-            )
-            real_p, imag_p = picked[:, :half], picked[:, half:]
-            product = jnp.concatenate(
-                [real_p * real_d - imag_p * imag_d, real_p * imag_d + imag_p * real_d], 1
-            ).astype(BF16)
-            totals[step] += jnp.dot(
-                summer_ref[:, at : at + rows], product, preferred_element_type=F32
-            )
-    for step in range(CHUNK):
-        result = totals[step].astype(BF16)
+    extended = [jnp.concatenate([main_ref[k], border_ref[k]], 0) for k in steps]
+    for distance, spectra_ref in zip(distances, spectra_refs):
+        for across in range(2):
+            block = 2 * distance + across
+            at = block * rows
+            spectra = spectra_ref[across * rows : (across + 1) * rows, :].astype(F32)
+            spectra = spectra * weight_ref[:, block : block + 1]
+            real_d, imag_d = spectra[:, :half], spectra[:, half:]
+            for number in range(len(steps)):
+                picked = jnp.dot(
+                    gather_ref[at : at + rows, :], extended[number], preferred_element_type=F32
+                )
+                real_p, imag_p = picked[:, :half], picked[:, half:]
+                product = jnp.concatenate(
+                    [real_p * real_d - imag_p * imag_d, real_p * imag_d + imag_p * real_d], 1
+                ).astype(BF16)
+                part = jnp.dot(
+                    summer_ref[:, at : at + rows], product, preferred_element_type=F32
+                )
+                totals[number] = part if totals[number] is None else totals[number] + part
+    return totals
+
+
+def early_kernel(distances, main_ref, border_ref, *refs):
+    masks, spectra_refs, partial_ref = refs[:3], refs[3:-1], refs[-1]
+    for first in range(0, STEPS, CHUNK):
+        steps = range(first, first + CHUNK)
+        totals = [None] * CHUNK
+        add_products(steps, distances, main_ref, border_ref, masks, spectra_refs, totals)
+        for number, step in enumerate(steps):
+            partial_ref[step] = totals[number]
+
+
+def early_sums(distances, main, border, masks, spectra):
+    cols = main.shape[2]
+    gather, summer, _ = masks
+    traces = len(spectra) * spectra[0].shape[0]
+    return pl.pallas_call(
+        functools.partial(early_kernel, distances),
+        out_shape=jax.ShapeDtypeStruct((STEPS, summer.shape[0], cols), F32),
+        in_specs=[vmem()] * (5 + len(spectra)),
+        out_specs=vmem(),
+        cost_estimate=pl.CostEstimate(
+            flops=2 * STEPS * cols * traces * (gather.shape[1] + summer.shape[0]),
+            bytes_accessed=2 * traces * cols,
+            transcendentals=0,
+        ),
+        compiler_params=params(24),
+        name="early_sums",
+    )(main, border, *masks, *spectra)
+
+
+def late_kernel(first, chips, distances, main_ref, border_ref, partial_ref, *refs):
+    masks, spectra_refs, outs = refs[:3], refs[3:-chips], refs[-chips:]
+    steps = range(first, first + CHUNK)
+    totals = [partial_ref[step] for step in steps]
+    add_products(steps, distances, main_ref, border_ref, masks, spectra_refs, totals)
+    for number in range(CHUNK):
+        result = totals[number].astype(BF16)
         for place in range(2 * chips):
             rows_of = result[place * RECV_DEV : (place + 1) * RECV_DEV]
-            outs[place // 2][place % 2, step] = rows_of
-
-
-def receivers_of(first, main, border, gather, summer, weight, spectra):
-    chips = len(spectra)
+            outs[place // 2][place % 2, number] = rows_of
+
+
+def late_sums(first, chips, distances, main, border, partial, masks, spectra):
     cols = main.shape[2]
-    return pl.pallas_call(
-        functools.partial(product_kernel, first, chips),
+    gather, summer, _ = masks
+    traces = len(spectra) * spectra[0].shape[0]
+    return pl.pallas_call(
+        functools.partial(late_kernel, first, chips, distances),
         out_shape=[jax.ShapeDtypeStruct((2, CHUNK, RECV_DEV, cols), BF16)] * chips,
-        in_specs=[vmem()] * (5 + chips),
+        in_specs=[vmem()] * (6 + len(spectra)),
         out_specs=[vmem()] * chips,
         cost_estimate=pl.CostEstimate(
-            flops=2 * CHUNK * cols * gather.shape[0] * (gather.shape[1] + summer.shape[0]),
-            bytes_accessed=2 * (gather.size + summer.size + gather.shape[0] * cols),
+            flops=2 * CHUNK * cols * traces * (gather.shape[1] + summer.shape[0]),
+            bytes_accessed=2 * traces * cols,
             transcendentals=0,
         ),
         compiler_params=params(24),
         name="receiver_sums",
-    )(main, border, gather, summer, weight, *spectra)
+    )(main, border, partial, *masks, *spectra)
 
 
 def weighted_sum(terms):
@@ -461,8 +491,8 @@
     chips = owners // 2
     samples = traces.shape[1]
     panel = panels[0, 0]
-    forward, inverse, turns = make_tables(samples, NF, owners)
-    forward = jnp.asarray(forward)
+    forward, forward_turns, inverse, turns = make_tables(samples, NF, owners)
+    tables = (jnp.asarray(forward), jnp.asarray(forward_turns))
     inverse = jnp.asarray(inverse)
     turns = jnp.asarray(turns)
 
@@ -477,23 +507,26 @@
     panel_across = swap(panel, 1)
     traces_across = swap(traces, 1)
     facts = [panel_index, receiver_slot, owner.reshape(-1), aperture_weight]
-    near_panels, tables = near_of(near_ids, panel, forward, facts)
+    *near_panels, table, wide = near_of(near_ids, panel, *tables, facts)
     near_panels = send_blocks(near_panels)
-    far_panels = forward_of(near_ids, [panel_across], tables, "far_panel_dft")
+    far_panels = forward_of(near_ids, [panel_across], table, wide, "far_panel_dft")
     far_panels = send_blocks(far_panels)
-    spectra = forward_of(near_ids, [traces, traces_across], tables, "trace_dft")
+    spectra = forward_of(near_ids, [traces, traces_across], table, wide, "trace_dft")
     spectra = send_blocks(spectra)
 
     blocks = [block for pair in zip(near_panels, far_panels) for block in pair]
     main, edges, near_facts = choose(near_ids, plan, blocks)
     facts = [near_facts, swap(near_facts, 1)]
     border = lax.ppermute(edges, "area", [(i, i + 1) for i in range(areas - 1)])
-    gather, summer, weight = masks_of(near_ids, facts, panel.shape[0], panel.shape[0] + EDGE)
-
+    masks = masks_of(near_ids, facts, panel.shape[0], panel.shape[0] + EDGE)
+
+    early = [0]
+    late = [d for d in range(chips) if d not in early]
+    partial = early_sums(early, main, border, masks, [spectra[d] for d in early])
     groups = []
     for first in range(0, STEPS, CHUNK):
-        sums = receivers_of(first, main, border, gather, summer, weight, spectra)
-        sums = send_blocks(sums)
+        given = (main, border, partial, masks, [spectra[d] for d in late])
+        sums = send_blocks(late_sums(first, chips, late, *given))
         across = swap(jnp.stack([block[1] for block in sums]), 1)
         groups.append(sums + [across])
     return inverse_of(all_ids, groups, inverse, turns)

time: 55.5 us -> 52.6 us (0.948)
  waiting for transfers between devices: 11.1 us -> 8.96 us
  Pallas kernels: 20.4 us -> 18.8 us
  starting transfers between devices: 23.3 us -> 24.1 us
    pallas_call x4, Pallas kernels: 11.7 us -> 8.58 us  [the longest x2 4.13 us: late_sums(): pl.pallas_call(functools.partial(late_kernel, first, chips, distances), o...]
    ppermute x20, waiting for transfers between devices: 11.1 us -> 8.95 us  [swap(): return lax.ppermute(array, 'line', [(i, i ^ distance) for i in devices])]
    pallas_call x2, Pallas kernels: 3.07 us -> 4.57 us  [forward_of(): pl.pallas_call(functools.partial(forward_kernel, chips, count), out_shape...]
    ppermute x20, starting transfers between devices: 19.6 us -> 20.6 us  [swap(): return lax.ppermute(array, 'line', [(i, i ^ distance) for i in devices])]
  transfers between devices with their start and end apart: 21 -> 21, of which waited for: 7 -> 6; matrix products, arithmetic and copies ran while one was open for 1% -> 1% of each run, Pallas kernels for 26% -> 26%
where the time goes in v4:
time: 52.6 us; the launch traced here: 52.4 us
  starting transfers between devices  24.1 us (46%)
  Pallas kernels  18.8 us (36%)
  waiting for transfers between devices  8.96 us (17%)
    ppermute x20, starting transfers between devices, swap(): return lax.ppermute(array, 'line', [(i, i ^ distance) for i in devices])  20.6 us
    ppermute x20, waiting for transfers between devices, swap(): return lax.ppermute(array, 'line', [(i, i ^ distance) for i in devices])  8.95 us
    pallas_call x2, Pallas kernels, forward_of(): pl.pallas_call(functools.partial(forward_kernel, chips, count), out_shape...  4.57 us
    pallas_call x2, Pallas kernels, late_sums(): pl.pallas_call(functools.partial(late_kernel, first, chips, distances), o...  4.13 us
    ppermute x1, starting transfers between devices, local(): border = lax.ppermute(edges, 'area', [(i, i + 1) for i in range(areas - 1)])  3.49 us
    pallas_call x1, Pallas kernels, near_of(): pl.pallas_call(functools.partial(first_kernel, chips), out_shape=[jax.Sha...  2.94 us
    pallas_call x1, Pallas kernels, inverse_of(): pl.pallas_call(functools.partial(inverse_kernel, owners // 2), in_specs=[...  2.89 us
    pallas_call x1, Pallas kernels, masks_of(): pl.pallas_call(functools.partial(masks_kernel, rows), out_shape=[jax.Shap...  1.99 us
  transfers between devices with their start and end apart: 21, of which 6 were waited for; matrix products, arithmetic and copies ran while one was open for 1% of the time, Pallas kernels for 26%

profile of v4, /device:TPU:0, one launch (start us, length us, event | category | flops | bytes accessed | tf_op | source)
XLA Modules:
  0.0 52.4 jit_solution(13898040934656763527)
XLA Ops:
  0.6 2.9 %near_panel_dft.1 = (bf16[272,256]{1,0:T(8,128)(2,1)S(1)}, bf16[272,256]{1,0:T(8,128)(2,1)S(1)}, bf16[272,256]{1,0:T(8,128)(2,1)S(1)}, bf16[272,256]{1,0:T(8,128...) custom-call(s32[8]{0:T(128)S(1)} %stack.65.ids_ref, bf16[512,256]{1,0:T(8,128)(2,1)} %constant.22.clone.table_ref, ...), custom_call_target="tpu_custom_call" | custom-call | flops 268435456 | bytes 2097152 | tf_op jit(solution)/shard_map/near_panel_dft/pallas_call | solution.py:157
  3.6 3.0 %collective-permute-start.1 = (bf16[272,256]{1,0:T(8,128)(2,1)S(1)}, bf16[272,256]{1,0:T(8,128)(2,1)S(1)}, u32[]{:S(2)}, u32[]{:S(2)}) collective-permute-start(bf16[272,256]{1,0:T(8,128)(2,1)S(1)} %get-tuple-element.37), channel_id=1, source_target_pairs={{0,2},{1,3},{2,0},{3,1},{4,6},{5,7},{6,4},{7,5},{8,10},{9,11},{10,... | collective-permute-start | bytes 417800 | tf_op jit(solution)/shard_map/ppermute | solution.py:479
  6.5 1.5 %collective-permute-start.3 = (bf16[272,256]{1,0:T(8,128)(2,1)S(1)}, bf16[272,256]{1,0:T(8,128)(2,1)S(1)}, u32[]{:S(2)}, u32[]{:S(2)}) collective-permute-start(bf16[272,256]{1,0:T(8,128)(2,1)S(1)} %get-tuple-element.39), channel_id=1, source_target_pairs={{0,4},{1,5},{2,6},{3,7},{4,0},{5,1},{6,2},{7,3},{8,12},{9,13},{10,... | collective-permute-start | bytes 417800 | tf_op jit(solution)/shard_map/ppermute | solution.py:479
  8.1 1.8 %far_panel_dft.1 = (bf16[256,256]{1,0:T(8,128)(2,1)S(1)}, bf16[256,256]{1,0:T(8,128)(2,1)S(1)}, bf16[256,256]{1,0:T(8,128)(2,1)S(1)}, bf16[256,256]{1,0:T(8,128)(2,1)S(1)}) custom-call(s32[8]{0:T(128)S(1)} %stack.65.ids_ref, bf16[512,256]{1,0:T(8,128)(2,1)S(1)} %get-tuple-element.34.table_ref, f32[4,8,16,256]{3,2,1,0:T(8,128)S(1)} %get-tuple-element.35.wide, ...), custom_call_target="tpu_custom_call" | custom-call | flops 134217728 | bytes 2097152 | tf_op jit(solution)/shard_map/far_panel_dft/pallas_call | solution.py:191
  9.9 2.0 %collective-permute-start.2 = (bf16[256,256]{1,0:T(8,128)(2,1)S(1)}, bf16[256,256]{1,0:T(8,128)(2,1)S(1)}, u32[]{:S(2)}, u32[]{:S(2)}) collective-permute-start(bf16[256,256]{1,0:T(8,128)(2,1)S(1)} %get-tuple-element.38), channel_id=1, source_target_pairs={{0,2},{1,3},{2,0},{3,1},{4,6},{5,7},{6,4},{7,5},{8,10},{9,11},{10,... | collective-permute-start | bytes 393224 | tf_op jit(solution)/shard_map/ppermute | solution.py:479
  11.9 1.5 %collective-permute-start.4 = (bf16[256,256]{1,0:T(8,128)(2,1)S(1)}, bf16[256,256]{1,0:T(8,128)(2,1)S(1)}, u32[]{:S(2)}, u32[]{:S(2)}) collective-permute-start(bf16[256,256]{1,0:T(8,128)(2,1)S(1)} %get-tuple-element.40), channel_id=1, source_target_pairs={{0,4},{1,5},{2,6},{3,7},{4,0},{5,1},{6,2},{7,3},{8,12},{9,13},{10,... | collective-permute-start | bytes 393224 | tf_op jit(solution)/shard_map/ppermute | solution.py:479
  13.4 1.1 %collective-permute-start.6 = (bf16[256,256]{1,0:T(8,128)(2,1)S(1)}, bf16[256,256]{1,0:T(8,128)(2,1)S(1)}, u32[]{:S(2)}, u32[]{:S(2)}) collective-permute-start(bf16[256,256]{1,0:T(8,128)(2,1)S(1)} %get-tuple-element.42), channel_id=1, source_target_pairs={{0,6},{1,7},{2,4},{3,5},{4,2},{5,3},{6,0},{7,1},{8,14},{9,15},{10,... | collective-permute-start | bytes 393224 | tf_op jit(solution)/shard_map/ppermute | solution.py:479
  14.5 2.8 %trace_dft.1 = (bf16[512,256]{1,0:T(8,128)(2,1)S(1)}, bf16[512,256]{1,0:T(8,128)(2,1)S(1)}, bf16[512,256]{1,0:T(8,128)(2,1)S(1)}, bf16[512,256]{1,0:T(8,128)(2,1)S(1)}) custom-call(s32[8]{0:T(128)S(1)} %stack.65.ids_ref, bf16[512,256]{1,0:T(8,128)(2,1)S(1)} %get-tuple-element.34.table_ref, f32[4,8,16,256]{3,2,1,0:T(8,128)S(1)} %get-tuple-element.35.wide, ...), custom_call_target="tpu_custom_call" | custom-call | flops 268435456 | bytes 4194304 | tf_op jit(solution)/shard_map/trace_dft/pallas_call | solution.py:191
  18.3 1.5 %collective-permute-start.11 = (bf16[512,256]{1,0:T(8,128)(2,1)S(1)}, bf16[512,256]{1,0:T(8,128)(2,1)S(1)}, u32[]{:S(2)}, u32[]{:S(2)}) collective-permute-start(bf16[512,256]{1,0:T(8,128)(2,1)S(1)} %get-tuple-element.51), channel_id=1, source_target_pairs={{0,4},{1,5},{2,6},{3,7},{4,0},{5,1},{6,2},{7,3},{8,12},{9,13},{10,... | collective-permute-start | bytes 786440 | tf_op jit(solution)/shard_map/ppermute | solution.py:479
  22.0 3.5 %collective-permute-start.7 = (bf16[4,64,256]{2,1,0:T(8,128)(2,1)S(1)}, bf16[4,64,256]{2,1,0:T(8,128)(2,1)S(1)}, u32[]{:S(2)}, u32[]{:S(2)}) collective-permute-start(bf16[4,64,256]{2,1,0:T(8,128)(2,1)S(1)} %get-tuple-element.44), channel_id=1, source_target_pairs={{0,8},{8,16},{16,24},{1,9},{9,17},{17,25},{2,10},{10,18},{18,26},{... | collective-permute-start | bytes 393224 | tf_op jit(solution)/shard_map/ppermute | solution.py:520
  25.6 1.2 %collective-permute-done.8.refs_1_ = bf16[4,16,256]{2,1,0:T(8,128)(2,1)S(1)} collective-permute-done((bf16[4,16,256]{2,1,0:T(8,128)(2,1)S(1)}, bf16[4,16,256]{2,1,0:T(8,128)(2,1)S(1)}, u32[]{:S(2)}, u32[]{:S(2)}) %collective-permute-start.8) | collective-permute-done | bytes 32800 | tf_op jit(solution)/shard_map/ppermute | solution.py:479
  26.8 2.0 %masks.1 = (bf16[2048,320]{1,0:T(8,128)(2,1)S(1)}, bf16[512,2048]{1,0:T(8,128)(2,1)S(1)}, f32[256,8]{1,0:T(8,128)S(1)}) custom-call(s32[8]{0:T(128)S(1)} %stack.65.ids_ref, bf16[4,16,256]{2,1,0:T(8,128)(2,1)S(1)} %get-tuple-element.45.refs_0_, bf16[4,16,256]{2,1,0:T(8,128)(2,1)S(1)} %collective-permute-done.8.refs_1_), custom_call_target="tpu_custom_call" | custom-call | flops 10223616 | bytes 3407872 | tf_op jit(solution)/shard_map/masks/pallas_call | solution.py:241
  28.8 1.5 %early_sums.1.partial_ref = f32[4,512,256]{2,1,0:T(8,128)S(1)} custom-call(bf16[4,256,256]{2,1,0:T(8,128)(2,1)S(1)} %get-tuple-element.43.main_ref, bf16[4,64,256]{2,1,0:T(8,128)(2,1)S(1)} %collective-permute-done.7.border_ref, bf16[2048,320]{1,0:T(8,128)(2,1)S(1)} %get-tuple-element.46.refs_0_, bf16[512,2048]{1,0:T(8,128)(2,1)S(1)} %get-tuple-element.47.refs_1_, ...), custom_call_target="tpu_custom_call" | custom-call | flops 872415232 | bytes 262144 | tf_op jit(solution)/shard_map/early_sums/pallas_call | solution.py:339
  30.3 1.4 %collective-permute-done.11.refs_4_ = bf16[512,256]{1,0:T(8,128)(2,1)S(1)} collective-permute-done((bf16[512,256]{1,0:T(8,128)(2,1)S(1)}, bf16[512,256]{1,0:T(8,128)(2,1)S(1)}, u32[]{:S(2)}, u32[]{:S(2)}) %collective-permute-start.11) | collective-permute-done | bytes 262176 | tf_op jit(solution)/shard_map/ppermute | solution.py:479
  31.8 2.1 %receiver_sums.2 = (bf16[2,2,64,256]{3,2,1,0:T(8,128)(2,1)S(1)}, bf16[2,2,64,256]{3,2,1,0:T(8,128)(2,1)S(1)}, bf16[2,2,64,256]{3,2,1,0:T(8,128)(2,1)S(1)}, bf16[2,2,64,256]{3,2,1,0:T(8,128)(2,1)S(1)}) custom-call(bf16[4,256,256]{2,1,0:T(8,128)(2,1)S(1)} %get-tuple-element.43.main_ref, bf16[4,64,256]{2,1,0:T(8,128)(2,1)S(1)} %collective-permute-done.7.border_ref, ...), custom_call_target="tpu_custom_call" | custom-call | flops 1308622848 | bytes 786432 | tf_op jit(solution)/shard_map/receiver_sums/pallas_call | solution.py:370
  33.8 1.4 %collective-permute-start.13 = (bf16[2,2,64,256]{3,2,1,0:T(8,128)(2,1)S(1)}, bf16[2,2,64,256]{3,2,1,0:T(8,128)(2,1)S(1)}, u32[]{:S(2)}, u32[]{:S(2)}) collective-permute-start(bf16[2,2,64,256]{3,2,1,0:T(8,128)(2,1)S(1)} %get-tuple-element.54), channel_id=1, source_target_pairs={{0,2},{1,3},{2,0},{3,1},{4,6},{5,7},{6,4},{7,5},{8,10},{9,11},{10,... | collective-permute-start | bytes 393224 | tf_op jit(solution)/shard_map/ppermute | solution.py:479
  35.9 1.4 %collective-permute-start.15 = (bf16[2,2,64,256]{3,2,1,0:T(8,128)(2,1)S(1)}, bf16[2,2,64,256]{3,2,1,0:T(8,128)(2,1)S(1)}, u32[]{:S(2)}, u32[]{:S(2)}) collective-permute-start(bf16[2,2,64,256]{3,2,1,0:T(8,128)(2,1)S(1)} %get-tuple-element.56), channel_id=1, source_target_pairs={{0,6},{1,7},{2,4},{3,5},{4,2},{5,3},{6,0},{7,1},{8,14},{9,15},{10,... | collective-permute-start | bytes 393224 | tf_op jit(solution)/shard_map/ppermute | solution.py:479
  37.4 2.1 %receiver_sums.3 = (bf16[2,2,64,256]{3,2,1,0:T(8,128)(2,1)S(1)}, bf16[2,2,64,256]{3,2,1,0:T(8,128)(2,1)S(1)}, bf16[2,2,64,256]{3,2,1,0:T(8,128)(2,1)S(1)}, bf16[2,2,64,256]{3,2,1,0:T(8,128)(2,1)S(1)}) custom-call(bf16[4,256,256]{2,1,0:T(8,128)(2,1)S(1)} %get-tuple-element.43.main_ref, bf16[4,64,256]{2,1,0:T(8,128)(2,1)S(1)} %collective-permute-done.7.border_ref, ...), custom_call_target="tpu_custom_call" | custom-call | flops 1308622848 | bytes 786432 | tf_op jit(solution)/shard_map/receiver_sums/pallas_call | solution.py:370
  39.5 1.4 %collective-permute-start.17 = (bf16[2,2,64,256]{3,2,1,0:T(8,128)(2,1)S(1)}, bf16[2,2,64,256]{3,2,1,0:T(8,128)(2,1)S(1)}, u32[]{:S(2)}, u32[]{:S(2)}) collective-permute-start(bf16[2,2,64,256]{3,2,1,0:T(8,128)(2,1)S(1)} %get-tuple-element.58), channel_id=1, source_target_pairs={{0,2},{1,3},{2,0},{3,1},{4,6},{5,7},{6,4},{7,5},{8,10},{9,11},{10,... | collective-permute-start | bytes 393224 | tf_op jit(solution)/shard_map/ppermute | solution.py:479
  41.6 1.4 %collective-permute-start.19 = (bf16[2,2,64,256]{3,2,1,0:T(8,128)(2,1)S(1)}, bf16[2,2,64,256]{3,2,1,0:T(8,128)(2,1)S(1)}, u32[]{:S(2)}, u32[]{:S(2)}) collective-permute-start(bf16[2,2,64,256]{3,2,1,0:T(8,128)(2,1)S(1)} %get-tuple-element.60), channel_id=1, source_target_pairs={{0,6},{1,7},{2,4},{3,5},{4,2},{5,3},{6,0},{7,1},{8,14},{9,15},{10,... | collective-permute-start | bytes 393224 | tf_op jit(solution)/shard_map/ppermute | solution.py:479
  43.2 2.6 %collective-permute-done.17.refs_6_ = bf16[2,2,64,256]{3,2,1,0:T(8,128)(2,1)S(1)} collective-permute-done((bf16[2,2,64,256]{3,2,1,0:T(8,128)(2,1)S(1)}, bf16[2,2,64,256]{3,2,1,0:T(8,128)(2,1)S(1)}, u32[]{:S(2)}, u32[]{:S(2)}) %collective-permute-start.17) | collective-permute-done | bytes 131104 | tf_op jit(solution)/shard_map/ppermute | solution.py:479
  45.9 2.0 %collective-permute-done.18.refs_7_ = bf16[2,2,64,256]{3,2,1,0:T(8,128)(2,1)S(1)} collective-permute-done((bf16[2,2,64,256]{3,2,1,0:T(8,128)(2,1)S(1)}, bf16[2,2,64,256]{3,2,1,0:T(8,128)(2,1)S(1)}, u32[]{:S(2)}, u32[]{:S(2)}) %collective-permute-start.18) | collective-permute-done | bytes 131104 | tf_op jit(solution)/shard_map/ppermute | solution.py:479
  48.1 1.4 %collective-permute-done.20.refs_9_ = bf16[4,2,64,256]{3,2,1,0:T(8,128)(2,1)S(1)} collective-permute-done((bf16[4,2,64,256]{3,2,1,0:T(8,128)(2,1)S(1)}, bf16[4,2,64,256]{3,2,1,0:T(8,128)(2,1)S(1)}, u32[]{:S(2)}, u32[]{:S(2)}) %collective-permute-start.20) | collective-permute-done | bytes 262176 | tf_op jit(solution)/shard_map/ppermute | solution.py:479
  49.5 2.9 %inverse_dft.1 = bf16[4,64,2048]{2,1,0:T(8,128)(2,1)} custom-call(s32[8]{0:T(128)S(1)} %stack.60.ids_ref, bf16[2,256,512]{2,1,0:T(8,128)(2,1)S(1)} %copy-done.1, f32[8,2,256]{2,1,0:T(2,128)S(1)} %copy-done.2, bf16[2,2,64,256]{3,2,1,0:T(8,128)(2,1)S(1)} %get-tuple-element.53.refs_0_, bf16[2,2,64,256]{3,2,1,0:T(8,128)(2,1)S(1)} %collective-permute-done.13.refs_1_, ...), custom_call_target="tpu_custom_call" | custom-call | flops 536870912 | bytes 1048576 | tf_op jit(solution)/shard_map/inverse_dft/pallas_call | solution.py:461
  (47 shorter events, 5.7 us)
Async XLA Ops:
  0.0 14.5 %copy-start = (bf16[256,2048]{1,0:T(8,128)(2,1)S(1)}, bf16[256,2048]{1,0:T(8,128)(2,1)}, u32[]{:S(2)}) copy-start(bf16[256,2048]{1,0:T(8,128)(2,1)} %refs_0_.3) | copy-start | bytes 3145732
  0.0 8.1 %collective-permute-start = (bf16[256,2048]{1,0:T(8,128)(2,1)}, bf16[256,2048]{1,0:T(8,128)(2,1)S(1)}, u32[]{:S(2)}, u32[]{:S(2)}) collective-permute-start(bf16[256,2048]{1,0:T(8,128)(2,1)} %bitcast.14), channel_id=1, source_target_pairs={{0,1},{1,0},{2,3},{3,2},{4,5},{5,4},{6,7},{7,6},{8,9},{9,8},{10,11... | collective-permute-start | bytes 3145736 | tf_op jit(solution)/shard_map/ppermute | solution.py:479
  0.5 12.9 %collective-permute-start.9 = (bf16[256,2048]{1,0:T(8,128)(2,1)}, bf16[256,2048]{1,0:T(8,128)(2,1)S(1)}, u32[]{:S(2)}, u32[]{:S(2)}) collective-permute-start(bf16[256,2048]{1,0:T(8,128)(2,1)} %refs_0_.3), channel_id=1, source_target_pairs={{0,1},{1,0},{2,3},{3,2},{4,5},{5,4},{6,7},{7,6},{8,9},{9,8},{10,11... | collective-permute-start | bytes 3145736 | tf_op jit(solution)/shard_map/ppermute | solution.py:479
  3.6 8.3 %collective-permute-start.1 = (bf16[272,256]{1,0:T(8,128)(2,1)S(1)}, bf16[272,256]{1,0:T(8,128)(2,1)S(1)}, u32[]{:S(2)}, u32[]{:S(2)}) collective-permute-start(bf16[272,256]{1,0:T(8,128)(2,1)S(1)} %get-tuple-element.37), channel_id=1, source_target_pairs={{0,2},{1,3},{2,0},{3,1},{4,6},{5,7},{6,4},{7,5},{8,10},{9,11},{10,... | collective-permute-start | bytes 417800 | tf_op jit(solution)/shard_map/ppermute | solution.py:479
  6.5 10.8 %collective-permute-start.3 = (bf16[272,256]{1,0:T(8,128)(2,1)S(1)}, bf16[272,256]{1,0:T(8,128)(2,1)S(1)}, u32[]{:S(2)}, u32[]{:S(2)}) collective-permute-start(bf16[272,256]{1,0:T(8,128)(2,1)S(1)} %get-tuple-element.39), channel_id=1, source_target_pairs={{0,4},{1,5},{2,6},{3,7},{4,0},{5,1},{6,2},{7,3},{8,12},{9,13},{10,... | collective-permute-start | bytes 417800 | tf_op jit(solution)/shard_map/ppermute | solution.py:479
  8.1 10.2 %collective-permute-start.5 = (bf16[272,256]{1,0:T(8,128)(2,1)S(1)}, bf16[272,256]{1,0:T(8,128)(2,1)S(1)}, u32[]{:S(2)}, u32[]{:S(2)}) collective-permute-start(bf16[272,256]{1,0:T(8,128)(2,1)S(1)} %get-tuple-element.41), channel_id=1, source_target_pairs={{0,6},{1,7},{2,4},{3,5},{4,2},{5,3},{6,0},{7,1},{8,14},{9,15},{10,... | collective-permute-start | bytes 417800 | tf_op jit(solution)/shard_map/ppermute | solution.py:479
  8.1 13.2 %copy-start.3 = (s32[4,4]{1,0:T(4,128)S(1)}, s32[4,4]{1,0:T(4,128)}, u32[]{:S(2)}) copy-start(s32[4,4]{1,0:T(4,128)} %plan_ref.1) | copy-start | bytes 196
  9.9 9.9 %collective-permute-start.2 = (bf16[256,256]{1,0:T(8,128)(2,1)S(1)}, bf16[256,256]{1,0:T(8,128)(2,1)S(1)}, u32[]{:S(2)}, u32[]{:S(2)}) collective-permute-start(bf16[256,256]{1,0:T(8,128)(2,1)S(1)} %get-tuple-element.38), channel_id=1, source_target_pairs={{0,2},{1,3},{2,0},{3,1},{4,6},{5,7},{6,4},{7,5},{8,10},{9,11},{10,... | collective-permute-start | bytes 393224 | tf_op jit(solution)/shard_map/ppermute | solution.py:479
  11.9 9.1 %collective-permute-start.4 = (bf16[256,256]{1,0:T(8,128)(2,1)S(1)}, bf16[256,256]{1,0:T(8,128)(2,1)S(1)}, u32[]{:S(2)}, u32[]{:S(2)}) collective-permute-start(bf16[256,256]{1,0:T(8,128)(2,1)S(1)} %get-tuple-element.40), channel_id=1, source_target_pairs={{0,4},{1,5},{2,6},{3,7},{4,0},{5,1},{6,2},{7,3},{8,12},{9,13},{10,... | collective-permute-start | bytes 393224 | tf_op jit(solution)/shard_map/ppermute | solution.py:479
  13.4 7.8 %collective-permute-start.6 = (bf16[256,256]{1,0:T(8,128)(2,1)S(1)}, bf16[256,256]{1,0:T(8,128)(2,1)S(1)}, u32[]{:S(2)}, u32[]{:S(2)}) collective-permute-start(bf16[256,256]{1,0:T(8,128)(2,1)S(1)} %get-tuple-element.42), channel_id=1, source_target_pairs={{0,6},{1,7},{2,4},{3,5},{4,2},{5,3},{6,0},{7,1},{8,14},{9,15},{10,... | collective-permute-start | bytes 393224 | tf_op jit(solution)/shard_map/ppermute | solution.py:479
  17.4 13.0 %collective-permute-start.10 = (bf16[512,256]{1,0:T(8,128)(2,1)S(1)}, bf16[512,256]{1,0:T(8,128)(2,1)S(1)}, u32[]{:S(2)}, u32[]{:S(2)}) collective-permute-start(bf16[512,256]{1,0:T(8,128)(2,1)S(1)} %get-tuple-element.50), channel_id=1, source_target_pairs={{0,2},{1,3},{2,0},{3,1},{4,6},{5,7},{6,4},{7,5},{8,10},{9,11},{10,... | collective-permute-start | bytes 786440 | tf_op jit(solution)/shard_map/ppermute | solution.py:479
  18.3 13.5 %collective-permute-start.11 = (bf16[512,256]{1,0:T(8,128)(2,1)S(1)}, bf16[512,256]{1,0:T(8,128)(2,1)S(1)}, u32[]{:S(2)}, u32[]{:S(2)}) collective-permute-start(bf16[512,256]{1,0:T(8,128)(2,1)S(1)} %get-tuple-element.51), channel_id=1, source_target_pairs={{0,4},{1,5},{2,6},{3,7},{4,0},{5,1},{6,2},{7,3},{8,12},{9,13},{10,... | collective-permute-start | bytes 786440 | tf_op jit(solution)/shard_map/ppermute | solution.py:479
  19.8 12.0 %collective-permute-start.12 = (bf16[512,256]{1,0:T(8,128)(2,1)S(1)}, bf16[512,256]{1,0:T(8,128)(2,1)S(1)}, u32[]{:S(2)}, u32[]{:S(2)}) collective-permute-start(bf16[512,256]{1,0:T(8,128)(2,1)S(1)} %get-tuple-element.52), channel_id=1, source_target_pairs={{0,6},{1,7},{2,4},{3,5},{4,2},{5,3},{6,0},{7,1},{8,14},{9,15},{10,... | collective-permute-start | bytes 786440 | tf_op jit(solution)/shard_map/ppermute | solution.py:479
  22.0 6.8 %collective-permute-start.7 = (bf16[4,64,256]{2,1,0:T(8,128)(2,1)S(1)}, bf16[4,64,256]{2,1,0:T(8,128)(2,1)S(1)}, u32[]{:S(2)}, u32[]{:S(2)}) collective-permute-start(bf16[4,64,256]{2,1,0:T(8,128)(2,1)S(1)} %get-tuple-element.44), channel_id=1, source_target_pairs={{0,8},{8,16},{16,24},{1,9},{9,17},{17,25},{2,10},{10,18},{18,26},{... | collective-permute-start | bytes 393224 | tf_op jit(solution)/shard_map/ppermute | solution.py:520
  25.5 1.3 %collective-permute-start.8 = (bf16[4,16,256]{2,1,0:T(8,128)(2,1)S(1)}, bf16[4,16,256]{2,1,0:T(8,128)(2,1)S(1)}, u32[]{:S(2)}, u32[]{:S(2)}) collective-permute-start(bf16[4,16,256]{2,1,0:T(8,128)(2,1)S(1)} %get-tuple-element.45.refs_0_), channel_id=1, source_target_pairs={{0,1},{1,0},{2,3},{3,2},{4,5},{5,4},{6,7},{7,6},{8,9},{9,8},{10,11... | collective-permute-start | bytes 98312 | tf_op jit(solution)/shard_map/ppermute | solution.py:479
  33.8 7.8 %collective-permute-start.13 = (bf16[2,2,64,256]{3,2,1,0:T(8,128)(2,1)S(1)}, bf16[2,2,64,256]{3,2,1,0:T(8,128)(2,1)S(1)}, u32[]{:S(2)}, u32[]{:S(2)}) collective-permute-start(bf16[2,2,64,256]{3,2,1,0:T(8,128)(2,1)S(1)} %get-tuple-element.54), channel_id=1, source_target_pairs={{0,2},{1,3},{2,0},{3,1},{4,6},{5,7},{6,4},{7,5},{8,10},{9,11},{10,... | collective-permute-start | bytes 393224 | tf_op jit(solution)/shard_map/ppermute | solution.py:479
  35.2 7.9 %collective-permute-start.14 = (bf16[2,2,64,256]{3,2,1,0:T(8,128)(2,1)S(1)}, bf16[2,2,64,256]{3,2,1,0:T(8,128)(2,1)S(1)}, u32[]{:S(2)}, u32[]{:S(2)}) collective-permute-start(bf16[2,2,64,256]{3,2,1,0:T(8,128)(2,1)S(1)} %get-tuple-element.55), channel_id=1, source_target_pairs={{0,4},{1,5},{2,6},{3,7},{4,0},{5,1},{6,2},{7,3},{8,12},{9,13},{10,... | collective-permute-start | bytes 393224 | tf_op jit(solution)/shard_map/ppermute | solution.py:479
  35.9 7.1 %collective-permute-start.15 = (bf16[2,2,64,256]{3,2,1,0:T(8,128)(2,1)S(1)}, bf16[2,2,64,256]{3,2,1,0:T(8,128)(2,1)S(1)}, u32[]{:S(2)}, u32[]{:S(2)}) collective-permute-start(bf16[2,2,64,256]{3,2,1,0:T(8,128)(2,1)S(1)} %get-tuple-element.56), channel_id=1, source_target_pairs={{0,6},{1,7},{2,4},{3,5},{4,2},{5,3},{6,0},{7,1},{8,14},{9,15},{10,... | collective-permute-start | bytes 393224 | tf_op jit(solution)/shard_map/ppermute | solution.py:479
  39.4 10.1 %copy-start.1 = (bf16[2,256,512]{2,1,0:T(8,128)(2,1)S(1)}, bf16[2,256,512]{2,1,0:T(8,128)(2,1)}, u32[]{:S(2)}) copy-start(bf16[2,256,512]{2,1,0:T(8,128)(2,1)} %constant.24.clone.table_ref) | copy-start | bytes 1572868
  39.5 6.4 %collective-permute-start.17 = (bf16[2,2,64,256]{3,2,1,0:T(8,128)(2,1)S(1)}, bf16[2,2,64,256]{3,2,1,0:T(8,128)(2,1)S(1)}, u32[]{:S(2)}, u32[]{:S(2)}) collective-permute-start(bf16[2,2,64,256]{3,2,1,0:T(8,128)(2,1)S(1)} %get-tuple-element.58), channel_id=1, source_target_pairs={{0,2},{1,3},{2,0},{3,1},{4,6},{5,7},{6,4},{7,5},{8,10},{9,11},{10,... | collective-permute-start | bytes 393224 | tf_op jit(solution)/shard_map/ppermute | solution.py:479
  40.9 7.0 %collective-permute-start.18 = (bf16[2,2,64,256]{3,2,1,0:T(8,128)(2,1)S(1)}, bf16[2,2,64,256]{3,2,1,0:T(8,128)(2,1)S(1)}, u32[]{:S(2)}, u32[]{:S(2)}) collective-permute-start(bf16[2,2,64,256]{3,2,1,0:T(8,128)(2,1)S(1)} %get-tuple-element.59), channel_id=1, source_target_pairs={{0,4},{1,5},{2,6},{3,7},{4,0},{5,1},{6,2},{7,3},{8,12},{9,13},{10,... | collective-permute-start | bytes 393224 | tf_op jit(solution)/shard_map/ppermute | solution.py:479
  41.6 6.3 %collective-permute-start.19 = (bf16[2,2,64,256]{3,2,1,0:T(8,128)(2,1)S(1)}, bf16[2,2,64,256]{3,2,1,0:T(8,128)(2,1)S(1)}, u32[]{:S(2)}, u32[]{:S(2)}) collective-permute-start(bf16[2,2,64,256]{3,2,1,0:T(8,128)(2,1)S(1)} %get-tuple-element.60), channel_id=1, source_target_pairs={{0,6},{1,7},{2,4},{3,5},{4,2},{5,3},{6,0},{7,1},{8,14},{9,15},{10,... | collective-permute-start | bytes 393224 | tf_op jit(solution)/shard_map/ppermute | solution.py:479
  43.2 5.0 %collective-permute-start.16 = (bf16[4,2,64,256]{3,2,1,0:T(8,128)(2,1)S(1)}, bf16[4,2,64,256]{3,2,1,0:T(8,128)(2,1)S(1)}, u32[]{:S(2)}, u32[]{:S(2)}) collective-permute-start(bf16[4,2,64,256]{3,2,1,0:T(8,128)(2,1)S(1)} %pad_maximum_fusion), channel_id=1, source_target_pairs={{0,1},{1,0},{2,3},{3,2},{4,5},{5,4},{6,7},{7,6},{8,9},{9,8},{10,11... | collective-permute-start | bytes 786440 | tf_op jit(solution)/shard_map/ppermute | solution.py:479
  47.9 1.6 %collective-permute-start.20 = (bf16[4,2,64,256]{3,2,1,0:T(8,128)(2,1)S(1)}, bf16[4,2,64,256]{3,2,1,0:T(8,128)(2,1)S(1)}, u32[]{:S(2)}, u32[]{:S(2)}) collective-permute-start(bf16[4,2,64,256]{3,2,1,0:T(8,128)(2,1)S(1)} %pad_maximum_fusion.1), channel_id=1, source_target_pairs={{0,1},{1,0},{2,3},{3,2},{4,5},{5,4},{6,7},{7,6},{8,9},{9,8},{10,11... | collective-permute-start | bytes 786440 | tf_op jit(solution)/shard_map/ppermute | solution.py:479
  (1 other events, 10.1 us)

commit v5 on v4

--- a/solution.py
+++ b/solution.py
@@ -405,21 +405,18 @@
     return total
 
 
-def inverse_kernel(chips, ids_ref, table_ref, turns_ref, *refs):
-    out_ref, real_ref, imag_ref = refs[-3:]
+def inverse_kernel(chips, first, ids_ref, table_ref, turns_ref, *refs):
+    group = refs[: chips + 1]
+    out_ref, real_ref, imag_ref, sems = refs[-4 - CHUNK : -1 - CHUNK] + refs[-1:]
+    ready = refs[-1 - CHUNK : -1]
     owners, _, period = turns_ref.shape
     cols = table_ref.shape[1]
-    per_chunk = chips + 1
-    groups = [refs[i * per_chunk : (i + 1) * per_chunk] for i in range(STEPS // CHUNK)]
     for distance in range(chips):
         for across in range(2):
-            parts = []
-            for group in groups:
-                part = group[distance][0] if across == 0 else group[chips][distance]
-                parts.append(part.reshape(CHUNK * RECV_DEV, cols))
+            part = group[distance][0] if across == 0 else group[chips][distance]
             line = ids_ref[2 * distance + across]
             spread = jnp.dot(
-                jnp.concatenate(parts, 0),
+                part.reshape(CHUNK * RECV_DEV, cols),
                 table_ref[jnp.minimum(line, 1)],
                 preferred_element_type=F32,
             )
@@ -430,11 +427,9 @@
 
     angles = [[2.0 * math.pi * (r * q % owners) / owners for r in range(owners)] for q in range(owners)]
 
-    @pl.loop(0, STEPS * RECV_DEV // ROWS)
-    def _(chunk):
-        at = pl.multiple_of(chunk * ROWS, ROWS)
-        step = at // RECV_DEV
-        row = pl.multiple_of(at % RECV_DEV, ROWS)
+    def add_up(step, chunk):
+        row = pl.multiple_of(chunk * ROWS, ROWS)
+        at = pl.multiple_of(step * RECV_DEV + chunk * ROWS, ROWS)
         for lane in range(0, period, LANES):
             lanes = slice(lane, min(lane + LANES, period))
             real = [real_ref[r, pl.ds(at, ROWS), lanes] for r in range(owners)]
@@ -449,21 +444,38 @@
                     sums.append(weighted_sum(terms))
                 for value, place in ((sums[0] + sums[1], q), (sums[0] - sums[1], q + owners // 2)):
                     start = place * period + lane
-                    out_ref[step, pl.ds(row, ROWS), start : start + lanes.stop - lane] = (
+                    ready[step][pl.ds(row, ROWS), start : start + lanes.stop - lane] = (
                         value.astype(BF16)
                     )
 
-
-def inverse_of(ids, groups, table, turns):
+    copies = [
+        pltpu.make_async_copy(ready[step], out_ref.at[first + step], sems.at[step])
+        for step in range(CHUNK)
+    ]
+    for step in range(CHUNK):
+        pl.loop(0, RECV_DEV // ROWS)(functools.partial(add_up, step))
+        copies[step].start()
+    for copy in copies:
+        copy.wait()
+
+
+def inverse_of(ids, first, group, table, turns, before):
     owners, _, period = turns.shape
-    arrays = [array for group in groups for array in group]
-    rows = STEPS * RECV_DEV
-    return pl.pallas_call(
-        functools.partial(inverse_kernel, owners // 2),
-        in_specs=[smem()] + [vmem()] * (2 + len(arrays)),
-        out_specs=vmem(),
-        out_shape=jax.ShapeDtypeStruct((STEPS, RECV_DEV, owners * period), BF16),
-        scratch_shapes=[pltpu.VMEM((owners, rows, period), F32)] * 2,
+    rows, samples = CHUNK * RECV_DEV, owners * period
+    given, aliases = [*group], {}
+    specs = [smem()] + [vmem()] * (2 + len(group))
+    if before is not None:
+        aliases = {len(specs): 0}
+        given, specs = given + [before], specs + [hbm()]
+    return pl.pallas_call(
+        functools.partial(inverse_kernel, owners // 2, first),
+        in_specs=specs,
+        out_specs=hbm(),
+        out_shape=jax.ShapeDtypeStruct((STEPS, RECV_DEV, samples), BF16),
+        scratch_shapes=[pltpu.VMEM((owners, rows, period), F32)] * 2
+        + [pltpu.VMEM((RECV_DEV, samples), BF16)] * CHUNK
+        + [pltpu.SemaphoreType.DMA((CHUNK,))],
+        input_output_aliases=aliases,
         cost_estimate=pl.CostEstimate(
             flops=2 * rows * owners * table[0].size,
             bytes_accessed=2 * rows * owners * period,
@@ -471,7 +483,7 @@
         ),
         compiler_params=params(24),
         name="inverse_dft",
-    )(ids, table, turns, *arrays)
+    )(ids, table, turns, *given)
 
 
 def swap(array, distance):
@@ -523,13 +535,13 @@
     early = [0]
     late = [d for d in range(chips) if d not in early]
     partial = early_sums(early, main, border, masks, [spectra[d] for d in early])
-    groups = []
+    result = None
     for first in range(0, STEPS, CHUNK):
         given = (main, border, partial, masks, [spectra[d] for d in late])
         sums = send_blocks(late_sums(first, chips, late, *given))
         across = swap(jnp.stack([block[1] for block in sums]), 1)
-        groups.append(sums + [across])
-    return inverse_of(all_ids, groups, inverse, turns)
+        result = inverse_of(all_ids, first, sums + [across], inverse, turns, result)
+    return result
 
 
 def solution(mesh):

time: 52.6 us -> 52.4 us (level)
  waiting for transfers between devices: 8.96 us -> 7.55 us
  Pallas kernels: 18.8 us -> 20 us
    ppermute x20, waiting for transfers between devices: 8.95 us -> 7.55 us  [swap(): return lax.ppermute(array, 'line', [(i, i ^ distance) for i in devices])]
    pallas_call x1 -> x2, Pallas kernels: 2.89 us -> 4.05 us  [inverse_of(): pl.pallas_call(functools.partial(inverse_kernel, owners // 2, first), in_...]
  transfers between devices with their start and end apart: 21 -> 21, of which waited for: 6 -> 5; matrix products, arithmetic and copies ran while one was open for 1% -> 1% of each run, Pallas kernels for 26% -> 30%
where the time goes in v5:
time: 52.4 us; the launch traced here: 52.2 us
  starting transfers between devices  24.1 us (46%)
  Pallas kernels  20 us (38%)
  waiting for transfers between devices  7.55 us (14%)
    ppermute x20, starting transfers between devices, swap(): return lax.ppermute(array, 'line', [(i, i ^ distance) for i in devices])  20.6 us
    ppermute x20, waiting for transfers between devices, swap(): return lax.ppermute(array, 'line', [(i, i ^ distance) for i in devices])  7.55 us
    pallas_call x2, Pallas kernels, forward_of(): pl.pallas_call(functools.partial(forward_kernel, chips, count), out_shape...  4.57 us
    pallas_call x2, Pallas kernels, late_sums(): pl.pallas_call(functools.partial(late_kernel, first, chips, distances), o...  4.13 us
    pallas_call x2, Pallas kernels, inverse_of(): pl.pallas_call(functools.partial(inverse_kernel, owners // 2, first), in_...  4.05 us
    ppermute x1, starting transfers between devices, local(): border = lax.ppermute(edges, 'area', [(i, i + 1) for i in range(areas - 1)])  3.49 us
    pallas_call x1, Pallas kernels, near_of(): pl.pallas_call(functools.partial(first_kernel, chips), out_shape=[jax.Sha...  2.94 us
    pallas_call x1, Pallas kernels, masks_of(): pl.pallas_call(functools.partial(masks_kernel, rows), out_shape=[jax.Shap...  1.99 us
  transfers between devices with their start and end apart: 21, of which 5 were waited for; matrix products, arithmetic and copies ran while one was open for 1% of the time, Pallas kernels for 30%

profile of v5, /device:TPU:0, one launch (start us, length us, event | category | flops | bytes accessed | tf_op | source)
XLA Modules:
  0.0 52.2 jit_solution(2126685260038850076)
XLA Ops:
  0.6 2.9 %near_panel_dft.1 = (bf16[272,256]{1,0:T(8,128)(2,1)S(1)}, bf16[272,256]{1,0:T(8,128)(2,1)S(1)}, bf16[272,256]{1,0:T(8,128)(2,1)S(1)}, bf16[272,256]{1,0:T(8,128...) custom-call(s32[8]{0:T(128)S(1)} %stack.65.ids_ref, bf16[512,256]{1,0:T(8,128)(2,1)} %constant.22.clone.table_ref, ...), custom_call_target="tpu_custom_call" | custom-call | flops 268435456 | bytes 2097152 | tf_op jit(solution)/shard_map/near_panel_dft/pallas_call | solution.py:157
  3.6 3.0 %collective-permute-start.1 = (bf16[272,256]{1,0:T(8,128)(2,1)S(1)}, bf16[272,256]{1,0:T(8,128)(2,1)S(1)}, u32[]{:S(2)}, u32[]{:S(2)}) collective-permute-start(bf16[272,256]{1,0:T(8,128)(2,1)S(1)} %get-tuple-element.37), channel_id=1, source_target_pairs={{0,2},{1,3},{2,0},{3,1},{4,6},{5,7},{6,4},{7,5},{8,10},{9,11},{10,... | collective-permute-start | bytes 417800 | tf_op jit(solution)/shard_map/ppermute | solution.py:491
  6.5 1.5 %collective-permute-start.3 = (bf16[272,256]{1,0:T(8,128)(2,1)S(1)}, bf16[272,256]{1,0:T(8,128)(2,1)S(1)}, u32[]{:S(2)}, u32[]{:S(2)}) collective-permute-start(bf16[272,256]{1,0:T(8,128)(2,1)S(1)} %get-tuple-element.39), channel_id=1, source_target_pairs={{0,4},{1,5},{2,6},{3,7},{4,0},{5,1},{6,2},{7,3},{8,12},{9,13},{10,... | collective-permute-start | bytes 417800 | tf_op jit(solution)/shard_map/ppermute | solution.py:491
  8.1 1.8 %far_panel_dft.1 = (bf16[256,256]{1,0:T(8,128)(2,1)S(1)}, bf16[256,256]{1,0:T(8,128)(2,1)S(1)}, bf16[256,256]{1,0:T(8,128)(2,1)S(1)}, bf16[256,256]{1,0:T(8,128)(2,1)S(1)}) custom-call(s32[8]{0:T(128)S(1)} %stack.65.ids_ref, bf16[512,256]{1,0:T(8,128)(2,1)S(1)} %get-tuple-element.34.table_ref, f32[4,8,16,256]{3,2,1,0:T(8,128)S(1)} %get-tuple-element.35.wide, ...), custom_call_target="tpu_custom_call" | custom-call | flops 134217728 | bytes 2097152 | tf_op jit(solution)/shard_map/far_panel_dft/pallas_call | solution.py:191
  9.9 2.0 %collective-permute-start.2 = (bf16[256,256]{1,0:T(8,128)(2,1)S(1)}, bf16[256,256]{1,0:T(8,128)(2,1)S(1)}, u32[]{:S(2)}, u32[]{:S(2)}) collective-permute-start(bf16[256,256]{1,0:T(8,128)(2,1)S(1)} %get-tuple-element.38), channel_id=1, source_target_pairs={{0,2},{1,3},{2,0},{3,1},{4,6},{5,7},{6,4},{7,5},{8,10},{9,11},{10,... | collective-permute-start | bytes 393224 | tf_op jit(solution)/shard_map/ppermute | solution.py:491
  11.9 1.5 %collective-permute-start.4 = (bf16[256,256]{1,0:T(8,128)(2,1)S(1)}, bf16[256,256]{1,0:T(8,128)(2,1)S(1)}, u32[]{:S(2)}, u32[]{:S(2)}) collective-permute-start(bf16[256,256]{1,0:T(8,128)(2,1)S(1)} %get-tuple-element.40), channel_id=1, source_target_pairs={{0,4},{1,5},{2,6},{3,7},{4,0},{5,1},{6,2},{7,3},{8,12},{9,13},{10,... | collective-permute-start | bytes 393224 | tf_op jit(solution)/shard_map/ppermute | solution.py:491
  13.4 1.1 %collective-permute-start.6 = (bf16[256,256]{1,0:T(8,128)(2,1)S(1)}, bf16[256,256]{1,0:T(8,128)(2,1)S(1)}, u32[]{:S(2)}, u32[]{:S(2)}) collective-permute-start(bf16[256,256]{1,0:T(8,128)(2,1)S(1)} %get-tuple-element.42), channel_id=1, source_target_pairs={{0,6},{1,7},{2,4},{3,5},{4,2},{5,3},{6,0},{7,1},{8,14},{9,15},{10,... | collective-permute-start | bytes 393224 | tf_op jit(solution)/shard_map/ppermute | solution.py:491
  14.5 2.8 %trace_dft.1 = (bf16[512,256]{1,0:T(8,128)(2,1)S(1)}, bf16[512,256]{1,0:T(8,128)(2,1)S(1)}, bf16[512,256]{1,0:T(8,128)(2,1)S(1)}, bf16[512,256]{1,0:T(8,128)(2,1)S(1)}) custom-call(s32[8]{0:T(128)S(1)} %stack.65.ids_ref, bf16[512,256]{1,0:T(8,128)(2,1)S(1)} %get-tuple-element.34.table_ref, f32[4,8,16,256]{3,2,1,0:T(8,128)S(1)} %get-tuple-element.35.wide, ...), custom_call_target="tpu_custom_call" | custom-call | flops 268435456 | bytes 4194304 | tf_op jit(solution)/shard_map/trace_dft/pallas_call | solution.py:191
  18.3 1.5 %collective-permute-start.11 = (bf16[512,256]{1,0:T(8,128)(2,1)S(1)}, bf16[512,256]{1,0:T(8,128)(2,1)S(1)}, u32[]{:S(2)}, u32[]{:S(2)}) collective-permute-start(bf16[512,256]{1,0:T(8,128)(2,1)S(1)} %get-tuple-element.51), channel_id=1, source_target_pairs={{0,4},{1,5},{2,6},{3,7},{4,0},{5,1},{6,2},{7,3},{8,12},{9,13},{10,... | collective-permute-start | bytes 786440 | tf_op jit(solution)/shard_map/ppermute | solution.py:491
  22.0 3.5 %collective-permute-start.7 = (bf16[4,64,256]{2,1,0:T(8,128)(2,1)S(1)}, bf16[4,64,256]{2,1,0:T(8,128)(2,1)S(1)}, u32[]{:S(2)}, u32[]{:S(2)}) collective-permute-start(bf16[4,64,256]{2,1,0:T(8,128)(2,1)S(1)} %get-tuple-element.44), channel_id=1, source_target_pairs={{0,8},{8,16},{16,24},{1,9},{9,17},{17,25},{2,10},{10,18},{18,26},{... | collective-permute-start | bytes 393224 | tf_op jit(solution)/shard_map/ppermute | solution.py:532
  25.6 1.2 %collective-permute-done.8.refs_1_ = bf16[4,16,256]{2,1,0:T(8,128)(2,1)S(1)} collective-permute-done((bf16[4,16,256]{2,1,0:T(8,128)(2,1)S(1)}, bf16[4,16,256]{2,1,0:T(8,128)(2,1)S(1)}, u32[]{:S(2)}, u32[]{:S(2)}) %collective-permute-start.8) | collective-permute-done | bytes 32800 | tf_op jit(solution)/shard_map/ppermute | solution.py:491
  26.8 2.0 %masks.1 = (bf16[2048,320]{1,0:T(8,128)(2,1)S(1)}, bf16[512,2048]{1,0:T(8,128)(2,1)S(1)}, f32[256,8]{1,0:T(8,128)S(1)}) custom-call(s32[8]{0:T(128)S(1)} %stack.65.ids_ref, bf16[4,16,256]{2,1,0:T(8,128)(2,1)S(1)} %get-tuple-element.45.refs_0_, bf16[4,16,256]{2,1,0:T(8,128)(2,1)S(1)} %collective-permute-done.8.refs_1_), custom_call_target="tpu_custom_call" | custom-call | flops 10223616 | bytes 3407872 | tf_op jit(solution)/shard_map/masks/pallas_call | solution.py:241
  28.8 1.5 %early_sums.1.partial_ref = f32[4,512,256]{2,1,0:T(8,128)S(1)} custom-call(bf16[4,256,256]{2,1,0:T(8,128)(2,1)S(1)} %get-tuple-element.43.main_ref, bf16[4,64,256]{2,1,0:T(8,128)(2,1)S(1)} %collective-permute-done.7.border_ref, bf16[2048,320]{1,0:T(8,128)(2,1)S(1)} %get-tuple-element.46.refs_0_, bf16[512,2048]{1,0:T(8,128)(2,1)S(1)} %get-tuple-element.47.refs_1_, ...), custom_call_target="tpu_custom_call" | custom-call | flops 872415232 | bytes 262144 | tf_op jit(solution)/shard_map/early_sums/pallas_call | solution.py:339
  30.3 1.4 %collective-permute-done.11.refs_4_ = bf16[512,256]{1,0:T(8,128)(2,1)S(1)} collective-permute-done((bf16[512,256]{1,0:T(8,128)(2,1)S(1)}, bf16[512,256]{1,0:T(8,128)(2,1)S(1)}, u32[]{:S(2)}, u32[]{:S(2)}) %collective-permute-start.11) | collective-permute-done | bytes 262176 | tf_op jit(solution)/shard_map/ppermute | solution.py:491
  31.8 2.1 %receiver_sums.3 = (bf16[2,2,64,256]{3,2,1,0:T(8,128)(2,1)S(1)}, bf16[2,2,64,256]{3,2,1,0:T(8,128)(2,1)S(1)}, bf16[2,2,64,256]{3,2,1,0:T(8,128)(2,1)S(1)}, bf16[2,2,64,256]{3,2,1,0:T(8,128)(2,1)S(1)}) custom-call(bf16[4,256,256]{2,1,0:T(8,128)(2,1)S(1)} %get-tuple-element.43.main_ref, bf16[4,64,256]{2,1,0:T(8,128)(2,1)S(1)} %collective-permute-done.7.border_ref, ...), custom_call_target="tpu_custom_call" | custom-call | flops 1308622848 | bytes 786432 | tf_op jit(solution)/shard_map/receiver_sums/pallas_call | solution.py:370
  33.8 1.4 %collective-permute-start.17 = (bf16[2,2,64,256]{3,2,1,0:T(8,128)(2,1)S(1)}, bf16[2,2,64,256]{3,2,1,0:T(8,128)(2,1)S(1)}, u32[]{:S(2)}, u32[]{:S(2)}) collective-permute-start(bf16[2,2,64,256]{3,2,1,0:T(8,128)(2,1)S(1)} %get-tuple-element.58), channel_id=1, source_target_pairs={{0,2},{1,3},{2,0},{3,1},{4,6},{5,7},{6,4},{7,5},{8,10},{9,11},{10,... | collective-permute-start | bytes 393224 | tf_op jit(solution)/shard_map/ppermute | solution.py:491
  35.9 1.4 %collective-permute-start.19 = (bf16[2,2,64,256]{3,2,1,0:T(8,128)(2,1)S(1)}, bf16[2,2,64,256]{3,2,1,0:T(8,128)(2,1)S(1)}, u32[]{:S(2)}, u32[]{:S(2)}) collective-permute-start(bf16[2,2,64,256]{3,2,1,0:T(8,128)(2,1)S(1)} %get-tuple-element.60), channel_id=1, source_target_pairs={{0,6},{1,7},{2,4},{3,5},{4,2},{5,3},{6,0},{7,1},{8,14},{9,15},{10,... | collective-permute-start | bytes 393224 | tf_op jit(solution)/shard_map/ppermute | solution.py:491
  37.4 2.1 %receiver_sums.2 = (bf16[2,2,64,256]{3,2,1,0:T(8,128)(2,1)S(1)}, bf16[2,2,64,256]{3,2,1,0:T(8,128)(2,1)S(1)}, bf16[2,2,64,256]{3,2,1,0:T(8,128)(2,1)S(1)}, bf16[2,2,64,256]{3,2,1,0:T(8,128)(2,1)S(1)}) custom-call(bf16[4,256,256]{2,1,0:T(8,128)(2,1)S(1)} %get-tuple-element.43.main_ref, bf16[4,64,256]{2,1,0:T(8,128)(2,1)S(1)} %collective-permute-done.7.border_ref, ...), custom_call_target="tpu_custom_call" | custom-call | flops 1308622848 | bytes 786432 | tf_op jit(solution)/shard_map/receiver_sums/pallas_call | solution.py:370
  39.5 1.4 %collective-permute-start.13 = (bf16[2,2,64,256]{3,2,1,0:T(8,128)(2,1)S(1)}, bf16[2,2,64,256]{3,2,1,0:T(8,128)(2,1)S(1)}, u32[]{:S(2)}, u32[]{:S(2)}) collective-permute-start(bf16[2,2,64,256]{3,2,1,0:T(8,128)(2,1)S(1)} %get-tuple-element.54), channel_id=1, source_target_pairs={{0,2},{1,3},{2,0},{3,1},{4,6},{5,7},{6,4},{7,5},{8,10},{9,11},{10,... | collective-permute-start | bytes 393224 | tf_op jit(solution)/shard_map/ppermute | solution.py:491
  41.6 1.4 %collective-permute-start.15 = (bf16[2,2,64,256]{3,2,1,0:T(8,128)(2,1)S(1)}, bf16[2,2,64,256]{3,2,1,0:T(8,128)(2,1)S(1)}, u32[]{:S(2)}, u32[]{:S(2)}) collective-permute-start(bf16[2,2,64,256]{3,2,1,0:T(8,128)(2,1)S(1)} %get-tuple-element.56), channel_id=1, source_target_pairs={{0,6},{1,7},{2,4},{3,5},{4,2},{5,3},{6,0},{7,1},{8,14},{9,15},{10,... | collective-permute-start | bytes 393224 | tf_op jit(solution)/shard_map/ppermute | solution.py:491
  43.2 2.6 %collective-permute-done.13.refs_1_ = bf16[2,2,64,256]{3,2,1,0:T(8,128)(2,1)S(1)} collective-permute-done((bf16[2,2,64,256]{3,2,1,0:T(8,128)(2,1)S(1)}, bf16[2,2,64,256]{3,2,1,0:T(8,128)(2,1)S(1)}, u32[]{:S(2)}, u32[]{:S(2)}) %collective-permute-start.13) | collective-permute-done | bytes 131104 | tf_op jit(solution)/shard_map/ppermute | solution.py:491
  45.9 2.0 %collective-permute-done.14.refs_2_ = bf16[2,2,64,256]{3,2,1,0:T(8,128)(2,1)S(1)} collective-permute-done((bf16[2,2,64,256]{3,2,1,0:T(8,128)(2,1)S(1)}, bf16[2,2,64,256]{3,2,1,0:T(8,128)(2,1)S(1)}, u32[]{:S(2)}, u32[]{:S(2)}) %collective-permute-start.14) | collective-permute-done | bytes 131104 | tf_op jit(solution)/shard_map/ppermute | solution.py:491
  48.1 2.0 %inverse_dft.2.refs_5_ = bf16[4,64,2048]{2,1,0:T(8,128)(2,1)} custom-call(s32[8]{0:T(128)S(1)} %stack.60.ids_ref, bf16[2,256,512]{2,1,0:T(8,128)(2,1)S(1)} %copy-done, f32[8,2,256]{2,1,0:T(2,128)S(1)} %copy-done.2, bf16[2,2,64,256]{3,2,1,0:T(8,128)(2,1)S(1)} %get-tuple-element.57.refs_0_, bf16[2,2,64,256]{3,2,1,0:T(8,128)(2,1)S(1)} %collective-permute-done.17.refs_1_, ...), custom_call_target="tpu_custom_call" | custom-call | flops 268435456 | bytes 524288 | tf_op jit(solution)/shard_map/inverse_dft/pallas_call | solution.py:470
  50.2 2.0 %inverse_dft.3 = bf16[4,64,2048]{2,1,0:T(8,128)(2,1)} custom-call(s32[8]{0:T(128)S(1)} %stack.60.ids_ref, bf16[2,256,512]{2,1,0:T(8,128)(2,1)S(1)} %copy-done, f32[8,2,256]{2,1,0:T(2,128)S(1)} %copy-done.2, bf16[2,2,64,256]{3,2,1,0:T(8,128)(2,1)S(1)} %get-tuple-element.53.refs_0_, ...), custom_call_target="tpu_custom_call", output_to_operand_aliasing={{}: (8, {})} | custom-call | flops 268435456 | bytes 524288 | tf_op jit(solution)/shard_map/inverse_dft/pallas_call | solution.py:470
  (48 shorter events, 5.7 us)
Async XLA Ops:
  0.0 14.5 %copy-start.1 = (bf16[256,2048]{1,0:T(8,128)(2,1)S(1)}, bf16[256,2048]{1,0:T(8,128)(2,1)}, u32[]{:S(2)}) copy-start(bf16[256,2048]{1,0:T(8,128)(2,1)} %refs_0_.3) | copy-start | bytes 3145732
  0.0 8.1 %collective-permute-start = (bf16[256,2048]{1,0:T(8,128)(2,1)}, bf16[256,2048]{1,0:T(8,128)(2,1)S(1)}, u32[]{:S(2)}, u32[]{:S(2)}) collective-permute-start(bf16[256,2048]{1,0:T(8,128)(2,1)} %bitcast.14), channel_id=1, source_target_pairs={{0,1},{1,0},{2,3},{3,2},{4,5},{5,4},{6,7},{7,6},{8,9},{9,8},{10,11... | collective-permute-start | bytes 3145736 | tf_op jit(solution)/shard_map/ppermute | solution.py:491
  0.5 12.9 %collective-permute-start.9 = (bf16[256,2048]{1,0:T(8,128)(2,1)}, bf16[256,2048]{1,0:T(8,128)(2,1)S(1)}, u32[]{:S(2)}, u32[]{:S(2)}) collective-permute-start(bf16[256,2048]{1,0:T(8,128)(2,1)} %refs_0_.3), channel_id=1, source_target_pairs={{0,1},{1,0},{2,3},{3,2},{4,5},{5,4},{6,7},{7,6},{8,9},{9,8},{10,11... | collective-permute-start | bytes 3145736 | tf_op jit(solution)/shard_map/ppermute | solution.py:491
  3.6 8.3 %collective-permute-start.1 = (bf16[272,256]{1,0:T(8,128)(2,1)S(1)}, bf16[272,256]{1,0:T(8,128)(2,1)S(1)}, u32[]{:S(2)}, u32[]{:S(2)}) collective-permute-start(bf16[272,256]{1,0:T(8,128)(2,1)S(1)} %get-tuple-element.37), channel_id=1, source_target_pairs={{0,2},{1,3},{2,0},{3,1},{4,6},{5,7},{6,4},{7,5},{8,10},{9,11},{10,... | collective-permute-start | bytes 417800 | tf_op jit(solution)/shard_map/ppermute | solution.py:491
  6.5 10.8 %collective-permute-start.3 = (bf16[272,256]{1,0:T(8,128)(2,1)S(1)}, bf16[272,256]{1,0:T(8,128)(2,1)S(1)}, u32[]{:S(2)}, u32[]{:S(2)}) collective-permute-start(bf16[272,256]{1,0:T(8,128)(2,1)S(1)} %get-tuple-element.39), channel_id=1, source_target_pairs={{0,4},{1,5},{2,6},{3,7},{4,0},{5,1},{6,2},{7,3},{8,12},{9,13},{10,... | collective-permute-start | bytes 417800 | tf_op jit(solution)/shard_map/ppermute | solution.py:491
  8.1 10.2 %collective-permute-start.5 = (bf16[272,256]{1,0:T(8,128)(2,1)S(1)}, bf16[272,256]{1,0:T(8,128)(2,1)S(1)}, u32[]{:S(2)}, u32[]{:S(2)}) collective-permute-start(bf16[272,256]{1,0:T(8,128)(2,1)S(1)} %get-tuple-element.41), channel_id=1, source_target_pairs={{0,6},{1,7},{2,4},{3,5},{4,2},{5,3},{6,0},{7,1},{8,14},{9,15},{10,... | collective-permute-start | bytes 417800 | tf_op jit(solution)/shard_map/ppermute | solution.py:491
  8.1 13.2 %copy-start.3 = (s32[4,4]{1,0:T(4,128)S(1)}, s32[4,4]{1,0:T(4,128)}, u32[]{:S(2)}) copy-start(s32[4,4]{1,0:T(4,128)} %plan_ref.1) | copy-start | bytes 196
  9.9 9.9 %collective-permute-start.2 = (bf16[256,256]{1,0:T(8,128)(2,1)S(1)}, bf16[256,256]{1,0:T(8,128)(2,1)S(1)}, u32[]{:S(2)}, u32[]{:S(2)}) collective-permute-start(bf16[256,256]{1,0:T(8,128)(2,1)S(1)} %get-tuple-element.38), channel_id=1, source_target_pairs={{0,2},{1,3},{2,0},{3,1},{4,6},{5,7},{6,4},{7,5},{8,10},{9,11},{10,... | collective-permute-start | bytes 393224 | tf_op jit(solution)/shard_map/ppermute | solution.py:491
  11.9 9.1 %collective-permute-start.4 = (bf16[256,256]{1,0:T(8,128)(2,1)S(1)}, bf16[256,256]{1,0:T(8,128)(2,1)S(1)}, u32[]{:S(2)}, u32[]{:S(2)}) collective-permute-start(bf16[256,256]{1,0:T(8,128)(2,1)S(1)} %get-tuple-element.40), channel_id=1, source_target_pairs={{0,4},{1,5},{2,6},{3,7},{4,0},{5,1},{6,2},{7,3},{8,12},{9,13},{10,... | collective-permute-start | bytes 393224 | tf_op jit(solution)/shard_map/ppermute | solution.py:491
  13.4 7.8 %collective-permute-start.6 = (bf16[256,256]{1,0:T(8,128)(2,1)S(1)}, bf16[256,256]{1,0:T(8,128)(2,1)S(1)}, u32[]{:S(2)}, u32[]{:S(2)}) collective-permute-start(bf16[256,256]{1,0:T(8,128)(2,1)S(1)} %get-tuple-element.42), channel_id=1, source_target_pairs={{0,6},{1,7},{2,4},{3,5},{4,2},{5,3},{6,0},{7,1},{8,14},{9,15},{10,... | collective-permute-start | bytes 393224 | tf_op jit(solution)/shard_map/ppermute | solution.py:491
  17.4 13.0 %collective-permute-start.10 = (bf16[512,256]{1,0:T(8,128)(2,1)S(1)}, bf16[512,256]{1,0:T(8,128)(2,1)S(1)}, u32[]{:S(2)}, u32[]{:S(2)}) collective-permute-start(bf16[512,256]{1,0:T(8,128)(2,1)S(1)} %get-tuple-element.50), channel_id=1, source_target_pairs={{0,2},{1,3},{2,0},{3,1},{4,6},{5,7},{6,4},{7,5},{8,10},{9,11},{10,... | collective-permute-start | bytes 786440 | tf_op jit(solution)/shard_map/ppermute | solution.py:491
  18.3 13.5 %collective-permute-start.11 = (bf16[512,256]{1,0:T(8,128)(2,1)S(1)}, bf16[512,256]{1,0:T(8,128)(2,1)S(1)}, u32[]{:S(2)}, u32[]{:S(2)}) collective-permute-start(bf16[512,256]{1,0:T(8,128)(2,1)S(1)} %get-tuple-element.51), channel_id=1, source_target_pairs={{0,4},{1,5},{2,6},{3,7},{4,0},{5,1},{6,2},{7,3},{8,12},{9,13},{10,... | collective-permute-start | bytes 786440 | tf_op jit(solution)/shard_map/ppermute | solution.py:491
  19.8 12.0 %collective-permute-start.12 = (bf16[512,256]{1,0:T(8,128)(2,1)S(1)}, bf16[512,256]{1,0:T(8,128)(2,1)S(1)}, u32[]{:S(2)}, u32[]{:S(2)}) collective-permute-start(bf16[512,256]{1,0:T(8,128)(2,1)S(1)} %get-tuple-element.52), channel_id=1, source_target_pairs={{0,6},{1,7},{2,4},{3,5},{4,2},{5,3},{6,0},{7,1},{8,14},{9,15},{10,... | collective-permute-start | bytes 786440 | tf_op jit(solution)/shard_map/ppermute | solution.py:491
  22.0 6.8 %collective-permute-start.7 = (bf16[4,64,256]{2,1,0:T(8,128)(2,1)S(1)}, bf16[4,64,256]{2,1,0:T(8,128)(2,1)S(1)}, u32[]{:S(2)}, u32[]{:S(2)}) collective-permute-start(bf16[4,64,256]{2,1,0:T(8,128)(2,1)S(1)} %get-tuple-element.44), channel_id=1, source_target_pairs={{0,8},{8,16},{16,24},{1,9},{9,17},{17,25},{2,10},{10,18},{18,26},{... | collective-permute-start | bytes 393224 | tf_op jit(solution)/shard_map/ppermute | solution.py:532
  25.5 1.3 %collective-permute-start.8 = (bf16[4,16,256]{2,1,0:T(8,128)(2,1)S(1)}, bf16[4,16,256]{2,1,0:T(8,128)(2,1)S(1)}, u32[]{:S(2)}, u32[]{:S(2)}) collective-permute-start(bf16[4,16,256]{2,1,0:T(8,128)(2,1)S(1)} %get-tuple-element.45.refs_0_), channel_id=1, source_target_pairs={{0,1},{1,0},{2,3},{3,2},{4,5},{5,4},{6,7},{7,6},{8,9},{9,8},{10,11... | collective-permute-start | bytes 98312 | tf_op jit(solution)/shard_map/ppermute | solution.py:491
  33.8 7.8 %collective-permute-start.17 = (bf16[2,2,64,256]{3,2,1,0:T(8,128)(2,1)S(1)}, bf16[2,2,64,256]{3,2,1,0:T(8,128)(2,1)S(1)}, u32[]{:S(2)}, u32[]{:S(2)}) collective-permute-start(bf16[2,2,64,256]{3,2,1,0:T(8,128)(2,1)S(1)} %get-tuple-element.58), channel_id=1, source_target_pairs={{0,2},{1,3},{2,0},{3,1},{4,6},{5,7},{6,4},{7,5},{8,10},{9,11},{10,... | collective-permute-start | bytes 393224 | tf_op jit(solution)/shard_map/ppermute | solution.py:491
  35.2 7.9 %collective-permute-start.18 = (bf16[2,2,64,256]{3,2,1,0:T(8,128)(2,1)S(1)}, bf16[2,2,64,256]{3,2,1,0:T(8,128)(2,1)S(1)}, u32[]{:S(2)}, u32[]{:S(2)}) collective-permute-start(bf16[2,2,64,256]{3,2,1,0:T(8,128)(2,1)S(1)} %get-tuple-element.59), channel_id=1, source_target_pairs={{0,4},{1,5},{2,6},{3,7},{4,0},{5,1},{6,2},{7,3},{8,12},{9,13},{10,... | collective-permute-start | bytes 393224 | tf_op jit(solution)/shard_map/ppermute | solution.py:491
  35.9 7.1 %collective-permute-start.19 = (bf16[2,2,64,256]{3,2,1,0:T(8,128)(2,1)S(1)}, bf16[2,2,64,256]{3,2,1,0:T(8,128)(2,1)S(1)}, u32[]{:S(2)}, u32[]{:S(2)}) collective-permute-start(bf16[2,2,64,256]{3,2,1,0:T(8,128)(2,1)S(1)} %get-tuple-element.60), channel_id=1, source_target_pairs={{0,6},{1,7},{2,4},{3,5},{4,2},{5,3},{6,0},{7,1},{8,14},{9,15},{10,... | collective-permute-start | bytes 393224 | tf_op jit(solution)/shard_map/ppermute | solution.py:491
  39.4 8.7 %copy-start = (bf16[2,256,512]{2,1,0:T(8,128)(2,1)S(1)}, bf16[2,256,512]{2,1,0:T(8,128)(2,1)}, u32[]{:S(2)}) copy-start(bf16[2,256,512]{2,1,0:T(8,128)(2,1)} %constant.24.clone.table_ref) | copy-start | bytes 1572868
  39.5 6.4 %collective-permute-start.13 = (bf16[2,2,64,256]{3,2,1,0:T(8,128)(2,1)S(1)}, bf16[2,2,64,256]{3,2,1,0:T(8,128)(2,1)S(1)}, u32[]{:S(2)}, u32[]{:S(2)}) collective-permute-start(bf16[2,2,64,256]{3,2,1,0:T(8,128)(2,1)S(1)} %get-tuple-element.54), channel_id=1, source_target_pairs={{0,2},{1,3},{2,0},{3,1},{4,6},{5,7},{6,4},{7,5},{8,10},{9,11},{10,... | collective-permute-start | bytes 393224 | tf_op jit(solution)/shard_map/ppermute | solution.py:491
  40.9 7.0 %collective-permute-start.14 = (bf16[2,2,64,256]{3,2,1,0:T(8,128)(2,1)S(1)}, bf16[2,2,64,256]{3,2,1,0:T(8,128)(2,1)S(1)}, u32[]{:S(2)}, u32[]{:S(2)}) collective-permute-start(bf16[2,2,64,256]{3,2,1,0:T(8,128)(2,1)S(1)} %get-tuple-element.55), channel_id=1, source_target_pairs={{0,4},{1,5},{2,6},{3,7},{4,0},{5,1},{6,2},{7,3},{8,12},{9,13},{10,... | collective-permute-start | bytes 393224 | tf_op jit(solution)/shard_map/ppermute | solution.py:491
  41.6 6.3 %collective-permute-start.15 = (bf16[2,2,64,256]{3,2,1,0:T(8,128)(2,1)S(1)}, bf16[2,2,64,256]{3,2,1,0:T(8,128)(2,1)S(1)}, u32[]{:S(2)}, u32[]{:S(2)}) collective-permute-start(bf16[2,2,64,256]{3,2,1,0:T(8,128)(2,1)S(1)} %get-tuple-element.56), channel_id=1, source_target_pairs={{0,6},{1,7},{2,4},{3,5},{4,2},{5,3},{6,0},{7,1},{8,14},{9,15},{10,... | collective-permute-start | bytes 393224 | tf_op jit(solution)/shard_map/ppermute | solution.py:491
  43.2 5.0 %collective-permute-start.20 = (bf16[4,2,64,256]{3,2,1,0:T(8,128)(2,1)S(1)}, bf16[4,2,64,256]{3,2,1,0:T(8,128)(2,1)S(1)}, u32[]{:S(2)}, u32[]{:S(2)}) collective-permute-start(bf16[4,2,64,256]{3,2,1,0:T(8,128)(2,1)S(1)} %pad_maximum_fusion.1), channel_id=1, source_target_pairs={{0,1},{1,0},{2,3},{3,2},{4,5},{5,4},{6,7},{7,6},{8,9},{9,8},{10,11... | collective-permute-start | bytes 786440 | tf_op jit(solution)/shard_map/ppermute | solution.py:491
  47.9 2.2 %collective-permute-start.16 = (bf16[4,2,64,256]{3,2,1,0:T(8,128)(2,1)S(1)}, bf16[4,2,64,256]{3,2,1,0:T(8,128)(2,1)S(1)}, u32[]{:S(2)}, u32[]{:S(2)}) collective-permute-start(bf16[4,2,64,256]{3,2,1,0:T(8,128)(2,1)S(1)} %pad_maximum_fusion), channel_id=1, source_target_pairs={{0,1},{1,0},{2,3},{3,2},{4,5},{5,4},{6,7},{7,6},{8,9},{9,8},{10,11... | collective-permute-start | bytes 786440 | tf_op jit(solution)/shard_map/ppermute | solution.py:491
  (1 other events, 8.7 us)

commit v6 on v5

--- a/solution.py
+++ b/solution.py
@@ -92,7 +92,7 @@
     half = owners // 2
     sign = ids_ref[chips].astype(F32)
 
-    @pl.loop(0, count // ROWS)
+    @pl.loop(0, count // ROWS, unroll=8)
     def _(chunk):
         row = pl.multiple_of(base + chunk * ROWS, ROWS)
         to = pl.multiple_of(at + chunk * ROWS, ROWS)
@@ -453,7 +453,7 @@
         for step in range(CHUNK)
     ]
     for step in range(CHUNK):
-        pl.loop(0, RECV_DEV // ROWS)(functools.partial(add_up, step))
+        pl.loop(0, RECV_DEV // ROWS, unroll=4)(functools.partial(add_up, step))
         copies[step].start()
     for copy in copies:
         copy.wait()

time: 52.4 us -> 52.5 us (level)
  no operation moved by 1% of the time
where the time goes in v6:
time: 52.5 us; the launch traced here: 52.3 us
  starting transfers between devices  24.3 us (46%)
  Pallas kernels  19.7 us (38%)
  waiting for transfers between devices  7.58 us (14%)
    ppermute x20, starting transfers between devices, swap(): return lax.ppermute(array, 'line', [(i, i ^ distance) for i in devices])  20.6 us
    ppermute x20, waiting for transfers between devices, swap(): return lax.ppermute(array, 'line', [(i, i ^ distance) for i in devices])  7.57 us
    pallas_call x2, Pallas kernels, forward_of(): pl.pallas_call(functools.partial(forward_kernel, chips, count), out_shape...  4.45 us
    pallas_call x2, Pallas kernels, late_sums(): pl.pallas_call(functools.partial(late_kernel, first, chips, distances), o...  4.13 us
    pallas_call x2, Pallas kernels, inverse_of(): pl.pallas_call(functools.partial(inverse_kernel, owners // 2, first), in_...  3.92 us
    ppermute x1, starting transfers between devices, local(): border = lax.ppermute(edges, 'area', [(i, i + 1) for i in range(areas - 1)])  3.67 us
    pallas_call x1, Pallas kernels, near_of(): pl.pallas_call(functools.partial(first_kernel, chips), out_shape=[jax.Sha...  2.89 us
    pallas_call x1, Pallas kernels, masks_of(): pl.pallas_call(functools.partial(masks_kernel, rows), out_shape=[jax.Shap...  1.99 us
  transfers between devices with their start and end apart: 21, of which 5 were waited for; matrix products, arithmetic and copies ran while one was open for 1% of the time, Pallas kernels for 30%

profile of v6, /device:TPU:0, one launch (start us, length us, event | category | flops | bytes accessed | tf_op | source)
XLA Modules:
  0.0 52.3 jit_solution(17433663208371594921)
XLA Ops:
  0.6 2.9 %near_panel_dft.1 = (bf16[272,256]{1,0:T(8,128)(2,1)S(1)}, bf16[272,256]{1,0:T(8,128)(2,1)S(1)}, bf16[272,256]{1,0:T(8,128)(2,1)S(1)}, bf16[272,256]{1,0:T(8,128...) custom-call(s32[8]{0:T(128)S(1)} %stack.65.ids_ref, bf16[512,256]{1,0:T(8,128)(2,1)} %constant.22.clone.table_ref, ...), custom_call_target="tpu_custom_call" | custom-call | flops 268435456 | bytes 2097152 | tf_op jit(solution)/shard_map/near_panel_dft/pallas_call | solution.py:157
  3.5 3.0 %collective-permute-start.1 = (bf16[272,256]{1,0:T(8,128)(2,1)S(1)}, bf16[272,256]{1,0:T(8,128)(2,1)S(1)}, u32[]{:S(2)}, u32[]{:S(2)}) collective-permute-start(bf16[272,256]{1,0:T(8,128)(2,1)S(1)} %get-tuple-element.37), channel_id=1, source_target_pairs={{0,2},{1,3},{2,0},{3,1},{4,6},{5,7},{6,4},{7,5},{8,10},{9,11},{10,... | collective-permute-start | bytes 417800 | tf_op jit(solution)/shard_map/ppermute | solution.py:491
  6.5 1.5 %collective-permute-start.3 = (bf16[272,256]{1,0:T(8,128)(2,1)S(1)}, bf16[272,256]{1,0:T(8,128)(2,1)S(1)}, u32[]{:S(2)}, u32[]{:S(2)}) collective-permute-start(bf16[272,256]{1,0:T(8,128)(2,1)S(1)} %get-tuple-element.39), channel_id=1, source_target_pairs={{0,4},{1,5},{2,6},{3,7},{4,0},{5,1},{6,2},{7,3},{8,12},{9,13},{10,... | collective-permute-start | bytes 417800 | tf_op jit(solution)/shard_map/ppermute | solution.py:491
  8.1 1.7 %far_panel_dft.1 = (bf16[256,256]{1,0:T(8,128)(2,1)S(1)}, bf16[256,256]{1,0:T(8,128)(2,1)S(1)}, bf16[256,256]{1,0:T(8,128)(2,1)S(1)}, bf16[256,256]{1,0:T(8,128)(2,1)S(1)}) custom-call(s32[8]{0:T(128)S(1)} %stack.65.ids_ref, bf16[512,256]{1,0:T(8,128)(2,1)S(1)} %get-tuple-element.34.table_ref, f32[4,8,16,256]{3,2,1,0:T(8,128)S(1)} %get-tuple-element.35.wide, ...), custom_call_target="tpu_custom_call" | custom-call | flops 134217728 | bytes 2097152 | tf_op jit(solution)/shard_map/far_panel_dft/pallas_call | solution.py:191
  9.8 2.0 %collective-permute-start.2 = (bf16[256,256]{1,0:T(8,128)(2,1)S(1)}, bf16[256,256]{1,0:T(8,128)(2,1)S(1)}, u32[]{:S(2)}, u32[]{:S(2)}) collective-permute-start(bf16[256,256]{1,0:T(8,128)(2,1)S(1)} %get-tuple-element.38), channel_id=1, source_target_pairs={{0,2},{1,3},{2,0},{3,1},{4,6},{5,7},{6,4},{7,5},{8,10},{9,11},{10,... | collective-permute-start | bytes 393224 | tf_op jit(solution)/shard_map/ppermute | solution.py:491
  11.8 1.5 %collective-permute-start.4 = (bf16[256,256]{1,0:T(8,128)(2,1)S(1)}, bf16[256,256]{1,0:T(8,128)(2,1)S(1)}, u32[]{:S(2)}, u32[]{:S(2)}) collective-permute-start(bf16[256,256]{1,0:T(8,128)(2,1)S(1)} %get-tuple-element.40), channel_id=1, source_target_pairs={{0,4},{1,5},{2,6},{3,7},{4,0},{5,1},{6,2},{7,3},{8,12},{9,13},{10,... | collective-permute-start | bytes 393224 | tf_op jit(solution)/shard_map/ppermute | solution.py:491
  13.3 1.2 %collective-permute-start.6 = (bf16[256,256]{1,0:T(8,128)(2,1)S(1)}, bf16[256,256]{1,0:T(8,128)(2,1)S(1)}, u32[]{:S(2)}, u32[]{:S(2)}) collective-permute-start(bf16[256,256]{1,0:T(8,128)(2,1)S(1)} %get-tuple-element.42), channel_id=1, source_target_pairs={{0,6},{1,7},{2,4},{3,5},{4,2},{5,3},{6,0},{7,1},{8,14},{9,15},{10,... | collective-permute-start | bytes 393224 | tf_op jit(solution)/shard_map/ppermute | solution.py:491
  14.5 2.7 %trace_dft.1 = (bf16[512,256]{1,0:T(8,128)(2,1)S(1)}, bf16[512,256]{1,0:T(8,128)(2,1)S(1)}, bf16[512,256]{1,0:T(8,128)(2,1)S(1)}, bf16[512,256]{1,0:T(8,128)(2,1)S(1)}) custom-call(s32[8]{0:T(128)S(1)} %stack.65.ids_ref, bf16[512,256]{1,0:T(8,128)(2,1)S(1)} %get-tuple-element.34.table_ref, f32[4,8,16,256]{3,2,1,0:T(8,128)S(1)} %get-tuple-element.35.wide, ...), custom_call_target="tpu_custom_call" | custom-call | flops 268435456 | bytes 4194304 | tf_op jit(solution)/shard_map/trace_dft/pallas_call | solution.py:191
  18.1 1.5 %collective-permute-start.11 = (bf16[512,256]{1,0:T(8,128)(2,1)S(1)}, bf16[512,256]{1,0:T(8,128)(2,1)S(1)}, u32[]{:S(2)}, u32[]{:S(2)}) collective-permute-start(bf16[512,256]{1,0:T(8,128)(2,1)S(1)} %get-tuple-element.51), channel_id=1, source_target_pairs={{0,4},{1,5},{2,6},{3,7},{4,0},{5,1},{6,2},{7,3},{8,12},{9,13},{10,... | collective-permute-start | bytes 786440 | tf_op jit(solution)/shard_map/ppermute | solution.py:491
  22.0 3.7 %collective-permute-start.7 = (bf16[4,64,256]{2,1,0:T(8,128)(2,1)S(1)}, bf16[4,64,256]{2,1,0:T(8,128)(2,1)S(1)}, u32[]{:S(2)}, u32[]{:S(2)}) collective-permute-start(bf16[4,64,256]{2,1,0:T(8,128)(2,1)S(1)} %get-tuple-element.44), channel_id=1, source_target_pairs={{0,8},{8,16},{16,24},{1,9},{9,17},{17,25},{2,10},{10,18},{18,26},{... | collective-permute-start | bytes 393224 | tf_op jit(solution)/shard_map/ppermute | solution.py:532
  25.8 1.2 %collective-permute-done.8.refs_1_ = bf16[4,16,256]{2,1,0:T(8,128)(2,1)S(1)} collective-permute-done((bf16[4,16,256]{2,1,0:T(8,128)(2,1)S(1)}, bf16[4,16,256]{2,1,0:T(8,128)(2,1)S(1)}, u32[]{:S(2)}, u32[]{:S(2)}) %collective-permute-start.8) | collective-permute-done | bytes 32800 | tf_op jit(solution)/shard_map/ppermute | solution.py:491
  27.0 2.0 %masks.1 = (bf16[2048,320]{1,0:T(8,128)(2,1)S(1)}, bf16[512,2048]{1,0:T(8,128)(2,1)S(1)}, f32[256,8]{1,0:T(8,128)S(1)}) custom-call(s32[8]{0:T(128)S(1)} %stack.65.ids_ref, bf16[4,16,256]{2,1,0:T(8,128)(2,1)S(1)} %get-tuple-element.45.refs_0_, bf16[4,16,256]{2,1,0:T(8,128)(2,1)S(1)} %collective-permute-done.8.refs_1_), custom_call_target="tpu_custom_call" | custom-call | flops 10223616 | bytes 3407872 | tf_op jit(solution)/shard_map/masks/pallas_call | solution.py:241
  29.0 1.5 %early_sums.1.partial_ref = f32[4,512,256]{2,1,0:T(8,128)S(1)} custom-call(bf16[4,256,256]{2,1,0:T(8,128)(2,1)S(1)} %get-tuple-element.43.main_ref, bf16[4,64,256]{2,1,0:T(8,128)(2,1)S(1)} %collective-permute-done.7.border_ref, bf16[2048,320]{1,0:T(8,128)(2,1)S(1)} %get-tuple-element.46.refs_0_, bf16[512,2048]{1,0:T(8,128)(2,1)S(1)} %get-tuple-element.47.refs_1_, ...), custom_call_target="tpu_custom_call" | custom-call | flops 872415232 | bytes 262144 | tf_op jit(solution)/shard_map/early_sums/pallas_call | solution.py:339
  30.5 1.2 %collective-permute-done.11.refs_4_ = bf16[512,256]{1,0:T(8,128)(2,1)S(1)} collective-permute-done((bf16[512,256]{1,0:T(8,128)(2,1)S(1)}, bf16[512,256]{1,0:T(8,128)(2,1)S(1)}, u32[]{:S(2)}, u32[]{:S(2)}) %collective-permute-start.11) | collective-permute-done | bytes 262176 | tf_op jit(solution)/shard_map/ppermute | solution.py:491
  31.7 2.1 %receiver_sums.3 = (bf16[2,2,64,256]{3,2,1,0:T(8,128)(2,1)S(1)}, bf16[2,2,64,256]{3,2,1,0:T(8,128)(2,1)S(1)}, bf16[2,2,64,256]{3,2,1,0:T(8,128)(2,1)S(1)}, bf16[2,2,64,256]{3,2,1,0:T(8,128)(2,1)S(1)}) custom-call(bf16[4,256,256]{2,1,0:T(8,128)(2,1)S(1)} %get-tuple-element.43.main_ref, bf16[4,64,256]{2,1,0:T(8,128)(2,1)S(1)} %collective-permute-done.7.border_ref, ...), custom_call_target="tpu_custom_call" | custom-call | flops 1308622848 | bytes 786432 | tf_op jit(solution)/shard_map/receiver_sums/pallas_call | solution.py:370
  33.8 1.4 %collective-permute-start.17 = (bf16[2,2,64,256]{3,2,1,0:T(8,128)(2,1)S(1)}, bf16[2,2,64,256]{3,2,1,0:T(8,128)(2,1)S(1)}, u32[]{:S(2)}, u32[]{:S(2)}) collective-permute-start(bf16[2,2,64,256]{3,2,1,0:T(8,128)(2,1)S(1)} %get-tuple-element.58), channel_id=1, source_target_pairs={{0,2},{1,3},{2,0},{3,1},{4,6},{5,7},{6,4},{7,5},{8,10},{9,11},{10,... | collective-permute-start | bytes 393224 | tf_op jit(solution)/shard_map/ppermute | solution.py:491
  35.9 1.4 %collective-permute-start.19 = (bf16[2,2,64,256]{3,2,1,0:T(8,128)(2,1)S(1)}, bf16[2,2,64,256]{3,2,1,0:T(8,128)(2,1)S(1)}, u32[]{:S(2)}, u32[]{:S(2)}) collective-permute-start(bf16[2,2,64,256]{3,2,1,0:T(8,128)(2,1)S(1)} %get-tuple-element.60), channel_id=1, source_target_pairs={{0,6},{1,7},{2,4},{3,5},{4,2},{5,3},{6,0},{7,1},{8,14},{9,15},{10,... | collective-permute-start | bytes 393224 | tf_op jit(solution)/shard_map/ppermute | solution.py:491
  37.3 2.1 %receiver_sums.2 = (bf16[2,2,64,256]{3,2,1,0:T(8,128)(2,1)S(1)}, bf16[2,2,64,256]{3,2,1,0:T(8,128)(2,1)S(1)}, bf16[2,2,64,256]{3,2,1,0:T(8,128)(2,1)S(1)}, bf16[2,2,64,256]{3,2,1,0:T(8,128)(2,1)S(1)}) custom-call(bf16[4,256,256]{2,1,0:T(8,128)(2,1)S(1)} %get-tuple-element.43.main_ref, bf16[4,64,256]{2,1,0:T(8,128)(2,1)S(1)} %collective-permute-done.7.border_ref, ...), custom_call_target="tpu_custom_call" | custom-call | flops 1308622848 | bytes 786432 | tf_op jit(solution)/shard_map/receiver_sums/pallas_call | solution.py:370
  39.4 1.4 %collective-permute-start.13 = (bf16[2,2,64,256]{3,2,1,0:T(8,128)(2,1)S(1)}, bf16[2,2,64,256]{3,2,1,0:T(8,128)(2,1)S(1)}, u32[]{:S(2)}, u32[]{:S(2)}) collective-permute-start(bf16[2,2,64,256]{3,2,1,0:T(8,128)(2,1)S(1)} %get-tuple-element.54), channel_id=1, source_target_pairs={{0,2},{1,3},{2,0},{3,1},{4,6},{5,7},{6,4},{7,5},{8,10},{9,11},{10,... | collective-permute-start | bytes 393224 | tf_op jit(solution)/shard_map/ppermute | solution.py:491
  41.5 1.4 %collective-permute-start.15 = (bf16[2,2,64,256]{3,2,1,0:T(8,128)(2,1)S(1)}, bf16[2,2,64,256]{3,2,1,0:T(8,128)(2,1)S(1)}, u32[]{:S(2)}, u32[]{:S(2)}) collective-permute-start(bf16[2,2,64,256]{3,2,1,0:T(8,128)(2,1)S(1)} %get-tuple-element.56), channel_id=1, source_target_pairs={{0,6},{1,7},{2,4},{3,5},{4,2},{5,3},{6,0},{7,1},{8,14},{9,15},{10,... | collective-permute-start | bytes 393224 | tf_op jit(solution)/shard_map/ppermute | solution.py:491
  43.2 2.6 %collective-permute-done.13.refs_1_ = bf16[2,2,64,256]{3,2,1,0:T(8,128)(2,1)S(1)} collective-permute-done((bf16[2,2,64,256]{3,2,1,0:T(8,128)(2,1)S(1)}, bf16[2,2,64,256]{3,2,1,0:T(8,128)(2,1)S(1)}, u32[]{:S(2)}, u32[]{:S(2)}) %collective-permute-start.13) | collective-permute-done | bytes 131104 | tf_op jit(solution)/shard_map/ppermute | solution.py:491
  45.8 2.1 %collective-permute-done.14.refs_2_ = bf16[2,2,64,256]{3,2,1,0:T(8,128)(2,1)S(1)} collective-permute-done((bf16[2,2,64,256]{3,2,1,0:T(8,128)(2,1)S(1)}, bf16[2,2,64,256]{3,2,1,0:T(8,128)(2,1)S(1)}, u32[]{:S(2)}, u32[]{:S(2)}) %collective-permute-start.14) | collective-permute-done | bytes 131104 | tf_op jit(solution)/shard_map/ppermute | solution.py:491
  48.2 2.0 %inverse_dft.2.refs_5_ = bf16[4,64,2048]{2,1,0:T(8,128)(2,1)} custom-call(s32[8]{0:T(128)S(1)} %stack.60.ids_ref, bf16[2,256,512]{2,1,0:T(8,128)(2,1)S(1)} %copy-done, f32[8,2,256]{2,1,0:T(2,128)S(1)} %copy-done.2, bf16[2,2,64,256]{3,2,1,0:T(8,128)(2,1)S(1)} %get-tuple-element.57.refs_0_, bf16[2,2,64,256]{3,2,1,0:T(8,128)(2,1)S(1)} %collective-permute-done.17.refs_1_, ...), custom_call_target="tpu_custom_call" | custom-call | flops 268435456 | bytes 524288 | tf_op jit(solution)/shard_map/inverse_dft/pallas_call | solution.py:470
  50.2 2.0 %inverse_dft.3 = bf16[4,64,2048]{2,1,0:T(8,128)(2,1)} custom-call(s32[8]{0:T(128)S(1)} %stack.60.ids_ref, bf16[2,256,512]{2,1,0:T(8,128)(2,1)S(1)} %copy-done, f32[8,2,256]{2,1,0:T(2,128)S(1)} %copy-done.2, bf16[2,2,64,256]{3,2,1,0:T(8,128)(2,1)S(1)} %get-tuple-element.53.refs_0_, ...), custom_call_target="tpu_custom_call", output_to_operand_aliasing={{}: (8, {})} | custom-call | flops 268435456 | bytes 524288 | tf_op jit(solution)/shard_map/inverse_dft/pallas_call | solution.py:470
  (48 shorter events, 5.8 us)
Async XLA Ops:
  0.0 14.5 %copy-start.1 = (bf16[256,2048]{1,0:T(8,128)(2,1)S(1)}, bf16[256,2048]{1,0:T(8,128)(2,1)}, u32[]{:S(2)}) copy-start(bf16[256,2048]{1,0:T(8,128)(2,1)} %refs_0_.3) | copy-start | bytes 3145732
  0.0 8.0 %collective-permute-start = (bf16[256,2048]{1,0:T(8,128)(2,1)}, bf16[256,2048]{1,0:T(8,128)(2,1)S(1)}, u32[]{:S(2)}, u32[]{:S(2)}) collective-permute-start(bf16[256,2048]{1,0:T(8,128)(2,1)} %bitcast.14), channel_id=1, source_target_pairs={{0,1},{1,0},{2,3},{3,2},{4,5},{5,4},{6,7},{7,6},{8,9},{9,8},{10,11... | collective-permute-start | bytes 3145736 | tf_op jit(solution)/shard_map/ppermute | solution.py:491
  0.5 12.9 %collective-permute-start.9 = (bf16[256,2048]{1,0:T(8,128)(2,1)}, bf16[256,2048]{1,0:T(8,128)(2,1)S(1)}, u32[]{:S(2)}, u32[]{:S(2)}) collective-permute-start(bf16[256,2048]{1,0:T(8,128)(2,1)} %refs_0_.3), channel_id=1, source_target_pairs={{0,1},{1,0},{2,3},{3,2},{4,5},{5,4},{6,7},{7,6},{8,9},{9,8},{10,11... | collective-permute-start | bytes 3145736 | tf_op jit(solution)/shard_map/ppermute | solution.py:491
  3.5 8.3 %collective-permute-start.1 = (bf16[272,256]{1,0:T(8,128)(2,1)S(1)}, bf16[272,256]{1,0:T(8,128)(2,1)S(1)}, u32[]{:S(2)}, u32[]{:S(2)}) collective-permute-start(bf16[272,256]{1,0:T(8,128)(2,1)S(1)} %get-tuple-element.37), channel_id=1, source_target_pairs={{0,2},{1,3},{2,0},{3,1},{4,6},{5,7},{6,4},{7,5},{8,10},{9,11},{10,... | collective-permute-start | bytes 417800 | tf_op jit(solution)/shard_map/ppermute | solution.py:491
  6.5 10.7 %collective-permute-start.3 = (bf16[272,256]{1,0:T(8,128)(2,1)S(1)}, bf16[272,256]{1,0:T(8,128)(2,1)S(1)}, u32[]{:S(2)}, u32[]{:S(2)}) collective-permute-start(bf16[272,256]{1,0:T(8,128)(2,1)S(1)} %get-tuple-element.39), channel_id=1, source_target_pairs={{0,4},{1,5},{2,6},{3,7},{4,0},{5,1},{6,2},{7,3},{8,12},{9,13},{10,... | collective-permute-start | bytes 417800 | tf_op jit(solution)/shard_map/ppermute | solution.py:491
  8.0 10.1 %collective-permute-start.5 = (bf16[272,256]{1,0:T(8,128)(2,1)S(1)}, bf16[272,256]{1,0:T(8,128)(2,1)S(1)}, u32[]{:S(2)}, u32[]{:S(2)}) collective-permute-start(bf16[272,256]{1,0:T(8,128)(2,1)S(1)} %get-tuple-element.41), channel_id=1, source_target_pairs={{0,6},{1,7},{2,4},{3,5},{4,2},{5,3},{6,0},{7,1},{8,14},{9,15},{10,... | collective-permute-start | bytes 417800 | tf_op jit(solution)/shard_map/ppermute | solution.py:491
  8.0 13.2 %copy-start.3 = (s32[4,4]{1,0:T(4,128)S(1)}, s32[4,4]{1,0:T(4,128)}, u32[]{:S(2)}) copy-start(s32[4,4]{1,0:T(4,128)} %plan_ref.1) | copy-start | bytes 196
  9.8 9.9 %collective-permute-start.2 = (bf16[256,256]{1,0:T(8,128)(2,1)S(1)}, bf16[256,256]{1,0:T(8,128)(2,1)S(1)}, u32[]{:S(2)}, u32[]{:S(2)}) collective-permute-start(bf16[256,256]{1,0:T(8,128)(2,1)S(1)} %get-tuple-element.38), channel_id=1, source_target_pairs={{0,2},{1,3},{2,0},{3,1},{4,6},{5,7},{6,4},{7,5},{8,10},{9,11},{10,... | collective-permute-start | bytes 393224 | tf_op jit(solution)/shard_map/ppermute | solution.py:491
  11.8 9.0 %collective-permute-start.4 = (bf16[256,256]{1,0:T(8,128)(2,1)S(1)}, bf16[256,256]{1,0:T(8,128)(2,1)S(1)}, u32[]{:S(2)}, u32[]{:S(2)}) collective-permute-start(bf16[256,256]{1,0:T(8,128)(2,1)S(1)} %get-tuple-element.40), channel_id=1, source_target_pairs={{0,4},{1,5},{2,6},{3,7},{4,0},{5,1},{6,2},{7,3},{8,12},{9,13},{10,... | collective-permute-start | bytes 393224 | tf_op jit(solution)/shard_map/ppermute | solution.py:491
  13.3 7.9 %collective-permute-start.6 = (bf16[256,256]{1,0:T(8,128)(2,1)S(1)}, bf16[256,256]{1,0:T(8,128)(2,1)S(1)}, u32[]{:S(2)}, u32[]{:S(2)}) collective-permute-start(bf16[256,256]{1,0:T(8,128)(2,1)S(1)} %get-tuple-element.42), channel_id=1, source_target_pairs={{0,6},{1,7},{2,4},{3,5},{4,2},{5,3},{6,0},{7,1},{8,14},{9,15},{10,... | collective-permute-start | bytes 393224 | tf_op jit(solution)/shard_map/ppermute | solution.py:491
  17.3 13.2 %collective-permute-start.10 = (bf16[512,256]{1,0:T(8,128)(2,1)S(1)}, bf16[512,256]{1,0:T(8,128)(2,1)S(1)}, u32[]{:S(2)}, u32[]{:S(2)}) collective-permute-start(bf16[512,256]{1,0:T(8,128)(2,1)S(1)} %get-tuple-element.50), channel_id=1, source_target_pairs={{0,2},{1,3},{2,0},{3,1},{4,6},{5,7},{6,4},{7,5},{8,10},{9,11},{10,... | collective-permute-start | bytes 786440 | tf_op jit(solution)/shard_map/ppermute | solution.py:491
  18.1 13.6 %collective-permute-start.11 = (bf16[512,256]{1,0:T(8,128)(2,1)S(1)}, bf16[512,256]{1,0:T(8,128)(2,1)S(1)}, u32[]{:S(2)}, u32[]{:S(2)}) collective-permute-start(bf16[512,256]{1,0:T(8,128)(2,1)S(1)} %get-tuple-element.51), channel_id=1, source_target_pairs={{0,4},{1,5},{2,6},{3,7},{4,0},{5,1},{6,2},{7,3},{8,12},{9,13},{10,... | collective-permute-start | bytes 786440 | tf_op jit(solution)/shard_map/ppermute | solution.py:491
  19.6 12.1 %collective-permute-start.12 = (bf16[512,256]{1,0:T(8,128)(2,1)S(1)}, bf16[512,256]{1,0:T(8,128)(2,1)S(1)}, u32[]{:S(2)}, u32[]{:S(2)}) collective-permute-start(bf16[512,256]{1,0:T(8,128)(2,1)S(1)} %get-tuple-element.52), channel_id=1, source_target_pairs={{0,6},{1,7},{2,4},{3,5},{4,2},{5,3},{6,0},{7,1},{8,14},{9,15},{10,... | collective-permute-start | bytes 786440 | tf_op jit(solution)/shard_map/ppermute | solution.py:491
  22.0 7.0 %collective-permute-start.7 = (bf16[4,64,256]{2,1,0:T(8,128)(2,1)S(1)}, bf16[4,64,256]{2,1,0:T(8,128)(2,1)S(1)}, u32[]{:S(2)}, u32[]{:S(2)}) collective-permute-start(bf16[4,64,256]{2,1,0:T(8,128)(2,1)S(1)} %get-tuple-element.44), channel_id=1, source_target_pairs={{0,8},{8,16},{16,24},{1,9},{9,17},{17,25},{2,10},{10,18},{18,26},{... | collective-permute-start | bytes 393224 | tf_op jit(solution)/shard_map/ppermute | solution.py:532
  25.7 1.3 %collective-permute-start.8 = (bf16[4,16,256]{2,1,0:T(8,128)(2,1)S(1)}, bf16[4,16,256]{2,1,0:T(8,128)(2,1)S(1)}, u32[]{:S(2)}, u32[]{:S(2)}) collective-permute-start(bf16[4,16,256]{2,1,0:T(8,128)(2,1)S(1)} %get-tuple-element.45.refs_0_), channel_id=1, source_target_pairs={{0,1},{1,0},{2,3},{3,2},{4,5},{5,4},{6,7},{7,6},{8,9},{9,8},{10,11... | collective-permute-start | bytes 98312 | tf_op jit(solution)/shard_map/ppermute | solution.py:491
  33.8 7.8 %collective-permute-start.17 = (bf16[2,2,64,256]{3,2,1,0:T(8,128)(2,1)S(1)}, bf16[2,2,64,256]{3,2,1,0:T(8,128)(2,1)S(1)}, u32[]{:S(2)}, u32[]{:S(2)}) collective-permute-start(bf16[2,2,64,256]{3,2,1,0:T(8,128)(2,1)S(1)} %get-tuple-element.58), channel_id=1, source_target_pairs={{0,2},{1,3},{2,0},{3,1},{4,6},{5,7},{6,4},{7,5},{8,10},{9,11},{10,... | collective-permute-start | bytes 393224 | tf_op jit(solution)/shard_map/ppermute | solution.py:491
  35.2 7.9 %collective-permute-start.18 = (bf16[2,2,64,256]{3,2,1,0:T(8,128)(2,1)S(1)}, bf16[2,2,64,256]{3,2,1,0:T(8,128)(2,1)S(1)}, u32[]{:S(2)}, u32[]{:S(2)}) collective-permute-start(bf16[2,2,64,256]{3,2,1,0:T(8,128)(2,1)S(1)} %get-tuple-element.59), channel_id=1, source_target_pairs={{0,4},{1,5},{2,6},{3,7},{4,0},{5,1},{6,2},{7,3},{8,12},{9,13},{10,... | collective-permute-start | bytes 393224 | tf_op jit(solution)/shard_map/ppermute | solution.py:491
  35.9 7.1 %collective-permute-start.19 = (bf16[2,2,64,256]{3,2,1,0:T(8,128)(2,1)S(1)}, bf16[2,2,64,256]{3,2,1,0:T(8,128)(2,1)S(1)}, u32[]{:S(2)}, u32[]{:S(2)}) collective-permute-start(bf16[2,2,64,256]{3,2,1,0:T(8,128)(2,1)S(1)} %get-tuple-element.60), channel_id=1, source_target_pairs={{0,6},{1,7},{2,4},{3,5},{4,2},{5,3},{6,0},{7,1},{8,14},{9,15},{10,... | collective-permute-start | bytes 393224 | tf_op jit(solution)/shard_map/ppermute | solution.py:491
  39.4 8.8 %copy-start = (bf16[2,256,512]{2,1,0:T(8,128)(2,1)S(1)}, bf16[2,256,512]{2,1,0:T(8,128)(2,1)}, u32[]{:S(2)}) copy-start(bf16[2,256,512]{2,1,0:T(8,128)(2,1)} %constant.24.clone.table_ref) | copy-start | bytes 1572868
  39.4 6.4 %collective-permute-start.13 = (bf16[2,2,64,256]{3,2,1,0:T(8,128)(2,1)S(1)}, bf16[2,2,64,256]{3,2,1,0:T(8,128)(2,1)S(1)}, u32[]{:S(2)}, u32[]{:S(2)}) collective-permute-start(bf16[2,2,64,256]{3,2,1,0:T(8,128)(2,1)S(1)} %get-tuple-element.54), channel_id=1, source_target_pairs={{0,2},{1,3},{2,0},{3,1},{4,6},{5,7},{6,4},{7,5},{8,10},{9,11},{10,... | collective-permute-start | bytes 393224 | tf_op jit(solution)/shard_map/ppermute | solution.py:491
  40.8 7.1 %collective-permute-start.14 = (bf16[2,2,64,256]{3,2,1,0:T(8,128)(2,1)S(1)}, bf16[2,2,64,256]{3,2,1,0:T(8,128)(2,1)S(1)}, u32[]{:S(2)}, u32[]{:S(2)}) collective-permute-start(bf16[2,2,64,256]{3,2,1,0:T(8,128)(2,1)S(1)} %get-tuple-element.55), channel_id=1, source_target_pairs={{0,4},{1,5},{2,6},{3,7},{4,0},{5,1},{6,2},{7,3},{8,12},{9,13},{10,... | collective-permute-start | bytes 393224 | tf_op jit(solution)/shard_map/ppermute | solution.py:491
  41.5 6.4 %collective-permute-start.15 = (bf16[2,2,64,256]{3,2,1,0:T(8,128)(2,1)S(1)}, bf16[2,2,64,256]{3,2,1,0:T(8,128)(2,1)S(1)}, u32[]{:S(2)}, u32[]{:S(2)}) collective-permute-start(bf16[2,2,64,256]{3,2,1,0:T(8,128)(2,1)S(1)} %get-tuple-element.56), channel_id=1, source_target_pairs={{0,6},{1,7},{2,4},{3,5},{4,2},{5,3},{6,0},{7,1},{8,14},{9,15},{10,... | collective-permute-start | bytes 393224 | tf_op jit(solution)/shard_map/ppermute | solution.py:491
  43.1 5.1 %collective-permute-start.20 = (bf16[4,2,64,256]{3,2,1,0:T(8,128)(2,1)S(1)}, bf16[4,2,64,256]{3,2,1,0:T(8,128)(2,1)S(1)}, u32[]{:S(2)}, u32[]{:S(2)}) collective-permute-start(bf16[4,2,64,256]{3,2,1,0:T(8,128)(2,1)S(1)} %pad_maximum_fusion.1), channel_id=1, source_target_pairs={{0,1},{1,0},{2,3},{3,2},{4,5},{5,4},{6,7},{7,6},{8,9},{9,8},{10,11... | collective-permute-start | bytes 786440 | tf_op jit(solution)/shard_map/ppermute | solution.py:491
  48.0 2.2 %collective-permute-start.16 = (bf16[4,2,64,256]{3,2,1,0:T(8,128)(2,1)S(1)}, bf16[4,2,64,256]{3,2,1,0:T(8,128)(2,1)S(1)}, u32[]{:S(2)}, u32[]{:S(2)}) collective-permute-start(bf16[4,2,64,256]{3,2,1,0:T(8,128)(2,1)S(1)} %pad_maximum_fusion), channel_id=1, source_target_pairs={{0,1},{1,0},{2,3},{3,2},{4,5},{5,4},{6,7},{7,6},{8,9},{9,8},{10,11... | collective-permute-start | bytes 786440 | tf_op jit(solution)/shard_map/ppermute | solution.py:491
  (1 other events, 8.8 us)
